TPU v7x, 512 devices: a whole 4x8x8 slice. The times are simulated.
512 devices in a mesh: dp: 32 (over y, x), feat: 16 (over z, core).
Axes of the slice: x: 4, y: 8, z: 8, core: 2. Of those that a mesh axis runs over, the one named last changes fastest.
Arguments:
- features: bfloat16 [65536, 1024], P('dp', 'feat'), may hold values from -6 to 6
- request_rows: int32 [32, 32, 512], P('dp'), may hold values from 0 to 2047
- self_slots: int32 [32, 704], P('dp'), may hold values from 0 to 16383
- adj_one: int32 [32, 704, 10], P('dp'), may hold values from 0 to 16383
- deg_one: int32 [32, 704], P('dp'), may hold values from 1 to 10
- adj_two: int32 [32, 64, 10], P('dp'), may hold values from 0 to 703
- deg_two: int32 [32, 64], P('dp'), may hold values from 1 to 10
- w1_self: bfloat16 [1024, 256], P('feat'), may hold values from -0.1875 to 0.1875
- w1_neigh: bfloat16 [1024, 256], P('feat'), may hold values from -0.1875 to 0.1875
- w2_self: bfloat16 [256, 256], replicated, may hold values from -0.375 to 0.375
- w2_neigh: bfloat16 [256, 256], replicated, may hold values from -0.375 to 0.375
- out_grad: bfloat16 [2048, 256], P('dp'), may hold values from -0.078125 to 0.078125
Outputs:
- embeddings: bfloat16 [2048, 256], P('dp')
- grad_w1_self: float32 [1024, 256], P('feat')
- grad_w1_neigh: float32 [1024, 256], P('feat')
- grad_w2_self: float32 [256, 256], replicated
- grad_w2_neigh: float32 [256, 256], replicated
Inputs may be any that keep to these rules, and one draw needn't show every extreme that they name: `adj_one`: entries of a padded list past its count are arbitrary valid slots and must not be used.
All inputs are finite; a program needn't handle non-finite values.
Results may differ from a plain program's by a relative error of at most 0.006.
Values may be sent and summed in bfloat16 or wider, within the bound.
A program may use at most 64 MiB of HBM per device.

v0:
```python
import jax
import jax.numpy as jnp
from jax import lax
from jax.sharding import PartitionSpec as P


def slot_weights(neighbours, degrees):
    fanout = neighbours.shape[-1]
    present = jnp.arange(fanout, dtype=jnp.int32)[None, :] < degrees[:, None]
    return present.astype(jnp.float32) / degrees[:, None].astype(jnp.float32)


def neighbour_mean(source, neighbours, degrees):
    weights = slot_weights(neighbours, degrees)
    gathered = source[neighbours].astype(jnp.float32)
    return jnp.sum(gathered * weights[:, :, None], axis=1).astype(jnp.bfloat16)


def neighbour_spread(values, neighbours, degrees, row_count):
    weights = slot_weights(neighbours, degrees)
    weighted = (values[:, None, :] * weights[:, :, None]).reshape(-1, values.shape[1])
    empty = jnp.zeros((row_count, values.shape[1]), jnp.float32)
    return empty.at[neighbours.reshape(-1)].add(weighted)


def silu_slope(pre):
    sigmoid_part = jax.nn.sigmoid(pre)
    return sigmoid_part * (1.0 + pre * (1.0 - sigmoid_part))


def local(
    features,
    request_rows,
    self_slots,
    adj_one,
    deg_one,
    adj_two,
    deg_two,
    w1_self,
    w1_neigh,
    w2_self,
    w2_neigh,
    out_grad,
):
    columns_here = features.shape[1]
    asked_rows = lax.all_to_all(request_rows, "dp", split_axis=1, concat_axis=0, tiled=True)
    picked = features[asked_rows.reshape(-1)].reshape(asked_rows.shape + (columns_here,))
    replies = lax.all_to_all(picked, "dp", split_axis=0, concat_axis=1, tiled=True)
    sampled = replies.reshape(-1, columns_here)
    own_rows = sampled[self_slots[0]]
    agg_one = neighbour_mean(sampled, adj_one[0], deg_one[0])
    partial_value = jnp.dot(own_rows, w1_self, preferred_element_type=jnp.float32) + jnp.dot(
        agg_one, w1_neigh, preferred_element_type=jnp.float32
    )
    targets = adj_two.shape[1]
    layer_rows = own_rows.shape[0]
    pre_one = lax.psum(partial_value, "feat")
    hidden = jax.nn.silu(pre_one).astype(jnp.bfloat16)
    agg_two = neighbour_mean(hidden, adj_two[0], deg_two[0])
    partial_out = jnp.dot(hidden[:targets], w2_self, preferred_element_type=jnp.float32) + jnp.dot(
        agg_two, w2_neigh, preferred_element_type=jnp.float32
    )
    embeddings = partial_out.astype(jnp.bfloat16)
    grad_two_self = jnp.dot(hidden[:targets].T, out_grad, preferred_element_type=jnp.float32)
    grad_two_neigh = jnp.dot(agg_two.T, out_grad, preferred_element_type=jnp.float32)
    grad_agg = jnp.dot(out_grad, w2_neigh.T, preferred_element_type=jnp.float32)
    grad_hidden = neighbour_spread(grad_agg, adj_two[0], deg_two[0], layer_rows)
    grad_hidden = grad_hidden.at[:targets].add(
        jnp.dot(out_grad, w2_self.T, preferred_element_type=jnp.float32)
    )
    grad_pre = (grad_hidden * silu_slope(pre_one)).astype(jnp.bfloat16)
    grad_one_self = jnp.dot(own_rows.T, grad_pre, preferred_element_type=jnp.float32)
    grad_one_neigh = jnp.dot(agg_one.T, grad_pre, preferred_element_type=jnp.float32)
    reduced = lax.psum((grad_one_self, grad_one_neigh, grad_two_self, grad_two_neigh), "dp")
    return (embeddings, reduced[0], reduced[1], reduced[2], reduced[3])


def solution(mesh):
    return jax.shard_map(
        local,
        mesh=mesh,
        in_specs=(
            P("dp", "feat"),
            P("dp", None, None),
            P("dp", None),
            P("dp", None, None),
            P("dp", None),
            P("dp", None, None),
            P("dp", None),
            P("feat", None),
            P("feat", None),
            P(),
            P(),
            P("dp", None),
        ),
        out_specs=(P("dp", None), P("feat", None), P("feat", None), P(), P()),
        check_vma=False,
    )
```

profile of v0, /device:TPU:1, one launch (start us, length us, event | category | flops | bytes accessed | tf_op | source)
XLA Modules:
  0.0 469.3 jit_solution(12442592216726278637)
XLA Ops:
  7.2 1.6 copy.29
  8.8 10.5 %all-to-all-start = ((s32[1,32,512]{2,0,1:T(1,128)}), s32[1,32,512]{2,0,1:T(1,128)S(1)}, u32[]{:S(2)}, u32[]{:S(2)}) async-start(s32[1,32,512]{2,0,1:T(1,128)} %copy.29), calls=%async_computation | async-start | bytes 131072 | tf_op jit(solution)/shard_map/all_to_all | solution.py:46
  19.3 1.2 copy.30
  20.5 7.6 %all-to-all-done = s32[1,32,512]{2,0,1:T(1,128)S(1)} async-done(((s32[1,32,512]{2,0,1:T(1,128)}), s32[1,32,512]{2,0,1:T(1,128)S(1)}, u32[]{:S(2)}, u32[]{:S(2)}) %all-to-all-start) | async-done | bytes 65568 | tf_op jit(solution)/shard_map/all_to_all | solution.py:46
  28.2 57.4 %gather_fusion = bf16[16384,64]{1,0:T(8,128)(2,1)} fusion(bf16[2048,64]{1,0:T(8,128)(2,1)S(1)} %copy.30, s32[16384]{0:T(1024)S(1)} %broadcast_clamp_fusion), kind=kCustom, calls=%fused_computation | custom fusion | bytes 4259840 | tf_op jit(solution)/shard_map/gather | solution.py:47
  85.6 4.8 %copy.31 = bf16[32,1,512,64]{2,3,1,0:T(8,128)(2,1)} copy(bf16[32,1,512,64]{3,2,0,1:T(8,128)(2,1)} %bitcast.36) | data formatting | bytes 4194304 | tf_op jit(solution)/shard_map/reshape | solution.py:47
  90.4 4.2 all-to-all-start.1
  96.0 45.5 %all-to-all-done.1 = bf16[32,1,512,64]{2,3,1,0:T(8,128)(2,1)S(1)} async-done(((bf16[32,1,512,64]{2,3,1,0:T(8,128)(2,1)}), bf16[32,1,512,64]{2,3,1,0:T(8,128)(2,1)S(1)}, u32[]{:S(2)}, u32[]{:S(2)}) %all-to-all-start.1) | async-done | bytes 2097184 | tf_op jit(solution)/shard_map/all_to_all | solution.py:48
  141.4 3.2 copy.32
  144.6 4.5 gather_fusion.1
  149.1 14.4 %gather_fusion.2 = bf16[7040,64]{1,0:T(8,128)(2,1)S(1)} fusion(bf16[16384,64]{1,0:T(8,128)(2,1)} %bitcast.35, s32[7168]{0:T(1024)S(1)} %pad_clamp_fusion), kind=kCustom, calls=%fused_computation.2 | custom fusion | bytes 1830400 | tf_op jit(solution)/shard_map/gather | solution.py:15
  163.6 2.9 reshape.343
  166.7 5.7 %multiply_reduce_fusion = bf16[704,64]{1,0:T(8,128)(2,1)S(1)} fusion(f32[704,10,64]{2,1,0:T(8,128)} %reshape.343, f32[704,10]{1,0:T(8,128)S(1)} %copy.34), kind=kLoop, calls=%fused_computation.5 | loop fusion | flops 856064 | bytes 1920512 | tf_op jit(solution)/shard_map/reduce_sum | solution.py:16
  172.4 1.1 convolution_add_fusion
  174.2 7.9 %scatter_custom_fusion = f32[704,256]{1,0:T(8,128)S(1)} fusion(s32[640]{0:T(1024)S(1)} %fusion.17, f32[640,256]{1,0:T(8,128)S(1)} %mul.51, f32[]{:T(128)} %constant.45.clone.1, f32[640]{0:T(1024)S(1)} %div.42), kind=kCustom, calls=%fused_computation.15 | custom fusion | flops 327680 | bytes 1380356 | tf_op jit(solution)/shard_map/scatter-add | solution.py:23
  182.4 111.0 %all-reduce.4.cloned.1.call-done = f32[704,256]{1,0:T(8,128)} async-done(((f32[704,256]{1,0:T(8,128)}), f32[704,256]{1,0:T(8,128)}) %all-reduce.4.cloned.1.call-update) | async-done | bytes 720912 | tf_op jit(solution)/shard_map/psum | solution.py:57
  293.4 1.4 multiply_convert_fusion
  297.4 2.8 gather_fusion.3
  300.6 0.9 fusion.22
  302.5 153.7 %all-reduce.6.cloned.1.call-done = (f32[64,256]{1,0:T(8,128)}, f32[64,256]{1,0:T(8,128)}, f32[256,256]{1,0:T(8,128)}, f32[256,256]{1,0:T(8,128)}) async-done(((f32[64,256]{1,0:T(8,128)}, f32[64,256]{1,0:T(8,128)}, f32[256,256]{1,0:T(8,128)}, f32[256,256]{1,0:T(8,128)}), (f32[64,256]{1,0:T(8,128)}, f32[64,256]{1,0:T(8,128)}, f32[256,256]{1,0:T(8,128)}, f32[256,256]{1,0:T(8,128)})) %all-reduce.6.cloned.1.call-update) | async-done | bytes 655376 | tf_op jit(solution)/shard_map/psum | solution.py:74
  456.2 1.5 copy.43
  457.7 1.5 copy.44
  459.1 1.7 copy.45
  460.8 1.7 copy.46
  (58 shorter events, 6.3 us)
Async XLA Ops:
  7.2 175.0 %copy-start = (bf16[256,256]{1,0:T(8,128)(2,1)S(1)}, bf16[256,256]{1,0:T(8,128)(2,1)}, u32[]{:S(2)}) copy-start(bf16[256,256]{1,0:T(8,128)(2,1)} %param.23) | copy-start | bytes 393220
  8.8 19.3 %all-to-all-start = ((s32[1,32,512]{2,0,1:T(1,128)}), s32[1,32,512]{2,0,1:T(1,128)S(1)}, u32[]{:S(2)}, u32[]{:S(2)}) async-start(s32[1,32,512]{2,0,1:T(1,128)} %copy.29), calls=%async_computation | async-start | bytes 131072 | tf_op jit(solution)/shard_map/all_to_all | solution.py:46
  85.6 9.1 %copy-start.6 = (s32[1,64,10]{1,0,2:T(1,128)S(1)}, s32[1,64,10]{1,0,2:T(1,128)}, u32[]{:S(2)}) copy-start(s32[1,64,10]{1,0,2:T(1,128)} %param.19) | copy-start | bytes 7684
  85.6 9.3 %copy-start.5 = (s32[1,704,10]{1,0,2:T(1,128)S(1)}, s32[1,704,10]{1,0,2:T(1,128)}, u32[]{:S(2)}) copy-start(s32[1,704,10]{1,0,2:T(1,128)} %param.17) | copy-start | bytes 84484
  85.6 9.8 %copy-start.8 = (s32[1,704]{1,0:T(1,128)S(1)}, s32[1,704]{1,0:T(1,128)}, u32[]{:S(2)}) copy-start(s32[1,704]{1,0:T(1,128)} %param.18) | copy-start | bytes 8452
  90.4 5.2 %copy-start.7 = (s32[1,704]{1,0:T(1,128)S(1)}, s32[1,704]{1,0:T(1,128)}, u32[]{:S(2)}) copy-start(s32[1,704]{1,0:T(1,128)} %param.16) | copy-start | bytes 8452
  90.4 5.3 %copy-start.9 = (s32[1,64]{1,0:T(1,128)S(1)}, s32[1,64]{1,0:T(1,128)}, u32[]{:S(2)}) copy-start(s32[1,64]{1,0:T(1,128)} %param.20) | copy-start | bytes 772
  90.4 5.4 %copy-start.1 = (bf16[64,256]{1,0:T(8,128)(2,1)S(1)}, bf16[64,256]{1,0:T(8,128)(2,1)}, u32[]{:S(2)}) copy-start(bf16[64,256]{1,0:T(8,128)(2,1)} %param.25) | copy-start | bytes 98308
  90.4 5.4 %copy-start.2 = (bf16[256,256]{1,0:T(8,128)(2,1)S(1)}, bf16[256,256]{1,0:T(8,128)(2,1)}, u32[]{:S(2)}) copy-start(bf16[256,256]{1,0:T(8,128)(2,1)} %param.24) | copy-start | bytes 393220
  90.4 51.0 %all-to-all-start.1 = ((bf16[32,1,512,64]{2,3,1,0:T(8,128)(2,1)}), bf16[32,1,512,64]{2,3,1,0:T(8,128)(2,1)S(1)}, u32[]{:S(2)}, u32[]{:S(2)}) async-start(bf16[32,1,512,64]{2,3,1,0:T(8,128)(2,1)} %copy.31), calls=%async_computation.1 | async-start | bytes 4194304 | tf_op jit(solution)/shard_map/all_to_all | solution.py:48
  94.6 198.8 %all-reduce.4.cloned.1.call-start = ((), (), s32[]{:S(2)}) async-start(), calls=%async_computation.2 | async-start | bytes 1441792 | tf_op jit(solution)/shard_map/psum | solution.py:57
  163.5 3.0 copy-start.3
  166.5 5.9 %copy-start.4 = (bf16[64,256]{1,0:T(8,128)(2,1)S(1)}, bf16[64,256]{1,0:T(8,128)(2,1)}, u32[]{:S(2)}) copy-start(bf16[64,256]{1,0:T(8,128)(2,1)} %param.22) | copy-start | bytes 98308
  173.6 282.6 %all-reduce.6.cloned.1.call-start = ((), (), s32[]{:S(2)}) async-start(), calls=%async_computation.3 | async-start | bytes 1310720 | tf_op jit(solution)/shard_map/psum | solution.py:74
Sparse Core Ops, SparseCore 0:
  173.7 119.6 all-reduce.3
  301.7 154.4 all-reduce.5
where the time goes:
time: 473 us; the launch traced here: 469 us
  waiting for transfers between devices  318 us (67%)
  local copies, waits for them, and re-layouts  101 us (21%)
  other arithmetic  15.6 us (3%)
  starting transfers between devices  14.7 us (3%)
  between operations  14.4 us (3%)
  matrix products  6.13 us (1%)
    psum x1, waiting for transfers between devices, local(): lax.psum((grad_one_self, grad_one_neigh, grad_two_self, grad_two_neigh),...  154 us
    psum x1, waiting for transfers between devices, local(): pre_one = lax.psum(partial_value, 'feat')  111 us
    gather x1, local copies, waits for them, and re-layouts, local(): features[asked_rows.reshape(-1)].reshape(asked_rows.shape + (columns_here,))  57.4 us
    all_to_all x1, waiting for transfers between devices, local(): lax.all_to_all(picked, 'dp', split_axis=0, concat_axis=1, tiled=True)  45.5 us
    gather x2, local copies, waits for them, and re-layouts, neighbour_mean(): gathered = source[neighbours].astype(jnp.float32)  17.2 us
    all_to_all x1, starting transfers between devices, local(): lax.all_to_all(request_rows, 'dp', split_axis=1, concat_axis=0, tiled=True)  10.5 us
  transfers between devices with their start and end apart: 4, of which 4 were waited for; matrix products, arithmetic and copies ran while one was open for 3% of the time, Pallas kernels for 0%

commit v1 on v0

v1 whole, which is shorter than its diff:
```python
import functools

import jax
import jax.numpy as jnp
from jax import lax
from jax.experimental import pallas as pl
from jax.experimental.pallas import tpu as pltpu
from jax.sharding import PartitionSpec as P

MESH = pl.DeviceIdType.MESH
ROWS = 768


def slot_weights(neighbours, degrees):
    fanout = neighbours.shape[-1]
    present = jnp.arange(fanout, dtype=jnp.int32)[None, :] < degrees[:, None]
    return present.astype(jnp.float32) / degrees[:, None].astype(jnp.float32)


def neighbour_mean(source, neighbours, degrees):
    weights = slot_weights(neighbours, degrees)
    gathered = source[neighbours].astype(jnp.float32)
    return jnp.sum(gathered * weights[:, :, None], axis=1).astype(jnp.bfloat16)


def contract_rows(a, b):
    return lax.dot_general(a, b, (((0,), (0,)), ((), ())), preferred_element_type=jnp.float32)


def contract_lanes(a, b):
    return lax.dot_general(a, b, (((1,), (1,)), ((), ())), preferred_element_type=jnp.float32)


def each(count, body):
    def step(k, carry):
        body(k)
        return carry

    lax.fori_loop(1, count, step, 0)


def tail_kernel(
    nd, nf,
    oa_ref, w1_ref, w2s_ref, w2n_ref, grad_ref, adj_ref, deg_ref,
    emb_ref, gw1_ref, gw2_ref,
    rows_buf, gh_buf, hg_buf, part1, part2, in1, in2, sum1, sum2, slice2,
    send_a, recv_a, send_h, recv_h, send_r, recv_r, send_q, recv_q,
    send_g, recv_g, send_b, recv_b, send_f, recv_f,
):
    d = lax.axis_index("dp")
    f = lax.axis_index("feat")
    block = ROWS // nf

    def feat_peer(k):
        return lax.rem(f + k, nf)

    def dp_peer(k):
        return lax.rem(d + k, nd)

    barrier = pltpu.get_barrier_semaphore()

    def greet_feat(k):
        pl.semaphore_signal(barrier, inc=1, device_id=(d, feat_peer(k)), device_id_type=MESH)

    def greet_dp(k):
        pl.semaphore_signal(barrier, inc=1, device_id=(dp_peer(k), f), device_id_type=MESH)

    each(nf, greet_feat)
    each(nd, greet_dp)
    pl.semaphore_wait(barrier, nf - 1 + nd - 1)

    def rows_at(index):
        return pl.ds(pl.multiple_of(index * block, 16), block)

    my_columns = pl.ds(pl.multiple_of(f * 128, 128), 128)

    def row_copy(k):
        to = feat_peer(k)
        return pltpu.make_async_remote_copy(
            src_ref=oa_ref.at[rows_at(to), :],
            dst_ref=rows_buf.at[:, my_columns],
            send_sem=send_a.at[k], recv_sem=recv_a.at[k],
            device_id=(d, to), device_id_type=MESH,
        )

    each(nf, lambda k: row_copy(k).start())
    rows_buf[:, my_columns] = oa_ref[rows_at(f), :]

    out_grad = grad_ref[...]
    degree = deg_ref[...].astype(jnp.float32)
    targets = degree.shape[0]
    column = lax.broadcasted_iota(jnp.int32, (targets, ROWS), 1)
    counts = jnp.zeros((targets, ROWS), jnp.float32)
    for j in range(adj_ref.shape[1]):
        match = (adj_ref[:, j:j + 1] == column) & (deg_ref[...] > j)
        counts = counts + jnp.where(match, 1.0, 0.0)
    grad_agg = contract_lanes(out_grad, w2n_ref[...]) / degree
    gh_buf[...] = lax.dot_general(
        counts, grad_agg, (((0,), (0,)), ((), ())),
        precision=lax.Precision.HIGHEST, preferred_element_type=jnp.float32,
    )
    gh_buf[:targets, :] += contract_lanes(out_grad, w2s_ref[...])

    each(nf, lambda k: row_copy(k).wait())
    pre = jnp.dot(rows_buf[...], w1_ref[...], preferred_element_type=jnp.float32)
    sig = 1.0 / (1.0 + jnp.exp(-pre))
    grad_pre = gh_buf[rows_at(f), :] * (sig * (1.0 + pre * (1.0 - sig)))
    hg_buf[rows_at(f), :256] = (pre * sig).astype(jnp.bfloat16)
    hg_buf[rows_at(f), 256:] = grad_pre.astype(jnp.bfloat16)

    def hidden_copy(k):
        return pltpu.make_async_remote_copy(
            src_ref=hg_buf.at[rows_at(f), :],
            dst_ref=hg_buf.at[rows_at(f), :],
            send_sem=send_h.at[k], recv_sem=recv_h.at[k],
            device_id=(d, feat_peer(k)), device_id_type=MESH,
        )

    def hidden_arrived(k):
        here = lax.rem(f - k + nf, nf)
        pltpu.make_async_remote_copy(
            src_ref=hg_buf.at[rows_at(f), :],
            dst_ref=hg_buf.at[rows_at(here), :],
            send_sem=send_h.at[k], recv_sem=recv_h.at[k],
            device_id=(d, feat_peer(k)), device_id_type=MESH,
        ).wait_recv()

    each(nf, lambda k: hidden_copy(k).start())
    each(nf, hidden_arrived)

    part1[...] = contract_rows(oa_ref[...], hg_buf[:, 256:])
    self_hidden = hg_buf[:targets, :256]
    agg_two = jnp.dot(counts.astype(jnp.bfloat16), hg_buf[:, :256], preferred_element_type=jnp.float32)
    agg_two = (agg_two / degree).astype(jnp.bfloat16)
    part2[0] = contract_rows(self_hidden, out_grad)
    part2[1] = contract_rows(agg_two, out_grad)

    def tile_of(part):
        return (
            pl.ds(pl.multiple_of(lax.div(part, 2) * 8, 8), 8),
            pl.ds(pl.multiple_of(lax.rem(part, 2) * 128, 128), 128),
        )

    def w1_copy(k):
        to = dp_peer(k)
        rows, lanes = tile_of(to)
        return pltpu.make_async_remote_copy(
            src_ref=part1.at[rows, lanes],
            dst_ref=in1.at[d],
            send_sem=send_r.at[k], recv_sem=recv_r.at[k],
            device_id=(to, f), device_id_type=MESH,
        )

    def w2_tile(part):
        return (
            lax.div(part, 4),
            pl.ds(pl.multiple_of(f * 16 + lax.rem(lax.div(part, 2), 2) * 8, 8), 8),
            pl.ds(pl.multiple_of(lax.rem(part, 2) * 128, 128), 128),
        )

    def keeper(part):
        return part * 4 + lax.rem(part, 4)

    my_part = lax.div(d, 4)
    keeping = keeper(my_part) == d

    def w2_copy(part):
        to = keeper(part)
        which, rows, lanes = w2_tile(part)
        return pltpu.make_async_remote_copy(
            src_ref=part2.at[which, rows, lanes],
            dst_ref=in2.at[d],
            send_sem=send_q.at[part], recv_sem=recv_q.at[d],
            device_id=(to, f), device_id_type=MESH,
        )

    def w2_send(part):
        @pl.when(keeper(part) != d)
        def _():
            w2_copy(part).start()

    lax.fori_loop(0, 8, lambda k, c: (w2_send(k), c)[1], 0)
    each(nd, lambda k: w1_copy(k).start())

    emb = jnp.dot(self_hidden, w2s_ref[...], preferred_element_type=jnp.float32)
    emb = emb + jnp.dot(agg_two, w2n_ref[...], preferred_element_type=jnp.float32)
    emb_ref[...] = emb.astype(jnp.bfloat16)

    def w2_in(k):
        here = lax.rem(d - k + nd, nd)
        pltpu.make_async_remote_copy(
            src_ref=in2.at[here], dst_ref=in2.at[here],
            send_sem=send_q.at[0], recv_sem=recv_q.at[here],
            device_id=(here, f), device_id_type=MESH,
        ).wait_recv()

    mine2 = pl.ds(pl.multiple_of(my_part // 2 * 8, 8), 8)
    lanes2 = pl.ds(pl.multiple_of(lax.rem(my_part, 2) * 128, 128), 128)

    def w2_out(k):
        return pltpu.make_async_remote_copy(
            src_ref=sum2, dst_ref=slice2.at[mine2, lanes2],
            send_sem=send_b.at[k], recv_sem=recv_b.at[my_part],
            device_id=(dp_peer(k), f), device_id_type=MESH,
        )

    @pl.when(keeping)
    def _():
        which, rows, lanes = w2_tile(my_part)
        in2[d] = part2[which, rows, lanes]
        each(nd, w2_in)
        sum2[...] = jnp.sum(in2[...], axis=0)
        each(nd, lambda k: w2_out(k).start())
        slice2[mine2, lanes2] = sum2[...]

    my_rows, my_lanes = tile_of(d)
    in1[d] = part1[my_rows, my_lanes]

    def w1_in(k):
        here = lax.rem(d - k + nd, nd)
        pltpu.make_async_remote_copy(
            src_ref=in1.at[here], dst_ref=in1.at[here],
            send_sem=send_r.at[k], recv_sem=recv_r.at[k],
            device_id=(here, f), device_id_type=MESH,
        ).wait_recv()

    each(nd, w1_in)
    sum1[...] = jnp.sum(in1[...], axis=0)
    gw1_ref[my_rows, my_lanes] = sum1[...]

    def w1_out(k):
        return pltpu.make_async_remote_copy(
            src_ref=sum1, dst_ref=gw1_ref.at[my_rows, my_lanes],
            send_sem=send_g.at[k], recv_sem=recv_g.at[k],
            device_id=(dp_peer(k), f), device_id_type=MESH,
        )

    each(nd, lambda k: w1_out(k).start())

    def w2_back(part):
        @pl.when(keeper(part) != d)
        def _():
            rows = pl.ds(pl.multiple_of(lax.div(part, 2) * 8, 8), 8)
            lanes = pl.ds(pl.multiple_of(lax.rem(part, 2) * 128, 128), 128)
            pltpu.make_async_remote_copy(
                src_ref=sum2, dst_ref=slice2.at[rows, lanes],
                send_sem=send_b.at[0], recv_sem=recv_b.at[part],
                device_id=(keeper(part), f), device_id_type=MESH,
            ).wait_recv()

    lax.fori_loop(0, 8, lambda k, c: (w2_back(k), c)[1], 0)
    gw2_ref[f] = slice2[...]

    def slice_copy(k):
        return pltpu.make_async_remote_copy(
            src_ref=slice2, dst_ref=gw2_ref.at[f],
            send_sem=send_f.at[k], recv_sem=recv_f.at[k],
            device_id=(d, feat_peer(k)), device_id_type=MESH,
        )

    each(nf, lambda k: slice_copy(k).start())

    def w1_back(k):
        rows, lanes = tile_of(lax.rem(d - k + nd, nd))
        pltpu.make_async_remote_copy(
            src_ref=sum1, dst_ref=gw1_ref.at[rows, lanes],
            send_sem=send_g.at[k], recv_sem=recv_g.at[k],
            device_id=(dp_peer(k), f), device_id_type=MESH,
        ).wait_recv()

    each(nd, w1_back)

    def slice_back(k):
        here = lax.rem(f - k + nf, nf)
        pltpu.make_async_remote_copy(
            src_ref=slice2, dst_ref=gw2_ref.at[here],
            send_sem=send_f.at[k], recv_sem=recv_f.at[k],
            device_id=(d, feat_peer(k)), device_id_type=MESH,
        ).wait_recv()

    each(nf, slice_back)

    each(nf, lambda k: hidden_copy(k).wait_send())
    each(nd, lambda k: w1_copy(k).wait_send())

    def w2_sent(part):
        @pl.when(keeper(part) != d)
        def _():
            w2_copy(part).wait_send()

    lax.fori_loop(0, 8, lambda k, c: (w2_sent(k), c)[1], 0)

    @pl.when(keeping)
    def _():
        each(nd, lambda k: w2_out(k).wait_send())

    each(nd, lambda k: w1_out(k).wait_send())
    each(nf, lambda k: slice_copy(k).wait_send())


def finish_kernel(emb_ref, gw1_ref, gw2_ref, out_emb, out_1s, out_1n, out_2s, out_2n):
    out_emb[...] = emb_ref[...]
    out_1s[...] = gw1_ref[:64, :]
    out_1n[...] = gw1_ref[64:, :]
    for i in range(gw2_ref.shape[0]):
        out_2s[16 * i:16 * i + 16, :] = gw2_ref[i, :16, :]
        out_2n[16 * i:16 * i + 16, :] = gw2_ref[i, 16:, :]


def tail(nd, nf, oa, w1, w2s, w2n, out_grad, adj_two, deg_two):
    vmem = pl.BlockSpec(memory_space=pltpu.VMEM)
    f32, bf16 = jnp.float32, jnp.bfloat16
    dma = pltpu.SemaphoreType.DMA
    emb, gw1, gw2 = pl.pallas_call(
        functools.partial(tail_kernel, nd, nf),
        out_shape=(
            jax.ShapeDtypeStruct((64, 256), bf16),
            jax.ShapeDtypeStruct((128, 256), f32),
            jax.ShapeDtypeStruct((nf, 32, 256), f32),
        ),
        in_specs=[vmem] * 7,
        out_specs=(vmem,) * 3,
        scratch_shapes=[
            pltpu.VMEM((ROWS // nf, nf * 128), bf16),
            pltpu.VMEM((ROWS, 256), f32),
            pltpu.VMEM((ROWS, 512), bf16),
            pltpu.VMEM((128, 256), f32),
            pltpu.VMEM((2, 256, 256), f32),
            pltpu.VMEM((nd, 8, 128), f32),
            pltpu.VMEM((nd, 8, 128), f32),
            pltpu.VMEM((8, 128), f32),
            pltpu.VMEM((8, 128), f32),
            pltpu.VMEM((32, 256), f32),
            dma((nf,)), dma((nf,)), dma((nf,)), dma((nf,)),
            dma((nd,)), dma((nd,)), dma((8,)), dma((nd,)),
            dma((nd,)), dma((nd,)), dma((nd,)), dma((8,)),
            dma((nf,)), dma((nf,)),
        ],
        compiler_params=pltpu.CompilerParams(
            collective_id=1, has_side_effects=True, vmem_limit_bytes=32 * 1024 * 1024
        ),
        name="tail",
    )(oa, w1, w2s, w2n, out_grad, adj_two, deg_two)
    return pl.pallas_call(
        finish_kernel,
        out_shape=(
            jax.ShapeDtypeStruct((64, 256), bf16),
            jax.ShapeDtypeStruct((64, 256), f32),
            jax.ShapeDtypeStruct((64, 256), f32),
            jax.ShapeDtypeStruct((256, 256), f32),
            jax.ShapeDtypeStruct((256, 256), f32),
        ),
        in_specs=[vmem] * 3,
        out_specs=(vmem,) * 5,
        name="finish",
    )(emb, gw1, gw2)


def local(
    nd, nf,
    features, request_rows, self_slots, adj_one, deg_one, adj_two, deg_two,
    w1_self, w1_neigh, w2_self, w2_neigh, out_grad,
):
    columns_here = features.shape[1]
    w1 = lax.all_gather(jnp.concatenate([w1_self, w1_neigh], axis=0), "feat", tiled=True)
    asked_rows = lax.all_to_all(request_rows, "dp", split_axis=1, concat_axis=0, tiled=True)
    picked = features[asked_rows.reshape(-1)].reshape(asked_rows.shape + (columns_here,))
    replies = lax.all_to_all(picked, "dp", split_axis=0, concat_axis=1, tiled=True)
    sampled = replies.reshape(-1, columns_here)
    own_rows = sampled[self_slots[0]]
    agg_one = neighbour_mean(sampled, adj_one[0], deg_one[0])
    oa = jnp.concatenate([own_rows, agg_one], axis=1)
    oa = jnp.pad(oa, ((0, ROWS - oa.shape[0]), (0, 0)))
    return tail(nd, nf, oa, w1, w2_self, w2_neigh, out_grad, adj_two[0], deg_two[0][:, None])


def solution(mesh):
    return jax.shard_map(
        functools.partial(local, mesh.shape["dp"], mesh.shape["feat"]),
        mesh=mesh,
        in_specs=(
            P("dp", "feat"),
            P("dp", None, None),
            P("dp", None),
            P("dp", None, None),
            P("dp", None),
            P("dp", None, None),
            P("dp", None),
            P("feat", None),
            P("feat", None),
            P(),
            P(),
            P("dp", None),
        ),
        out_specs=(P("dp", None), P("feat", None), P("feat", None), P(), P()),
        check_vma=False,
    )
```

time: 473 us -> 256 us (0.54)
  waiting for transfers between devices: 318 us -> 52.8 us
  Pallas kernels: 0 us -> 72.7 us
  other arithmetic: 15.6 us -> 6.67 us
  local copies, waits for them, and re-layouts: 101 us -> 94.1 us
  matrix products: 6.13 us -> 0 us
    psum x2 -> x0, waiting for transfers between devices: 265 us -> none  [the longest x1 154 us: local(): lax.psum((grad_one_self, grad_one_neigh, grad_two_self, grad_two_neigh),...]
    pallas_call x0 -> x2, Pallas kernels: none -> 72.7 us  [the longest x1 70.7 us: tail(): pl.pallas_call(functools.partial(tail_kernel, nd, nf), out_shape=(jax.Sha...]
    scatter-add x1 -> x0, other arithmetic: 7.94 us -> none  [neighbour_spread(): return empty.at[neighbours.reshape(-1)].add(weighted)]
    dot_general x10 -> x0, matrix products: 6.13 us -> none  [the longest x1 1.1 us: local(): jnp.dot(agg_one, w1_neigh, preferred_element_type=jnp.float32)]
    gather x2 -> x1, local copies, waits for them, and re-layouts: 17.2 us -> 14.4 us  [neighbour_mean(): gathered = source[neighbours].astype(jnp.float32)]
  transfers between devices with their start and end apart: 4 -> 3, of which waited for: 4 -> 2; matrix products, arithmetic and copies ran while one was open for 3% -> 13% of each run, Pallas kernels for 0% -> 0%
where the time goes in v1:
time: 256 us; the launch traced here: 255 us
  local copies, waits for them, and re-layouts  94.1 us (37%)
  Pallas kernels  72.7 us (28%)
  waiting for transfers between devices  52.8 us (21%)
  starting transfers between devices  14.7 us (6%)
  between operations  14.3 us (6%)
  other arithmetic  6.67 us (3%)
    pallas_call x1, Pallas kernels, tail(): pl.pallas_call(functools.partial(tail_kernel, nd, nf), out_shape=(jax.Sha...  70.7 us
    gather x1, local copies, waits for them, and re-layouts, local(): features[asked_rows.reshape(-1)].reshape(asked_rows.shape + (columns_here,))  57.4 us
    all_to_all x1, waiting for transfers between devices, local(): lax.all_to_all(picked, 'dp', split_axis=0, concat_axis=1, tiled=True)  45.2 us
    gather x1, local copies, waits for them, and re-layouts, neighbour_mean(): gathered = source[neighbours].astype(jnp.float32)  14.4 us
    all_to_all x1, starting transfers between devices, local(): lax.all_to_all(request_rows, 'dp', split_axis=1, concat_axis=0, tiled=True)  10.5 us
    all_to_all x1, waiting for transfers between devices, local(): lax.all_to_all(request_rows, 'dp', split_axis=1, concat_axis=0, tiled=True)  7.59 us
    unnamed x31, local copies, waits for them, and re-layouts  6.15 us
    reduce_sum x1, other arithmetic, neighbour_mean(): return jnp.sum(gathered * weights[:, :, None], axis=1).astype(jnp.bfloat16)  5.74 us
  transfers between devices with their start and end apart: 3, of which 2 were waited for; matrix products, arithmetic and copies ran while one was open for 13% of the time, Pallas kernels for 0%

profile of v1, /device:TPU:1, one launch (start us, length us, event | category | flops | bytes accessed | tf_op | source)
XLA Modules:
  0.0 255.2 jit_solution(6811419253971662531)
XLA Ops:
  7.2 1.5 copy.31
  8.7 10.5 %all-to-all-start = ((s32[1,32,512]{2,0,1:T(1,128)}), s32[1,32,512]{2,0,1:T(1,128)S(1)}, u32[]{:S(2)}, u32[]{:S(2)}) async-start(s32[1,32,512]{2,0,1:T(1,128)} %copy.31), calls=%async_computation | async-start | bytes 131072 | tf_op jit(solution)/shard_map/all_to_all | solution.py:366
  19.2 1.2 copy.32
  20.4 7.6 %all-to-all-done = s32[1,32,512]{2,0,1:T(1,128)S(1)} async-done(((s32[1,32,512]{2,0,1:T(1,128)}), s32[1,32,512]{2,0,1:T(1,128)S(1)}, u32[]{:S(2)}, u32[]{:S(2)}) %all-to-all-start) | async-done | bytes 65568 | tf_op jit(solution)/shard_map/all_to_all | solution.py:366
  28.1 57.4 %gather_fusion = bf16[16384,64]{1,0:T(8,128)(2,1)} fusion(bf16[2048,64]{1,0:T(8,128)(2,1)S(1)} %copy.32, s32[16384]{0:T(1024)S(1)} %broadcast_clamp_fusion), kind=kCustom, calls=%fused_computation | custom fusion | bytes 4259840 | tf_op jit(solution)/shard_map/gather | solution.py:367
  85.6 4.8 %copy.33 = bf16[32,1,512,64]{2,3,1,0:T(8,128)(2,1)} copy(bf16[32,1,512,64]{3,2,0,1:T(8,128)(2,1)} %bitcast.15) | data formatting | bytes 4194304 | tf_op jit(solution)/shard_map/reshape | solution.py:367
  90.4 4.1 %all-to-all-start.1 = ((bf16[32,1,512,64]{2,3,1,0:T(8,128)(2,1)}), bf16[32,1,512,64]{2,3,1,0:T(8,128)(2,1)S(1)}, u32[]{:S(2)}, u32[]{:S(2)}) async-start(bf16[32,1,512,64]{2,3,1,0:T(8,128)(2,1)} %copy.33), calls=%async_computation.1 | async-start | bytes 4194304 | tf_op jit(solution)/shard_map/all_to_all | solution.py:368
  94.6 0.6 pad_maximum_fusion
  95.5 0.2 copy.36
  95.8 0.2 copy.35
  95.9 0.3 reshape.179
  96.3 45.2 %all-to-all-done.1 = bf16[32,1,512,64]{2,3,1,0:T(8,128)(2,1)S(1)} async-done(((bf16[32,1,512,64]{2,3,1,0:T(8,128)(2,1)}), bf16[32,1,512,64]{2,3,1,0:T(8,128)(2,1)S(1)}, u32[]{:S(2)}, u32[]{:S(2)}) %all-to-all-start.1) | async-done | bytes 2097184 | tf_op jit(solution)/shard_map/all_to_all | solution.py:368
  141.4 3.2 %copy.34 = bf16[32,1,512,64]{3,2,0,1:T(8,128)(2,1)} copy(bf16[32,1,512,64]{2,3,1,0:T(8,128)(2,1)S(1)} %all-to-all-done.1) | data formatting | bytes 4194304 | tf_op jit(solution)/shard_map/all_to_all | solution.py:368
  144.6 4.5 %gather_fusion.1 = bf16[704,64]{1,0:T(8,128)(2,1)S(1)} fusion(bf16[16384,64]{1,0:T(8,128)(2,1)} %bitcast.13, s32[1024]{0:T(1024)S(1)} %pad_clamp_fusion.1), kind=kCustom, calls=%fused_computation.1 | custom fusion | bytes 183040 | tf_op jit(solution)/shard_map/gather | solution.py:370
  149.1 14.4 %gather_fusion.2 = bf16[7040,64]{1,0:T(8,128)(2,1)S(1)} fusion(bf16[16384,64]{1,0:T(8,128)(2,1)} %bitcast.14, s32[7168]{0:T(1024)S(1)} %pad_clamp_fusion), kind=kCustom, calls=%fused_computation.2 | custom fusion | bytes 1830400 | tf_op jit(solution)/shard_map/gather | solution.py:22
  163.5 2.9 %reshape.186 = f32[704,10,64]{2,1,0:T(8,128)} reshape(bf16[7040,64]{1,0:T(8,128)(2,1)S(1)} %gather_fusion.2) | data formatting | bytes 2703360 | tf_op jit(solution)/shard_map/convert_element_type | solution.py:22
  166.5 5.7 %multiply_reduce_fusion = bf16[704,64]{1,0:T(8,128)(2,1)S(1)} fusion(f32[704,10,64]{2,1,0:T(8,128)} %reshape.186, f32[704,10]{1,0:T(8,128)S(1)} %copy.36), kind=kLoop, calls=%fused_computation.3 | loop fusion | flops 856064 | bytes 1920512 | tf_op jit(solution)/shard_map/reduce_sum | solution.py:23
  172.2 0.1 fusion.2.oa_ref
  172.4 1.2 copy-done
  173.6 70.7 %tail.1 = (bf16[64,256]{1,0:T(8,128)(2,1)S(1)}, f32[128,256]{1,0:T(8,128)S(1)}, f32[16,32,256]{2,1,0:T(8,128)S(1)}) custom-call(bf16[768,128]{1,0:T(8,128)(2,1)S(1)} %fusion.2.oa_ref, bf16[2048,256]{1,0:T(8,128)(2,1)S(1)} %copy-done, bf16[256,256]{1,0:T(8,128)(2,1)S(1)} %copy-done.2, bf16[256,256]{1,0:T(8,128)(2,1)S(1)} %copy-done.3, ...), custom_call_target="tpu_custom_call" | custom-call | tf_op jit(solution)/shard_map/tail/pallas_call | solution.py:314
  244.4 0.8 copy-done.1
  245.2 0.6 copy-done.4
  245.8 0.6 copy-done.6
  246.4 2.0 finish.1
  (38 shorter events, 0.5 us)
Async XLA Ops:
  8.7 19.3 %all-to-all-start = ((s32[1,32,512]{2,0,1:T(1,128)}), s32[1,32,512]{2,0,1:T(1,128)S(1)}, u32[]{:S(2)}, u32[]{:S(2)}) async-start(s32[1,32,512]{2,0,1:T(1,128)} %copy.31), calls=%async_computation | async-start | bytes 131072 | tf_op jit(solution)/shard_map/all_to_all | solution.py:366
  85.5 9.1 %copy-start.7 = (bf16[64,256]{1,0:T(8,128)(2,1)S(1)}, bf16[64,256]{1,0:T(8,128)(2,1)}, u32[]{:S(2)}) copy-start(bf16[64,256]{1,0:T(8,128)(2,1)} %param.20) | copy-start | bytes 98308
  85.5 9.1 %copy-start.8 = (bf16[64,256]{1,0:T(8,128)(2,1)S(1)}, bf16[64,256]{1,0:T(8,128)(2,1)}, u32[]{:S(2)}) copy-start(bf16[64,256]{1,0:T(8,128)(2,1)} %param.19) | copy-start | bytes 98308
  85.5 9.7 %copy-start.12 = (s32[1,704]{1,0:T(1,128)S(1)}, s32[1,704]{1,0:T(1,128)}, u32[]{:S(2)}) copy-start(s32[1,704]{1,0:T(1,128)} %param.16) | copy-start | bytes 8452
  85.5 9.8 %copy-start.10 = (s32[1,64,10]{1,0,2:T(1,128)S(1)}, s32[1,64,10]{1,0,2:T(1,128)}, u32[]{:S(2)}) copy-start(s32[1,64,10]{1,0,2:T(1,128)} %param.17) | copy-start | bytes 7684
  85.5 9.9 %copy-start.13 = (s32[1,64]{1,0:T(1,128)S(1)}, s32[1,64]{1,0:T(1,128)}, u32[]{:S(2)}) copy-start(s32[1,64]{1,0:T(1,128)} %param.18) | copy-start | bytes 772
  85.6 10.2 %copy-start.9 = (s32[1,704,10]{1,0,2:T(1,128)S(1)}, s32[1,704,10]{1,0,2:T(1,128)}, u32[]{:S(2)}) copy-start(s32[1,704,10]{1,0,2:T(1,128)} %param.15) | copy-start | bytes 84484
  90.4 5.8 %copy-start.11 = (s32[1,704]{1,0:T(1,128)S(1)}, s32[1,704]{1,0:T(1,128)}, u32[]{:S(2)}) copy-start(s32[1,704]{1,0:T(1,128)} %param.14) | copy-start | bytes 8452
  90.4 51.0 %all-to-all-start.1 = ((bf16[32,1,512,64]{2,3,1,0:T(8,128)(2,1)}), bf16[32,1,512,64]{2,3,1,0:T(8,128)(2,1)S(1)}, u32[]{:S(2)}, u32[]{:S(2)}) async-start(bf16[32,1,512,64]{2,3,1,0:T(8,128)(2,1)} %copy.33), calls=%async_computation.1 | async-start | bytes 4194304 | tf_op jit(solution)/shard_map/all_to_all | solution.py:368
  94.5 77.8 %all-gather.2.cloned.1.call-start = ((), (), s32[]{:S(2)}) async-start(), calls=%async_computation.2 | async-start | bytes 1114112 | tf_op jit(solution)/shard_map/all_gather | solution.py:365
  166.5 5.9 %copy-start.2 = (bf16[256,256]{1,0:T(8,128)(2,1)S(1)}, bf16[256,256]{1,0:T(8,128)(2,1)}, u32[]{:S(2)}) copy-start(bf16[256,256]{1,0:T(8,128)(2,1)} %w2s_ref.1) | copy-start | bytes 393220
  166.5 5.9 %copy-start.3 = (bf16[256,256]{1,0:T(8,128)(2,1)S(1)}, bf16[256,256]{1,0:T(8,128)(2,1)}, u32[]{:S(2)}) copy-start(bf16[256,256]{1,0:T(8,128)(2,1)} %w2n_ref.1) | copy-start | bytes 393220
  166.5 5.9 %copy-start.5 = (bf16[64,256]{1,0:T(8,128)(2,1)S(1)}, bf16[64,256]{1,0:T(8,128)(2,1)}, u32[]{:S(2)}) copy-start(bf16[64,256]{1,0:T(8,128)(2,1)} %grad_ref.1) | copy-start | bytes 98308
  172.4 1.2 copy-start
  244.4 0.8 copy-start.1
  245.2 0.6 copy-start.4
  245.8 0.6 copy-start.6
Sparse Core Ops, SparseCore 0:
  98.1 48.3 all-gather.1

commit v2 on v1

--- a/solution.py
+++ b/solution.py
@@ -9,18 +9,6 @@
 
 MESH = pl.DeviceIdType.MESH
 ROWS = 768
-
-
-def slot_weights(neighbours, degrees):
-    fanout = neighbours.shape[-1]
-    present = jnp.arange(fanout, dtype=jnp.int32)[None, :] < degrees[:, None]
-    return present.astype(jnp.float32) / degrees[:, None].astype(jnp.float32)
-
-
-def neighbour_mean(source, neighbours, degrees):
-    weights = slot_weights(neighbours, degrees)
-    gathered = source[neighbours].astype(jnp.float32)
-    return jnp.sum(gathered * weights[:, :, None], axis=1).astype(jnp.bfloat16)
 
 
 def contract_rows(a, b):
@@ -356,21 +344,276 @@
     )(emb, gw1, gw2)
 
 
+def front_kernel(
+    nd, nf, feat_ref, req_ref, w1_ref, samp_ref, w1_out,
+    blocks, req_by_x, req_in, stage,
+    up_send, up_recv, down_send, down_recv, req_send, req_recv,
+    x_send, x_recv, w1_send, w1_recv, local_sem,
+):
+    d = lax.axis_index("dp")
+    f = lax.axis_index("feat")
+    nx, ny = 4, nd // 4
+    x, y = lax.rem(d, nx), lax.div(d, nx)
+
+    def at_x(j):
+        return lax.rem(x + j, nx)
+
+    def at_y(s):
+        return lax.rem(y + s + ny, ny)
+
+    def feat_peer(k):
+        return lax.rem(f + k, nf)
+
+    barrier = pltpu.get_barrier_semaphore()
+
+    def greet(to):
+        pl.semaphore_signal(barrier, inc=1, device_id=to, device_id_type=MESH)
+
+    for j in range(1, nx):
+        greet((y * nx + at_x(j), f))
+    greet((at_y(1) * nx + x, f))
+    greet((at_y(-1) * nx + x, f))
+    each(nf, lambda k: greet((d, feat_peer(k))))
+
+    for q in range(4):
+        blocks[y, 64 * q:64 * q + 64, :] = feat_ref[:, 512 * q:512 * q + 512]
+    for owner in range(nd):
+        req_by_x[owner % nx, owner // nx:owner // nx + 1, :] = req_ref[owner:owner + 1, :]
+
+    pl.semaphore_wait(barrier, nx - 1 + 2 + nf - 1)
+
+    def req_copy(j):
+        to = at_x(j)
+        return pltpu.make_async_remote_copy(
+            src_ref=req_by_x.at[to], dst_ref=req_in.at[x],
+            send_sem=req_send.at[j], recv_sem=req_recv.at[x],
+            device_id=(y * nx + to, f), device_id_type=MESH,
+        )
+
+    def half(source, h):
+        return blocks.at[source, pl.ds(128 * h, 128), :]
+
+    def up_copy(t, source):
+        return pltpu.make_async_remote_copy(
+            src_ref=half(source, t % 2), dst_ref=half(source, t % 2),
+            send_sem=up_send.at[t], recv_sem=up_recv.at[t],
+            device_id=(at_y(1) * nx + x, f), device_id_type=MESH,
+        )
+
+    def down_copy(t, source):
+        return pltpu.make_async_remote_copy(
+            src_ref=half(source, 1 - t % 2), dst_ref=half(source, 1 - t % 2),
+            send_sem=down_send.at[t], recv_sem=down_recv.at[t],
+            device_id=(at_y(-1) * nx + x, f), device_id_type=MESH,
+        )
+
+    def w1_copy(k):
+        return pltpu.make_async_remote_copy(
+            src_ref=w1_ref, dst_ref=w1_out.at[f],
+            send_sem=w1_send.at[k], recv_sem=w1_recv.at[k],
+            device_id=(d, feat_peer(k)), device_id_type=MESH,
+        )
+
+    for j in range(1, nx):
+        req_copy(j).start()
+    for t in range(2):
+        up_copy(t, y).start()
+        down_copy(t, y).start()
+    each(nf, lambda k: w1_copy(k).start())
+    own_w1 = pltpu.make_async_copy(w1_ref, w1_out.at[f], local_sem.at[ny])
+    own_w1.start()
+    req_in[x] = req_by_x[x]
+    for j in range(1, nx):
+        source = at_x(j)
+        pltpu.make_async_remote_copy(
+            src_ref=req_by_x.at[source], dst_ref=req_in.at[source],
+            send_sem=req_send.at[j], recv_sem=req_recv.at[source],
+            device_id=(y * nx + source, f), device_id_type=MESH,
+        ).wait_recv()
+
+    def x_copy(source, j):
+        slot = source * nx + x
+        return pltpu.make_async_remote_copy(
+            src_ref=stage.at[source, j], dst_ref=samp_ref.at[slot],
+            send_sem=x_send.at[source * nx + j], recv_sem=x_recv.at[slot],
+            device_id=(y * nx + at_x(j), f), device_id_type=MESH,
+        )
+
+    def own_copy(source):
+        return pltpu.make_async_copy(
+            stage.at[source, 0], samp_ref.at[source * nx + x], local_sem.at[source]
+        )
+
+    node = lax.broadcasted_iota(jnp.int32, (512, 512), 0)
+
+    def pick(source, j):
+        asked = req_in[at_x(j), pl.ds(source, 1), :]
+        low, quarter = asked & 511, asked >> 9
+        one_hot = jnp.where(node == low, 1.0, 0.0).astype(jnp.bfloat16)
+        rows = jnp.dot(blocks[source], one_hot, preferred_element_type=jnp.float32)
+        chosen = rows[192:256, :]
+        for q in range(3):
+            chosen = jnp.where(quarter == q, rows[64 * q:64 * q + 64, :], chosen)
+        stage[source, j] = chosen.astype(jnp.bfloat16)
+
+    def process(count, source_of):
+        def step(k, carry):
+            source = source_of(lax.div(k, nx))
+            j = lax.rem(k + 1, nx)
+            pick(source, j)
+
+            @pl.when(j > 0)
+            def _():
+                x_copy(source, j).start()
+
+            @pl.when(j == 0)
+            def _():
+                own_copy(source).start()
+
+            return carry
+
+        lax.fori_loop(0, count * nx, step, 0)
+
+    process(1, lambda i: y)
+    for s in range(ny // 2):
+        below, above = at_y(-1 - s), at_y(1 + s)
+        for h in range(2 if s < ny // 2 - 1 else 1):
+            t = 2 * s + h
+            up_copy(t, below).wait_recv()
+            if t + 2 < ny - 1:
+                up_copy(t + 2, below).start()
+            down_copy(t, above).wait_recv()
+            if t + 2 < ny - 1:
+                down_copy(t + 2, above).start()
+        if s < ny // 2 - 1:
+            process(2, lambda i: lax.rem(y + (2 * i - 1) * (1 + s) + ny, ny))
+        else:
+            process(1, lambda i: below)
+
+    def x_back(source):
+        for j in range(1, nx):
+            slot = source * nx + at_x(j)
+            pltpu.make_async_remote_copy(
+                src_ref=stage.at[source, j], dst_ref=samp_ref.at[slot],
+                send_sem=x_send.at[source * nx + j], recv_sem=x_recv.at[slot],
+                device_id=(y * nx + at_x(j), f), device_id_type=MESH,
+            ).wait_recv()
+            x_copy(source, j).wait_send()
+        own_copy(source).wait()
+
+    lax.fori_loop(0, ny, lambda k, c: (x_back(k), c)[1], 0)
+
+    def w1_back(k):
+        here = lax.rem(f - k + nf, nf)
+        pltpu.make_async_remote_copy(
+            src_ref=w1_ref, dst_ref=w1_out.at[here],
+            send_sem=w1_send.at[k], recv_sem=w1_recv.at[k],
+            device_id=(d, here), device_id_type=MESH,
+        ).wait_recv()
+        w1_copy(k).wait_send()
+
+    each(nf, w1_back)
+    own_w1.wait()
+    for j in range(1, nx):
+        req_copy(j).wait_send()
+    for t in range(ny - 1):
+        up_copy(t, at_y(-(t // 2))).wait_send()
+        down_copy(t, at_y(t // 2)).wait_send()
+
+
+def front(nd, nf, features, request_rows, w1):
+    vmem = pl.BlockSpec(memory_space=pltpu.VMEM)
+    anywhere = pl.BlockSpec(memory_space=pl.ANY)
+    bf16, i32 = jnp.bfloat16, jnp.int32
+    dma = pltpu.SemaphoreType.DMA
+    ny = nd // 4
+    return pl.pallas_call(
+        functools.partial(front_kernel, nd, nf),
+        out_shape=(
+            jax.ShapeDtypeStruct((nd, 64, 512), bf16),
+            jax.ShapeDtypeStruct((nf, 128, 256), bf16),
+        ),
+        in_specs=[vmem] * 3,
+        out_specs=(anywhere, anywhere),
+        scratch_shapes=[
+            pltpu.VMEM((ny, 256, 512), bf16),
+            pltpu.VMEM((4, ny, 512), i32),
+            pltpu.VMEM((4, ny, 512), i32),
+            pltpu.VMEM((ny, 4, 64, 512), bf16),
+            dma((ny - 1,)), dma((ny - 1,)), dma((ny - 1,)), dma((ny - 1,)),
+            dma((4,)), dma((4,)), dma((nd,)), dma((nd,)),
+            dma((nf,)), dma((nf,)), dma((ny + 1,)),
+        ],
+        compiler_params=pltpu.CompilerParams(
+            collective_id=2, has_side_effects=True, vmem_limit_bytes=32 * 1024 * 1024
+        ),
+        name="front",
+    )(features.T, request_rows, w1)
+
+
+def mean_kernel(slots_ref, samp_ref, scale_ref, out_ref, table, own, total):
+    pairs, width, cap = samp_ref.shape
+
+    def unpack(p, carry):
+        both = samp_ref[p].astype(jnp.float32).T
+        table[pl.ds(pl.multiple_of(2 * cap * p, 8), cap), :] = both
+        table[pl.ds(pl.multiple_of(2 * cap * p + cap, 8), cap), :] = pltpu.roll(both, 64, 1)
+        return carry
+
+    lax.fori_loop(0, pairs, unpack, 0)
+    table[2 * cap * pairs:, :] = jnp.zeros((8, width), jnp.float32)
+    rows = scale_ref.shape[0]
+    lists = slots_ref.shape[0] // rows
+
+    def gather(block, carry):
+        for r in range(8):
+            i = block * 8 + r
+            own[pl.ds(i, 1), :] = table[pl.ds(slots_ref[i], 1), :]
+            terms = [table[pl.ds(slots_ref[j * rows + i], 1), :] for j in range(1, lists)]
+            while len(terms) > 1:
+                terms = [sum(terms[k:k + 2][1:], terms[k]) for k in range(0, len(terms), 2)]
+            total[pl.ds(i, 1), :] = terms[0]
+        return carry
+
+    lax.fori_loop(0, rows // 8, gather, 0)
+    lane = lax.broadcasted_iota(jnp.int32, (rows, width), 1)
+    mean = pltpu.roll(total[...] * scale_ref[...], 64, 1)
+    out_ref[:rows, :] = jnp.where(lane < 64, own[...], mean).astype(jnp.bfloat16)
+    out_ref[rows:, :] = jnp.zeros((ROWS - rows, width), jnp.bfloat16)
+
+
+def neighbour_mean(sampled, self_slots, neighbours, degrees):
+    nd, columns, cap = sampled.shape
+    rows, fanout = neighbours.shape
+    order = jnp.arange(fanout, dtype=jnp.int32)[:, None]
+    listed = jnp.where(order < degrees[None, :], neighbours.T, nd * cap)
+    slots = jnp.concatenate([self_slots[None, :], listed], axis=0).reshape(-1)
+    scale = 1.0 / degrees.astype(jnp.float32)[:, None]
+    vmem = pl.BlockSpec(memory_space=pltpu.VMEM)
+    return pl.pallas_call(
+        mean_kernel,
+        out_shape=jax.ShapeDtypeStruct((ROWS, 2 * columns), jnp.bfloat16),
+        in_specs=[pl.BlockSpec(memory_space=pltpu.SMEM), vmem, vmem],
+        out_specs=vmem,
+        scratch_shapes=[
+            pltpu.VMEM((nd * cap + 8, 2 * columns), jnp.float32),
+            pltpu.VMEM((rows, 2 * columns), jnp.float32),
+            pltpu.VMEM((rows, 2 * columns), jnp.float32),
+        ],
+        compiler_params=pltpu.CompilerParams(vmem_limit_bytes=32 * 1024 * 1024),
+        name="mean",
+    )(slots, sampled.reshape(nd // 2, 2 * columns, cap), scale)
+
+
 def local(
     nd, nf,
     features, request_rows, self_slots, adj_one, deg_one, adj_two, deg_two,
     w1_self, w1_neigh, w2_self, w2_neigh, out_grad,
 ):
-    columns_here = features.shape[1]
-    w1 = lax.all_gather(jnp.concatenate([w1_self, w1_neigh], axis=0), "feat", tiled=True)
-    asked_rows = lax.all_to_all(request_rows, "dp", split_axis=1, concat_axis=0, tiled=True)
-    picked = features[asked_rows.reshape(-1)].reshape(asked_rows.shape + (columns_here,))
-    replies = lax.all_to_all(picked, "dp", split_axis=0, concat_axis=1, tiled=True)
-    sampled = replies.reshape(-1, columns_here)
-    own_rows = sampled[self_slots[0]]
-    agg_one = neighbour_mean(sampled, adj_one[0], deg_one[0])
-    oa = jnp.concatenate([own_rows, agg_one], axis=1)
-    oa = jnp.pad(oa, ((0, ROWS - oa.shape[0]), (0, 0)))
+    w1 = jnp.concatenate([w1_self, w1_neigh], axis=0)
+    sampled, w1 = front(nd, nf, features, request_rows[0], w1)
+    oa = neighbour_mean(sampled, self_slots[0], adj_one[0], deg_one[0])
+    w1 = w1.reshape(-1, w1.shape[-1])
     return tail(nd, nf, oa, w1, w2_self, w2_neigh, out_grad, adj_two[0], deg_two[0][:, None])
 
 

time: 256 us -> 134 us (0.52)
  local copies, waits for them, and re-layouts: 94.1 us -> 9.23 us
  waiting for transfers between devices: 52.8 us -> 0 us
  Pallas kernels: 72.7 us -> 119 us
  starting transfers between devices: 14.7 us -> 0 us
  between operations: 14.3 us -> 0.71 us
    gather x3 -> x0, local copies, waits for them, and re-layouts: 76.3 us -> none  [the longest x1 57.4 us: local(): features[asked_rows.reshape(-1)].reshape(asked_rows.shape + (columns_here,))]
    pallas_call x0 -> x2, Pallas kernels: none -> 55.1 us  [the longest x1 44.3 us: front(): pl.pallas_call(functools.partial(front_kernel, nd, nf), out_shape=(jax.Sh...]
    all_to_all x2 -> x0, waiting for transfers between devices: 52.7 us -> none  [the longest x1 45.2 us: local(): lax.all_to_all(picked, 'dp', split_axis=0, concat_axis=1, tiled=True)]
    all_to_all x2 -> x0, starting transfers between devices: 14.6 us -> none  [the longest x1 10.5 us: local(): lax.all_to_all(request_rows, 'dp', split_axis=1, concat_axis=0, tiled=True)]
    pallas_call x1, Pallas kernels: 70.7 us -> 62.2 us  [tail(): pl.pallas_call(functools.partial(tail_kernel, nd, nf), out_shape=(jax.Sha...]
    reduce_sum x1 -> x0, other arithmetic: 5.74 us -> none  [neighbour_mean(): return jnp.sum(gathered * weights[:, :, None], axis=1).astype(jnp.bfloat16)]
    reshape x1, local copies, waits for them, and re-layouts: 4.82 us -> 0.88 us  [neighbour_mean(): slots = jnp.concatenate([self_slots[None, :], listed], axis=0).reshape(-1)]
    all_to_all x1 -> x0, local copies, waits for them, and re-layouts: 3.16 us -> none  [local(): lax.all_to_all(picked, 'dp', split_axis=0, concat_axis=1, tiled=True)]
  transfers between devices with their start and end apart: 3 -> 0, of which waited for: 2 -> 0; matrix products, arithmetic and copies ran while one was open for 13% -> 0% of each run, Pallas kernels for 0% -> 0%
where the time goes in v2:
time: 134 us
  Pallas kernels  119 us (89%)
  local copies, waits for them, and re-layouts  9.23 us (7%)
  other arithmetic  4.27 us (3%)
    pallas_call x1, Pallas kernels, tail(): pl.pallas_call(functools.partial(tail_kernel, nd, nf), out_shape=(jax.Sha...  62.2 us
    pallas_call x1, Pallas kernels, front(): pl.pallas_call(functools.partial(front_kernel, nd, nf), out_shape=(jax.Sh...  44.3 us
    pallas_call x1, Pallas kernels, neighbour_mean(): pl.pallas_call(mean_kernel, out_shape=jax.ShapeDtypeStruct((ROWS, 2 * col...  10.8 us
    unnamed x25, local copies, waits for them, and re-layouts  8.08 us

profile of v2, /device:TPU:1, one launch (start us, length us, event | category | flops | bytes accessed | tf_op | source)
XLA Modules:
  0.0 133.5 jit_solution(12049965150022384945)
XLA Ops:
  0.7 0.8 pad_maximum_fusion.w1_ref
  1.4 0.9 copy-done.3
  2.4 0.8 copy-done.7
  3.2 44.3 %front.1 = (bf16[32,64,512]{2,1,0:T(8,128)(2,1)S(1)}, bf16[16,128,256]{2,1,0:T(8,128)(2,1)S(1)}) custom-call(bf16[64,2048]{1,0:T(8,128)(2,1)S(1)} %bitcast.14, s32[32,512]{1,0:T(8,128)S(1)} %bitcast.16, bf16[128,256]{1,0:T(8,128)(2,1)S(1)} %pad_maximum_fusion.w1_ref), custom_call_target="tpu_custom_call" | custom-call | tf_op jit(solution)/shard_map/front/pallas_call | solution.py:530
  47.6 0.7 divide_bitcast_fusion
  48.3 0.2 copy.19.scale_ref
  48.4 0.7 reduce
  49.2 0.8 bitcast_select_fusion
  49.9 1.3 pad_add_fusion
  51.2 0.9 reshape.36.slots_ref
  52.1 10.8 %mean.1.oa_ref = bf16[768,128]{1,0:T(8,128)(2,1)S(1)} custom-call(s32[7744]{0:T(1024)S(1)} %reshape.36.slots_ref, bf16[16,128,512]{2,1,0:T(8,128)(2,1)S(1)} %bitcast.12, f32[704,1]{1,0:T(8,128)S(1)} %copy.19.scale_ref), custom_call_target="tpu_custom_call" | custom-call | tf_op jit(solution)/shard_map/mean/pallas_call | solution.py:593
  62.9 0.0 copy-start
  62.9 0.7 copy-done
  63.6 0.1 copy.20
  63.7 0.1 copy.21.deg_ref
  63.8 0.9 copy-done.1
  64.7 0.9 copy-done.4
  65.6 0.9 copy-done.5
  66.5 0.8 copy-done.8
  67.3 62.2 %tail.1 = (bf16[64,256]{1,0:T(8,128)(2,1)S(1)}, f32[128,256]{1,0:T(8,128)S(1)}, f32[16,32,256]{2,1,0:T(8,128)S(1)}) custom-call(bf16[768,128]{1,0:T(8,128)(2,1)S(1)} %copy-done.1, bf16[2048,256]{1,0:T(8,128)(2,1)S(1)} %bitcast.13, bf16[256,256]{1,0:T(8,128)(2,1)S(1)} %copy-done.4, bf16[256,256]{1,0:T(8,128)(2,1)S(1)} %copy-done.5, ...), custom_call_target="tpu_custom_call" | custom-call | tf_op jit(solution)/shard_map/tail/pallas_call | solution.py:302
  129.5 0.8 copy-done.2
  130.3 0.6 copy-done.6
  131.0 0.6 copy-done.9
  131.6 2.0 %finish.1 = (bf16[64,256]{1,0:T(8,128)(2,1)}, f32[64,256]{1,0:T(8,128)}, f32[64,256]{1,0:T(8,128)}, f32[256,256]{1,0:T(8,128)}, f32[256,256]{1,0:T(8,128)}) custom-call(bf16[64,256]{1,0:T(8,128)(2,1)} %copy-done.9, f32[128,256]{1,0:T(8,128)} %copy-done.6, f32[16,32,256]{2,1,0:T(8,128)} %copy-done.2), custom_call_target="tpu_custom_call" | custom-call | tf_op jit(solution)/shard_map/finish/pallas_call | solution.py:332
  (13 shorter events, 0.0 us)
Async XLA Ops:
  0.6 63.0 %copy-start.10 = (s32[1,64,10]{1,0,2:T(1,128)S(1)}, s32[1,64,10]{1,0,2:T(1,128)}, u32[]{:S(2)}) copy-start(s32[1,64,10]{1,0,2:T(1,128)} %param.17) | copy-start | bytes 7684
  0.6 63.0 %copy-start.11 = (s32[1,64]{1,0:T(1,128)S(1)}, s32[1,64]{1,0:T(1,128)}, u32[]{:S(2)}) copy-start(s32[1,64]{1,0:T(1,128)} %param.18) | copy-start | bytes 772
  1.4 0.9 copy-start.3
  2.4 0.8 copy-start.7
  62.9 0.7 copy-start
  63.8 0.9 copy-start.1
  64.7 0.9 copy-start.4
  65.6 0.9 copy-start.5
  66.5 0.8 copy-start.8
  129.5 0.8 copy-start.2
  130.3 0.6 copy-start.6
  131.0 0.6 copy-start.9

commit v3 on v2

v3 whole, which is shorter than its diff:
```python
import functools

import jax
import jax.numpy as jnp
from jax import lax
from jax.experimental import pallas as pl
from jax.experimental.pallas import tpu as pltpu
from jax.sharding import PartitionSpec as P

MESH = pl.DeviceIdType.MESH
ROWS = 768


def contract_rows(a, b):
    return lax.dot_general(a, b, (((0,), (0,)), ((), ())), preferred_element_type=jnp.float32)


def contract_lanes(a, b):
    return lax.dot_general(a, b, (((1,), (1,)), ((), ())), preferred_element_type=jnp.float32)


def each(count, body):
    def step(k, carry):
        body(k)
        return carry

    lax.fori_loop(1, count, step, 0)


Z_ORDER = (4, 3, 5, 2, 6, 1, 7)


def tail_kernel(
    nd, nf,
    oa_ref, w1_any, w2s_any, w2n_any, grad_any, adj_any, deg_any,
    emb_ref, gw1_ref, gw2_ref,
    w1, w2s, w2n, grad_ref, adj_ref, deg_ref, both, x_in, gh_buf, hid, gpre, grads, turned, w2_in, part1, in1, sum1,
    fetch, sib_send, sib_recv, a_send, a_recv, h_send, h_recv, p_send, p_recv,
    g_send, g_recv, q_send, q_recv, r_send, r_recv, b_send, b_recv, f_send, f_recv,
):
    d = lax.axis_index("dp")
    f = lax.axis_index("feat")
    nz = nf // 2
    z, c = lax.div(f, 2), lax.rem(f, 2)
    block = ROWS // nf
    half = ROWS // 2
    mine = c * nz + z
    sibling = (d, 2 * z + 1 - c)

    def along_z(k):
        to = lax.rem(z + k, nz)
        return to, (d, 2 * to + c)

    def dp_peer(k):
        return lax.rem(d + k, nd)

    def remote(src, dst, send_sem, recv_sem, to):
        return pltpu.make_async_remote_copy(
            src_ref=src, dst_ref=dst, send_sem=send_sem, recv_sem=recv_sem,
            device_id=to, device_id_type=MESH,
        )

    fetches = [
        pltpu.make_async_copy(w1_any, w1, fetch.at[0]),
        pltpu.make_async_copy(w2s_any, w2s, fetch.at[1]),
        pltpu.make_async_copy(w2n_any, w2n, fetch.at[2]),
        pltpu.make_async_copy(adj_any, adj_ref, fetch.at[3]),
        pltpu.make_async_copy(deg_any, deg_ref, fetch.at[4]),
        pltpu.make_async_copy(grad_any, grad_ref, fetch.at[5]),
    ]
    for copy in reversed(fetches):
        copy.start()

    barrier = pltpu.get_barrier_semaphore()

    def greet(to):
        pl.semaphore_signal(barrier, inc=1, device_id=to, device_id_type=MESH)

    greet(sibling)
    for k in range(1, nz):
        greet(along_z(k)[1])
    each(nd, lambda k: greet((dp_peer(k), f)))
    mine_c = pl.ds(pl.multiple_of(c * half, 16), half)
    other_c = pl.ds(pl.multiple_of((1 - c) * half, 16), half)
    both[c] = oa_ref[mine_c, :]
    g_rows = pl.ds(pl.multiple_of(c * 32, 16), 32)
    for copy in fetches[1:]:
        copy.wait()
    grads[d, g_rows, :] = grad_ref[g_rows, :]
    pl.semaphore_wait(barrier, 1 + nz - 1 + nd - 1)

    swap = remote(oa_ref.at[other_c, :], both.at[c], sib_send.at[0], sib_recv.at[0], sibling)
    swap.start()
    swap.wait()

    def rows_of(index):
        return pl.ds(pl.multiple_of(index * block, 16), block)

    def row_copy(k):
        to, device = along_z(k)
        return remote(both.at[:, rows_of(to), :], x_in.at[z], a_send.at[k], a_recv.at[z], device)

    def row_back(k):
        source, device = along_z(k)
        return remote(both.at[:, rows_of(source), :], x_in.at[source], a_send.at[k], a_recv.at[source], device)

    for k in Z_ORDER:
        row_copy(k).start()

    def grad_copy(k):
        to = (dp_peer(k), f)
        return remote(grad_ref.at[g_rows, :], grads.at[d, g_rows, :], g_send.at[k], g_recv.at[k], to)

    each(nd, lambda k: grad_copy(k).start())
    x_in[z] = both[:, rows_of(z), :]

    out_grad = grad_ref[...]
    degree_row = deg_ref[...]
    targets = degree_row.shape[1]
    row = lax.broadcasted_iota(jnp.int32, (ROWS, targets), 0)
    counts = jnp.zeros((ROWS, targets), jnp.float32)
    for j in range(adj_ref.shape[0]):
        listed = jnp.where(degree_row > j, adj_ref[j], -1)
        counts = counts + jnp.where(row == listed, 1.0, 0.0)
    degree_row = degree_row.astype(jnp.float32)
    degree = jnp.broadcast_to(degree_row, (8, targets)).T[:, :1]
    grad_agg = contract_lanes(out_grad, w2n[...]) / degree
    gh_buf[...] = jnp.dot(
        counts, grad_agg, precision=lax.Precision.HIGHEST, preferred_element_type=jnp.float32
    )
    gh_buf[:targets, :] += contract_lanes(out_grad, w2s[...])
    counts = counts.T.astype(jnp.bfloat16)
    fetches[0].wait()

    for k in Z_ORDER:
        row_back(k).wait_recv()
    pre = jnp.zeros((block, w1.shape[-1]), jnp.float32)
    for source in range(nz):
        for core in range(2):
            pre = pre + jnp.dot(x_in[source, core], w1[core, source], preferred_element_type=jnp.float32)
    sig = 1.0 / (1.0 + jnp.exp(-pre))
    grad_pre = gh_buf[rows_of(mine), :] * (sig * (1.0 + pre * (1.0 - sig)))
    hid[mine] = (pre * sig).astype(jnp.bfloat16)
    gpre[mine] = grad_pre.astype(jnp.bfloat16)

    def spread(buf, send_sem, recv_sem, k):
        return remote(buf.at[mine], buf.at[mine], send_sem.at[k], recv_sem.at[z], along_z(k)[1])

    def spread_back(buf, send_sem, recv_sem, k):
        source, device = along_z(k)
        slot = c * nz + source
        return remote(buf.at[slot], buf.at[slot], send_sem.at[k], recv_sem.at[source], device)

    def hand_over(buf, i):
        ours = buf.at[pl.ds(c * nz, nz)]
        return remote(ours, ours, sib_send.at[i], sib_recv.at[i], sibling)

    def handed(buf, i):
        theirs = buf.at[pl.ds((1 - c) * nz, nz)]
        return remote(theirs, theirs, sib_send.at[i], sib_recv.at[i], sibling)

    for k in Z_ORDER:
        spread(hid, h_send, h_recv, k).start()
    for k in Z_ORDER:
        spread(gpre, p_send, p_recv, k).start()

    def grad_in(k):
        here = lax.rem(d - k + nd, nd)
        return remote(
            grads.at[here, g_rows, :], grads.at[here, g_rows, :], g_send.at[k], g_recv.at[k], (here, f)
        )

    each(nd, lambda k: grad_in(k).wait_recv())
    grads_over = remote(
        grads.at[:, g_rows, :], grads.at[:, g_rows, :], sib_send.at[1], sib_recv.at[1], sibling
    )
    grads_over.start()

    for k in Z_ORDER:
        spread_back(hid, h_send, h_recv, k).wait_recv()
    hand_over(hid, 2).start()
    handed(hid, 2).wait_recv()

    hidden = hid[...].reshape(ROWS, hid.shape[-1])
    self_hidden = hidden[:targets, :]
    agg_two = jnp.dot(counts, hidden, preferred_element_type=jnp.float32) / degree
    agg_two = agg_two.astype(jnp.bfloat16)
    pair = jnp.concatenate([self_hidden, agg_two], axis=0)
    turned[...] = pair.astype(jnp.float32).T.astype(jnp.bfloat16)
    columns = pl.ds(pl.multiple_of(f * 16, 16), 16)
    w2_in[d] = turned[columns, :]

    def w2_copy(k):
        return remote(turned.at[columns, :], w2_in.at[d], q_send.at[k], q_recv.at[k], (dp_peer(k), f))

    def w2_back(k):
        here = lax.rem(d - k + nd, nd)
        return remote(w2_in.at[here], w2_in.at[here], q_send.at[k], q_recv.at[k], (here, f))

    each(nd, lambda k: w2_copy(k).start())

    for k in Z_ORDER:
        spread_back(gpre, p_send, p_recv, k).wait_recv()
    hand_over(gpre, 3).start()
    handed(gpre, 3).wait_recv()
    part1[...] = contract_rows(oa_ref[...], gpre[...].reshape(ROWS, gpre.shape[-1]))

    def tile_of(part):
        return (
            pl.ds(pl.multiple_of(lax.div(part, 2) * 8, 8), 8),
            pl.ds(pl.multiple_of(lax.rem(part, 2) * 128, 128), 128),
        )

    my_rows, my_lanes = tile_of(d)

    def w1_copy(k):
        to = dp_peer(k)
        rows, lanes = tile_of(to)
        return remote(part1.at[rows, lanes], in1.at[d], r_send.at[k], r_recv.at[k], (to, f))

    def w1_in(k):
        here = lax.rem(d - k + nd, nd)
        return remote(in1.at[here], in1.at[here], r_send.at[k], r_recv.at[k], (here, f))

    each(nd, lambda k: w1_copy(k).start())
    in1[d] = part1[my_rows, my_lanes]
    emb = jnp.dot(self_hidden, w2s[...], preferred_element_type=jnp.float32)
    emb = emb + jnp.dot(agg_two, w2n[...], preferred_element_type=jnp.float32)
    emb_ref[...] = emb.astype(jnp.bfloat16)

    grads_over.wait_send()
    remote(
        grads.at[:, pl.ds(pl.multiple_of((1 - c) * 32, 16), 32), :],
        grads.at[:, pl.ds(pl.multiple_of((1 - c) * 32, 16), 32), :],
        sib_send.at[1], sib_recv.at[1], sibling,
    ).wait_recv()
    each(nd, lambda k: w2_back(k).wait_recv())
    lane = lax.broadcasted_iota(jnp.int32, (16, 128), 1)
    total2 = jnp.zeros((32, out_grad.shape[-1]), jnp.float32)
    for p in range(nd // 2):
        first, second = w2_in[2 * p].astype(jnp.float32), w2_in[2 * p + 1].astype(jnp.float32)
        selfs = jnp.where(lane < 64, first, pltpu.roll(second, 64, 1))
        neighs = jnp.where(lane < 64, pltpu.roll(first, 64, 1), second)
        left = jnp.concatenate([selfs, neighs], axis=0).astype(jnp.bfloat16)
        right = grads[2 * p:2 * p + 2].reshape(128, out_grad.shape[-1])
        total2 = total2 + jnp.dot(left, right, preferred_element_type=jnp.float32)
    gw2_ref[mine] = total2.astype(jnp.bfloat16)
    for k in Z_ORDER:
        spread(gw2_ref, f_send, f_recv, k).start()

    each(nd, lambda k: w1_in(k).wait_recv())
    sum1[...] = jnp.sum(in1[...], axis=0)
    gw1_ref[my_rows, my_lanes] = sum1[...]

    def w1_out(k):
        return remote(sum1, gw1_ref.at[my_rows, my_lanes], b_send.at[k], b_recv.at[k], (dp_peer(k), f))

    def w1_back(k):
        here = lax.rem(d - k + nd, nd)
        rows, lanes = tile_of(here)
        return remote(sum1, gw1_ref.at[rows, lanes], b_send.at[k], b_recv.at[k], (here, f))

    each(nd, lambda k: w1_out(k).start())
    for k in Z_ORDER:
        spread_back(gw2_ref, f_send, f_recv, k).wait_recv()
    hand_over(gw2_ref, 4).start()

    for k in Z_ORDER:
        row_copy(k).wait_send()
        spread(hid, h_send, h_recv, k).wait_send()
        spread(gpre, p_send, p_recv, k).wait_send()
        spread(gw2_ref, f_send, f_recv, k).wait_send()
    hand_over(hid, 2).wait_send()
    hand_over(gpre, 3).wait_send()

    def sent(k):
        grad_copy(k).wait_send()
        w2_copy(k).wait_send()
        w1_copy(k).wait_send()

    each(nd, sent)
    handed(gw2_ref, 4).wait_recv()
    hand_over(gw2_ref, 4).wait_send()

    def finished(k):
        w1_back(k).wait_recv()
        w1_out(k).wait_send()

    each(nd, finished)


def finish_kernel(
    emb_any, gw1_any, gw2_ref, out_emb, out_1s, out_1n, out_2s, out_2n, sem
):
    copies = [
        pltpu.make_async_copy(emb_any, out_emb, sem.at[0]),
        pltpu.make_async_copy(gw1_any.at[:64, :], out_1s, sem.at[1]),
        pltpu.make_async_copy(gw1_any.at[64:, :], out_1n, sem.at[2]),
    ]
    for copy in copies:
        copy.start()
    nz = gw2_ref.shape[0] // 2
    for i in range(2 * nz):
        f = 2 * (i % nz) + i // nz
        out_2s[16 * f:16 * f + 16, :] = gw2_ref[i, :16, :].astype(jnp.float32)
        out_2n[16 * f:16 * f + 16, :] = gw2_ref[i, 16:, :].astype(jnp.float32)
    for copy in copies:
        copy.wait()


def tail(nd, nf, oa, w1, w2s, w2n, out_grad, adj_two, deg_two):
    vmem = pl.BlockSpec(memory_space=pltpu.VMEM)
    anywhere = pl.BlockSpec(memory_space=pltpu.HBM)
    f32, bf16 = jnp.float32, jnp.bfloat16
    dma = pltpu.SemaphoreType.DMA
    nz = nf // 2
    emb, gw1, gw2 = pl.pallas_call(
        functools.partial(tail_kernel, nd, nf),
        out_shape=(
            jax.ShapeDtypeStruct((64, 256), bf16),
            jax.ShapeDtypeStruct((128, 256), f32),
            jax.ShapeDtypeStruct((nf, 32, 256), bf16),
        ),
        in_specs=[vmem] + [anywhere] * 6,
        out_specs=(vmem,) * 3,
        scratch_shapes=[
            pltpu.VMEM((2, nz, 128, 256), bf16),
            pltpu.VMEM((256, 256), bf16),
            pltpu.VMEM((256, 256), bf16),
            pltpu.VMEM(out_grad.shape, bf16),
            pltpu.VMEM(adj_two.shape, jnp.int32),
            pltpu.VMEM(deg_two.shape, jnp.int32),
            pltpu.VMEM((2, ROWS // 2, 128), bf16),
            pltpu.VMEM((nz, 2, ROWS // nf, 128), bf16),
            pltpu.VMEM((ROWS, 256), f32),
            pltpu.VMEM((nf, ROWS // nf, 256), bf16),
            pltpu.VMEM((nf, ROWS // nf, 256), bf16),
            pltpu.VMEM((nd, 64, 256), bf16),
            pltpu.VMEM((256, 128), bf16),
            pltpu.VMEM((nd, 16, 128), bf16),
            pltpu.VMEM((128, 256), f32),
            pltpu.VMEM((nd, 8, 128), f32),
            pltpu.VMEM((8, 128), f32),
            dma((6,)), dma((5,)), dma((5,)),
            dma((nz,)), dma((nz,)), dma((nz,)), dma((nz,)), dma((nz,)), dma((nz,)),
            dma((nd,)), dma((nd,)), dma((nd,)), dma((nd,)), dma((nd,)), dma((nd,)),
            dma((nd,)), dma((nd,)), dma((nz,)), dma((nz,)),
        ],
        compiler_params=pltpu.CompilerParams(
            collective_id=1, has_side_effects=True, vmem_limit_bytes=60 * 1024 * 1024
        ),
        name="tail",
    )(oa, w1, w2s, w2n, out_grad, adj_two, deg_two)
    return pl.pallas_call(
        finish_kernel,
        out_shape=(
            jax.ShapeDtypeStruct((64, 256), bf16),
            jax.ShapeDtypeStruct((64, 256), f32),
            jax.ShapeDtypeStruct((64, 256), f32),
            jax.ShapeDtypeStruct((256, 256), f32),
            jax.ShapeDtypeStruct((256, 256), f32),
        ),
        in_specs=[anywhere, anywhere, vmem],
        out_specs=(anywhere, anywhere, anywhere, vmem, vmem),
        scratch_shapes=[dma((3,))],
        compiler_params=pltpu.CompilerParams(vmem_limit_bytes=60 * 1024 * 1024),
        name="finish",
    )(emb, gw1, gw2)


def front_kernel(
    nd, nf, feat_any, req_any, w1s_any, w1n_any, adj_any, deg_any, self_any,
    samp_ref, w1_out, slots_ref, scale_ref,
    blocks, req_ref, w1_ref, adj_ref, deg_ref, self_ref, req_by_x, req_in, stage,
    up_send, up_recv, down_send, down_recv, req_send, req_recv,
    x_send, x_recv, w1_send, w1_recv, local_sem, fetch, sib_send, sib_recv,
):
    d = lax.axis_index("dp")
    f = lax.axis_index("feat")
    nx, ny = 4, nd // 4
    x, y = lax.rem(d, nx), lax.div(d, nx)

    def at_x(j):
        return lax.rem(x + j, nx)

    def at_y(s):
        return lax.rem(y + s + ny, ny)

    nz = nf // 2
    z, c = lax.div(f, 2), lax.rem(f, 2)
    sibling = (d, 2 * z + 1 - c)

    def along_z(k):
        to = lax.rem(z + k, nz)
        return to, (d, 2 * to + c)

    fetches = [
        pltpu.make_async_copy(feat_any.at[:, 512 * q:512 * q + 512], blocks.at[y, 64 * q:64 * q + 64, :], fetch.at[q])
        for q in range(4)
    ] + [
        pltpu.make_async_copy(req_any, req_ref, fetch.at[4]),
        pltpu.make_async_copy(w1s_any, w1_ref.at[:64, :], fetch.at[5]),
        pltpu.make_async_copy(w1n_any, w1_ref.at[64:, :], fetch.at[6]),
        pltpu.make_async_copy(adj_any, adj_ref, fetch.at[7]),
        pltpu.make_async_copy(deg_any, deg_ref, fetch.at[8]),
        pltpu.make_async_copy(self_any, self_ref, fetch.at[9]),
    ]
    for copy in fetches:
        copy.start()

    barrier = pltpu.get_barrier_semaphore()

    def greet(to):
        pl.semaphore_signal(barrier, inc=1, device_id=to, device_id_type=MESH)

    for j in range(1, nx):
        greet((y * nx + at_x(j), f))
    greet((at_y(1) * nx + x, f))
    greet((at_y(-1) * nx + x, f))
    greet(sibling)
    for k in range(1, nz):
        greet(along_z(k)[1])

    fetches[4].wait()
    for owner in range(nd):
        req_by_x[owner % nx, owner // nx:owner // nx + 1, :] = req_ref[owner:owner + 1, :]

    for copy in fetches[:4] + fetches[5:]:
        copy.wait()
    pl.semaphore_wait(barrier, nx - 1 + 2 + 1 + nz - 1)

    def req_copy(j):
        to = at_x(j)
        return pltpu.make_async_remote_copy(
            src_ref=req_by_x.at[to], dst_ref=req_in.at[x],
            send_sem=req_send.at[j], recv_sem=req_recv.at[x],
            device_id=(y * nx + to, f), device_id_type=MESH,
        )

    def half(source, h):
        return blocks.at[source, pl.ds(128 * h, 128), :]

    def up_copy(t, source):
        return pltpu.make_async_remote_copy(
            src_ref=half(source, t % 2), dst_ref=half(source, t % 2),
            send_sem=up_send.at[t], recv_sem=up_recv.at[t],
            device_id=(at_y(1) * nx + x, f), device_id_type=MESH,
        )

    def down_copy(t, source):
        return pltpu.make_async_remote_copy(
            src_ref=half(source, 1 - t % 2), dst_ref=half(source, 1 - t % 2),
            send_sem=down_send.at[t], recv_sem=down_recv.at[t],
            device_id=(at_y(-1) * nx + x, f), device_id_type=MESH,
        )

    def w1_copy(k):
        return pltpu.make_async_remote_copy(
            src_ref=w1_ref, dst_ref=w1_out.at[c, z],
            send_sem=w1_send.at[k], recv_sem=w1_recv.at[z],
            device_id=along_z(k)[1], device_id_type=MESH,
        )

    for j in range(1, nx):
        req_copy(j).start()
    for t in range(2):
        up_copy(t, y).start()
        down_copy(t, y).start()
    for k in Z_ORDER:
        w1_copy(k).start()
    own_w1 = pltpu.make_async_copy(w1_ref, w1_out.at[c, z], local_sem.at[ny])
    own_w1.start()
    req_in[x] = req_by_x[x]
    for j in range(1, nx):
        source = at_x(j)
        pltpu.make_async_remote_copy(
            src_ref=req_by_x.at[source], dst_ref=req_in.at[source],
            send_sem=req_send.at[j], recv_sem=req_recv.at[source],
            device_id=(y * nx + source, f), device_id_type=MESH,
        ).wait_recv()

    def x_copy(source, j):
        slot = source * nx + x
        return pltpu.make_async_remote_copy(
            src_ref=stage.at[source, j], dst_ref=samp_ref.at[slot],
            send_sem=x_send.at[source * nx + j], recv_sem=x_recv.at[slot],
            device_id=(y * nx + at_x(j), f), device_id_type=MESH,
        )

    def own_copy(source):
        return pltpu.make_async_copy(
            stage.at[source, 0], samp_ref.at[source * nx + x], local_sem.at[source]
        )

    node = lax.broadcasted_iota(jnp.int32, (512, 512), 0)

    def pick(source, j):
        asked = req_in[at_x(j), pl.ds(source, 1), :]
        low, quarter = asked & 511, asked >> 9
        one_hot = jnp.where(node == low, 1.0, 0.0).astype(jnp.bfloat16)
        rows = jnp.dot(blocks[source], one_hot, preferred_element_type=jnp.float32)
        chosen = rows[192:256, :]
        for q in range(3):
            chosen = jnp.where(quarter == q, rows[64 * q:64 * q + 64, :], chosen)
        stage[source, j] = chosen.astype(jnp.bfloat16)

    def process(count, source_of):
        def step(k, carry):
            source = source_of(lax.div(k, nx))
            j = lax.rem(k + 1, nx)
            pick(source, j)

            @pl.when(j > 0)
            def _():
                x_copy(source, j).start()

            @pl.when(j == 0)
            def _():
                own_copy(source).start()

            return carry

        lax.fori_loop(0, count * nx, step, 0)

    def w1_over(core):
        return pltpu.make_async_remote_copy(
            src_ref=w1_out.at[core], dst_ref=w1_out.at[core],
            send_sem=sib_send.at[0], recv_sem=sib_recv.at[0],
            device_id=sibling, device_id_type=MESH,
        )

    process(1, lambda i: y)
    fanout = adj_ref.shape[0]
    for j in range(fanout):
        slots_ref[j:j + 1, :] = jnp.where(deg_ref[...] > j, adj_ref[j], nd * 512)
    slots_ref[fanout:, :] = self_ref[...]
    scale_ref[...] = 1.0 / deg_ref[...].astype(jnp.float32)
    for s in range(ny // 2):
        below, above = at_y(-1 - s), at_y(1 + s)
        for h in range(2 if s < ny // 2 - 1 else 1):
            t = 2 * s + h
            up_copy(t, below).wait_recv()
            if t + 2 < ny - 1:
                up_copy(t + 2, below).start()
            down_copy(t, above).wait_recv()
            if t + 2 < ny - 1:
                down_copy(t + 2, above).start()
        if s == ny // 2 - 1:
            own_w1.wait()
            for k in Z_ORDER:
                source, device = along_z(k)
                pltpu.make_async_remote_copy(
                    src_ref=w1_ref, dst_ref=w1_out.at[c, source],
                    send_sem=w1_send.at[k], recv_sem=w1_recv.at[source],
                    device_id=device, device_id_type=MESH,
                ).wait_recv()
            w1_given = w1_over(c)
            w1_taken = w1_over(1 - c)
            w1_given.start()
        if s < ny // 2 - 1:
            process(2, lambda i: lax.rem(y + (2 * i - 1) * (1 + s) + ny, ny))
        else:
            process(1, lambda i: below)

    def x_back(source):
        for j in range(1, nx):
            slot = source * nx + at_x(j)
            pltpu.make_async_remote_copy(
                src_ref=stage.at[source, j], dst_ref=samp_ref.at[slot],
                send_sem=x_send.at[source * nx + j], recv_sem=x_recv.at[slot],
                device_id=(y * nx + at_x(j), f), device_id_type=MESH,
            ).wait_recv()
            x_copy(source, j).wait_send()
        own_copy(source).wait()

    lax.fori_loop(0, ny, lambda k, c: (x_back(k), c)[1], 0)

    for k in Z_ORDER:
        w1_copy(k).wait_send()
    w1_given.wait_send()
    w1_taken.wait_recv()
    for j in range(1, nx):
        req_copy(j).wait_send()
    for t in range(ny - 1):
        up_copy(t, at_y(-(t // 2))).wait_send()
        down_copy(t, at_y(t // 2)).wait_send()


def front(nd, nf, features, request_rows, w1_self, w1_neigh, adj_one, deg_one, self_slots):
    vmem = pl.BlockSpec(memory_space=pltpu.VMEM)
    anywhere = pl.BlockSpec(memory_space=pltpu.HBM)
    bf16, i32 = jnp.bfloat16, jnp.int32
    dma = pltpu.SemaphoreType.DMA
    ny = nd // 4
    return pl.pallas_call(
        functools.partial(front_kernel, nd, nf),
        out_shape=(
            jax.ShapeDtypeStruct((nd, 64, 512), bf16),
            jax.ShapeDtypeStruct((2, nf // 2, 128, 256), bf16),
            jax.ShapeDtypeStruct((adj_one.shape[0] + 1, adj_one.shape[2]), i32),
            jax.ShapeDtypeStruct(deg_one.shape, jnp.float32),
        ),
        in_specs=[anywhere] * 7,
        out_specs=(anywhere, anywhere, vmem, vmem),
        scratch_shapes=[
            pltpu.VMEM((ny, 256, 512), bf16),
            pltpu.VMEM((nd, 512), i32),
            pltpu.VMEM((128, 256), bf16),
            pltpu.VMEM(adj_one.shape, i32),
            pltpu.VMEM(deg_one.shape, i32),
            pltpu.VMEM(self_slots.shape, i32),
            pltpu.VMEM((4, ny, 512), i32),
            pltpu.VMEM((4, ny, 512), i32),
            pltpu.VMEM((ny, 4, 64, 512), bf16),
            dma((ny - 1,)), dma((ny - 1,)), dma((ny - 1,)), dma((ny - 1,)),
            dma((4,)), dma((4,)), dma((nd,)), dma((nd,)),
            dma((nf // 2,)), dma((nf // 2,)), dma((ny + 1,)), dma((10,)), dma((1,)), dma((1,)),
        ],
        compiler_params=pltpu.CompilerParams(
            collective_id=2, has_side_effects=True, vmem_limit_bytes=60 * 1024 * 1024
        ),
        name="front",
    )(features.T, request_rows, w1_self, w1_neigh, adj_one, deg_one, self_slots)


def mean_kernel(slots_ref, scale_ref, samp_any, out_ref, samp, table, own, total, sem):
    pairs, width, cap = samp.shape
    pieces = sem.shape[0]
    step = pairs // pieces
    fetches = [
        pltpu.make_async_copy(samp_any.at[pl.ds(i * step, step)], samp.at[pl.ds(i * step, step)], sem.at[i])
        for i in range(pieces)
    ]
    for copy in fetches:
        copy.start()
    table[2 * cap * pairs:, :] = jnp.zeros((8, width), jnp.float32)

    def unpack(p, carry):
        turned = samp[p].astype(jnp.float32).T
        table[pl.ds(pl.multiple_of(2 * cap * p, 8), cap), :] = turned
        table[pl.ds(pl.multiple_of(2 * cap * p + cap, 8), cap), :] = pltpu.roll(turned, 64, 1)
        return carry

    for i in range(pieces):
        fetches[i].wait()
        lax.fori_loop(i * step, (i + 1) * step, unpack, 0)
    lists, rows = slots_ref.shape

    def gather(block, carry):
        for r in range(8):
            i = block * 8 + r
            own[pl.ds(i, 1), :] = table[pl.ds(slots_ref[lists - 1, i], 1), :]
            terms = [table[pl.ds(slots_ref[j, i], 1), :] for j in range(lists - 1)]
            while len(terms) > 1:
                terms = [sum(terms[k:k + 2][1:], terms[k]) for k in range(0, len(terms), 2)]
            total[pl.ds(i, 1), :] = terms[0] * scale_ref[0, i]
        return carry

    lax.fori_loop(0, rows // 8, gather, 0)
    lane = lax.broadcasted_iota(jnp.int32, (rows, width), 1)
    mean = pltpu.roll(total[...], 64, 1)
    out_ref[:rows, :] = jnp.where(lane < 64, own[...], mean).astype(jnp.bfloat16)
    out_ref[rows:, :] = jnp.zeros((ROWS - rows, width), jnp.bfloat16)


def neighbour_mean(sampled, slots, scale):
    nd, columns, cap = sampled.shape
    rows = slots.shape[1]
    smem = pl.BlockSpec(memory_space=pltpu.SMEM)
    return pl.pallas_call(
        mean_kernel,
        out_shape=jax.ShapeDtypeStruct((ROWS, 2 * columns), jnp.bfloat16),
        in_specs=[smem, smem, pl.BlockSpec(memory_space=pltpu.HBM)],
        out_specs=pl.BlockSpec(memory_space=pltpu.VMEM),
        scratch_shapes=[
            pltpu.VMEM((nd // 2, 2 * columns, cap), jnp.bfloat16),
            pltpu.VMEM((nd * cap + 8, 2 * columns), jnp.float32),
            pltpu.VMEM((rows, 2 * columns), jnp.float32),
            pltpu.VMEM((rows, 2 * columns), jnp.float32),
            pltpu.SemaphoreType.DMA((4,)),
        ],
        compiler_params=pltpu.CompilerParams(vmem_limit_bytes=60 * 1024 * 1024),
        name="mean",
    )(slots, scale, sampled.reshape(nd // 2, 2 * columns, cap))


def local(
    nd, nf,
    features, request_rows, self_slots, adj_one, deg_one, adj_two, deg_two,
    w1_self, w1_neigh, w2_self, w2_neigh, out_grad,
):
    sampled, w1, slots, scale = front(
        nd, nf, features, request_rows[0], w1_self, w1_neigh, adj_one.transpose(2, 0, 1), deg_one, self_slots
    )
    oa = neighbour_mean(sampled, slots, scale)
    return tail(nd, nf, oa, w1, w2_self, w2_neigh, out_grad, adj_two.transpose(2, 0, 1), deg_two)


def solution(mesh):
    return jax.shard_map(
        functools.partial(local, mesh.shape["dp"], mesh.shape["feat"]),
        mesh=mesh,
        in_specs=(
            P("dp", "feat"),
            P("dp", None, None),
            P("dp", None),
            P("dp", None, None),
            P("dp", None),
            P("dp", None, None),
            P("dp", None),
            P("feat", None),
            P("feat", None),
            P(),
            P(),
            P("dp", None),
        ),
        out_specs=(P("dp", None), P("feat", None), P("feat", None), P(), P()),
        check_vma=False,
    )
```

time: 134 us -> 114 us (0.85)
  local copies, waits for them, and re-layouts: 9.23 us -> 0 us
  Pallas kernels: 119 us -> 113 us
  other arithmetic: 4.27 us -> 0 us
    pallas_call x1, Pallas kernels: 62.2 us -> 47.4 us  [tail(): pl.pallas_call(functools.partial(tail_kernel, nd, nf), out_shape=(jax.Sha...]
    unnamed x25 -> x0, local copies, waits for them, and re-layouts: 8.08 us -> none
    pallas_call x1, Pallas kernels: 1.98 us -> 7.83 us  [tail(): pl.pallas_call(finish_kernel, out_shape=(jax.ShapeDtypeStruct((64, 256),...]
    pallas_call x1, Pallas kernels: 10.8 us -> 15.5 us  [neighbour_mean(): pl.pallas_call(mean_kernel, out_shape=jax.ShapeDtypeStruct((ROWS, 2 * col...]
    concatenate x2 -> x0, other arithmetic: 2.1 us -> none  [the longest x1 1.31 us: neighbour_mean(): slots = jnp.concatenate([self_slots[None, :], listed], axis=0).reshape(-1)]
    pallas_call x1, Pallas kernels: 44.3 us -> 42.6 us  [front(): pl.pallas_call(functools.partial(front_kernel, nd, nf), out_shape=(jax.Sh...]
where the time goes in v3:
time: 114 us
  Pallas kernels  113 us (99%)
    pallas_call x1, Pallas kernels, tail(): pl.pallas_call(functools.partial(tail_kernel, nd, nf), out_shape=(jax.Sha...  47.4 us
    pallas_call x1, Pallas kernels, front(): pl.pallas_call(functools.partial(front_kernel, nd, nf), out_shape=(jax.Sh...  42.6 us
    pallas_call x1, Pallas kernels, neighbour_mean(): pl.pallas_call(mean_kernel, out_shape=jax.ShapeDtypeStruct((ROWS, 2 * col...  15.5 us
    pallas_call x1, Pallas kernels, tail(): pl.pallas_call(finish_kernel, out_shape=(jax.ShapeDtypeStruct((64, 256),...  7.83 us

profile of v3, /device:TPU:1, one launch (start us, length us, event | category | flops | bytes accessed | tf_op | source)
XLA Modules:
  0.0 113.9 jit_solution(4687246274451180442)
XLA Ops:
  0.6 42.6 %front.1 = (bf16[32,64,512]{2,1,0:T(8,128)(2,1)}, bf16[2,8,128,256]{3,2,1,0:T(8,128)(2,1)}, s32[11,704]{1,0:T(8,128)}, f32[1,704]{1,0:T(1,128)}) custom-call(bf16[64,2048]{1,0:T(8,128)(2,1)} %bitcast.6, s32[32,512]{1,0:T(8,128)} %bitcast.7, bf16[64,256]{1,0:T(8,128)(2,1)} %w1s_any.1, bf16[64,256]{1,0:T(8,128)(2,1)} %w1n_any.1, s32[10,1,704]{2,1,0:T(1,128)} %bitcast.8, ...), custom_call_target="tpu_custom_call" | custom-call | tf_op jit(solution)/shard_map/front/pallas_call | solution.py:595
  43.2 15.5 %mean.1.oa_ref = bf16[768,128]{1,0:T(8,128)(2,1)} custom-call(s32[11,704]{1,0:T(8,128)} %get-tuple-element.12.slots_ref, f32[1,704]{1,0:T(1,128)} %get-tuple-element.13.scale_ref, bf16[16,128,512]{2,1,0:T(8,128)(2,1)} %bitcast.5), custom_call_target="tpu_custom_call" | custom-call | tf_op jit(solution)/shard_map/mean/pallas_call | solution.py:670
  58.7 47.4 %tail.1 = (bf16[64,256]{1,0:T(8,128)(2,1)}, f32[128,256]{1,0:T(8,128)}, bf16[16,32,256]{2,1,0:T(8,128)(2,1)}) custom-call(bf16[768,128]{1,0:T(8,128)(2,1)} %mean.1.oa_ref, bf16[2,8,128,256]{3,2,1,0:T(8,128)(2,1)} %get-tuple-element.15.w1_any, bf16[256,256]{1,0:T(8,128)(2,1)} %w2s_any.1, bf16[256,256]{1,0:T(8,128)(2,1)} %w2n_any.1, bf16[64,256]{1,0:T(8,128)(2,1)} %grad_any.1, ...), custom_call_target="tpu_custom_call" | custom-call | tf_op jit(solution)/shard_map/tail/pallas_call | solution.py:317
  106.0 7.8 %finish.1 = (bf16[64,256]{1,0:T(8,128)(2,1)}, f32[64,256]{1,0:T(8,128)}, f32[64,256]{1,0:T(8,128)}, f32[256,256]{1,0:T(8,128)}, f32[256,256]{1,0:T(8,128)}) custom-call(bf16[64,256]{1,0:T(8,128)(2,1)} %get-tuple-element.16.emb_any, f32[128,256]{1,0:T(8,128)} %get-tuple-element.17.gw1_any, bf16[16,32,256]{2,1,0:T(8,128)(2,1)} %get-tuple-element.18.gw2_ref), custom_call_target="tpu_custom_call" | custom-call | tf_op jit(solution)/shard_map/finish/pallas_call | solution.py:354

commit v4 on v0

v4 whole, which is shorter than its diff:
```python
import functools

import jax
import jax.numpy as jnp
from jax import lax
from jax.experimental import pallas as pl
from jax.experimental.pallas import tpu as pltpu
from jax.sharding import PartitionSpec as P

MESH = pl.DeviceIdType.MESH
ROWS = 768


def contract_rows(a, b):
    return lax.dot_general(a, b, (((0,), (0,)), ((), ())), preferred_element_type=jnp.float32)


def contract_lanes(a, b):
    return lax.dot_general(a, b, (((1,), (1,)), ((), ())), preferred_element_type=jnp.float32)


def each(count, body):
    def step(k, carry):
        body(k)
        return carry

    lax.fori_loop(1, count, step, 0)


Z_ORDER = (4, 3, 5, 2, 6, 1, 7)


def step_kernel(
    nd, nf,
    feat_any, req_any, w1s_any, w1n_any, adj_any, deg_any, self_any,
    adj_two_any, deg_two_any, w2s_any, w2n_any, grad_any,
    emb_ref, gw1_ref, gw2_ref,
    blocks, req_ref, req_by_x, req_in, stage, samp, table, w1,
    adj_ref, deg_ref, self_ref, padded, lists, slots, scale, own, total,
    adj_two, deg_two, w2s, w2n, grad_ref,
    x_out, x_in, gh_buf, hid, gpre, grads, turned, rows_t, w2_in, part, part_in, part1, in1, sum1,
    fetch, up_send, up_recv, down_send, down_recv, req_send, req_recv, x_send, x_recv,
    pair_send, pair_recv, w1_send, w1_recv, sib_send, sib_recv, a_send, a_recv, h_send, h_recv,
    p_send, p_recv, g_send, g_recv, q_send, q_recv, r_send, r_recv, b_send, b_recv,
    f_send, f_recv, smem_sem,
):
    d = lax.axis_index("dp")
    f = lax.axis_index("feat")
    nx, ny, nz = 4, nd // 4, nf // 2
    cap = 512
    x, y = lax.rem(d, nx), lax.div(d, nx)
    z, c = lax.div(f, 2), lax.rem(f, 2)
    block, half_rows = ROWS // nf, ROWS // 2
    mine = c * nz + z
    sibling = (d, 2 * z + 1 - c)

    def at_x(j):
        return lax.rem(x + j, nx)

    def at_y(s):
        return lax.rem(y + s + ny, ny)

    def along_z(k):
        to = lax.rem(z + k, nz)
        return to, (d, 2 * to + c)

    def dp_peer(k):
        return lax.rem(d + k, nd)

    def dp_from(k):
        return lax.rem(d - k + nd, nd)

    def remote(src, dst, send_sem, recv_sem, to):
        return pltpu.make_async_remote_copy(
            src_ref=src, dst_ref=dst, send_sem=send_sem, recv_sem=recv_sem,
            device_id=to, device_id_type=MESH,
        )

    def core_rows(core, size):
        return pl.ds(pl.multiple_of(core * size, 16), size)

    sources = [
        (feat_any.at[:, 512 * q:512 * q + 512], blocks.at[y, 64 * q:64 * q + 64, :]) for q in range(4)
    ] + [
        (req_any, req_ref),
        (w1s_any, w1.at[0, z, core_rows(c, 64), :]),
        (w1n_any, w1.at[1, z, core_rows(c, 64), :]),
        (adj_any, adj_ref), (deg_any, deg_ref), (self_any, self_ref),
        (adj_two_any, adj_two), (deg_two_any, deg_two),
        (w2s_any, w2s), (w2n_any, w2n), (grad_any, grad_ref),
    ]
    fetches = [pltpu.make_async_copy(src, dst, fetch.at[i]) for i, (src, dst) in enumerate(sources)]
    for copy in fetches:
        copy.start()

    barrier = pltpu.get_barrier_semaphore()

    def greet(to):
        pl.semaphore_signal(barrier, inc=1, device_id=to, device_id_type=MESH)

    greet(sibling)
    for k in range(1, nz):
        greet(along_z(k)[1])
    each(nd, lambda k: greet((dp_peer(k), f)))
    fetches[4].wait()
    for owner in range(nd):
        req_by_x[owner % nx, owner // nx:owner // nx + 1, :] = req_ref[owner:owner + 1, :]
    for copy in fetches[:4] + fetches[5:7]:
        copy.wait()
    pl.semaphore_wait(barrier, 1 + nz - 1 + nd - 1)

    def req_copy(j):
        to = at_x(j)
        return remote(req_by_x.at[to], req_in.at[x], req_send.at[j], req_recv.at[x], (y * nx + to, f))

    def req_back(j):
        here = at_x(j)
        return remote(req_by_x.at[here], req_in.at[here], req_send.at[j], req_recv.at[here], (y * nx + here, f))

    def half(source, h):
        return blocks.at[source, pl.ds(128 * h, 128), :]

    def up_copy(t, source):
        part = half(source, t % 2)
        return remote(part, part, up_send.at[t], up_recv.at[t], (at_y(1) * nx + x, f))

    def down_copy(t, source):
        part = half(source, 1 - t % 2)
        return remote(part, part, down_send.at[t], down_recv.at[t], (at_y(-1) * nx + x, f))

    def w1_part(source):
        return w1.at[:, source, core_rows(c, 64), :]

    def w1_copy(k):
        return remote(w1_part(z), w1_part(z), w1_send.at[k], w1_recv.at[z], along_z(k)[1])

    def w1_back(k):
        source, device = along_z(k)
        return remote(w1_part(source), w1_part(source), w1_send.at[k], w1_recv.at[source], device)

    def w1_over(core):
        ours = w1.at[:, :, core_rows(core, 64), :]
        return remote(ours, ours, sib_send.at[0], sib_recv.at[0], sibling)

    for j in range(1, nx):
        req_copy(j).start()
    for t in range(2):
        up_copy(t, y).start()
        down_copy(t, y).start()
    for k in Z_ORDER:
        w1_copy(k).start()
    req_in[x] = req_by_x[x]
    for j in range(1, nx):
        req_back(j).wait_recv()

    def x_copy(source, j):
        slot = source * nx + x
        return remote(
            stage.at[source, j], samp.at[slot, core_rows(c, 64), :],
            x_send.at[source * nx + j], x_recv.at[slot], (y * nx + at_x(j), f),
        )

    def x_back(source, j):
        slot = source * nx + at_x(j)
        return remote(
            stage.at[source, j], samp.at[slot, core_rows(c, 64), :],
            x_send.at[source * nx + j], x_recv.at[slot], (y * nx + at_x(j), f),
        )

    def pair_copy(slot, core):
        ours = samp.at[slot, core_rows(core, 64), :]
        return remote(ours, ours, pair_send.at[slot], pair_recv.at[slot], sibling)

    node = lax.broadcasted_iota(jnp.int32, (512, cap), 0)

    def pick(source, j):
        asked = req_in[at_x(j), pl.ds(source, 1), :]
        low, quarter = asked & 511, asked >> 9
        one_hot = jnp.where(node == low, 1.0, 0.0).astype(jnp.bfloat16)
        rows = jnp.dot(blocks[source], one_hot, preferred_element_type=jnp.float32)
        chosen = rows[192:256, :]
        for q in range(3):
            chosen = jnp.where(quarter == q, rows[64 * q:64 * q + 64, :], chosen)
        return chosen.astype(jnp.bfloat16)

    def process(count, source_of):
        def step(k, carry):
            source = source_of(lax.div(k, nx))
            j = lax.rem(k + 1, nx)
            stage[source, j] = pick(source, j)

            @pl.when(j > 0)
            def _():
                x_copy(source, j).start()

            return carry

        lax.fori_loop(0, count * nx, step, 0)

    def collect(count, source_of):
        def step(k, carry):
            source = source_of(lax.div(k, nx))
            j = lax.rem(k, nx)

            @pl.when(j > 0)
            def _():
                x_back(source, j).wait_recv()

            @pl.when(j == 0)
            def _():
                samp[source * nx + x, core_rows(c, 64), :] = stage[source, 0]

            pair_copy(source * nx + at_x(j), c).start()
            return carry

        lax.fori_loop(0, count * nx, step, 0)

    def absorb(count, source_of):
        def step(k, carry):
            source = source_of(lax.div(k, nx))
            slot = source * nx + at_x(lax.rem(k, nx))
            pair_copy(slot, 1 - c).wait_recv()
            here = pl.ds(pl.multiple_of(slot * cap, 8), cap)
            table[here, :] = samp[slot].astype(jnp.float32).T
            return carry

        lax.fori_loop(0, count * nx, step, 0)

    process(1, lambda i: y)

    for copy in fetches[7:]:
        copy.wait()
    fanout = adj_ref.shape[0]
    present = self_ref.shape[1]
    table[nd * cap:, :] = jnp.zeros((8, 128), jnp.float32)
    padded[...] = jnp.full(padded.shape, nd * cap, jnp.int32)
    for j in range(fanout):
        padded[j:j + 1, :present] = jnp.where(deg_ref[...] > j, adj_ref[j], nd * cap)
    padded[fanout:fanout + 1, :present] = self_ref[...]
    my_lanes_half = pl.ds(pl.multiple_of(c * half_rows, 128), half_rows)
    for j in range(fanout + 1):
        line = padded[j:j + 1, my_lanes_half]
        for to in range(nz):
            at = to * (fanout + 1) + j
            lists[at:at + 1, :block] = line[:, block * to:block * to + block]
    to_smem = pltpu.make_async_copy(lists, slots, smem_sem.at[0])
    to_smem.start()
    padded[:1, :] = jnp.ones((1, ROWS), jnp.int32)
    padded[:1, :present] = deg_ref[...]
    inverse = 1.0 / padded[:1, my_lanes_half].astype(jnp.float32)
    scale[...] = jnp.broadcast_to(jnp.broadcast_to(inverse, (8, half_rows)).T[:, :1], scale.shape)

    out_grad = grad_ref[...]
    degree_row = deg_two[...]
    targets = degree_row.shape[1]
    row = lax.broadcasted_iota(jnp.int32, (ROWS, targets), 0)
    counts = jnp.zeros((ROWS, targets), jnp.float32)
    for j in range(fanout):
        listed = jnp.where(degree_row > j, adj_two[j], -1)
        counts = counts + jnp.where(row == listed, 1.0, 0.0)
    degree_row = degree_row.astype(jnp.float32)
    degree = jnp.broadcast_to(degree_row, (8, targets)).T[:, :1]
    grad_agg = contract_lanes(out_grad, w2n[...]) / degree
    gh_buf[...] = jnp.dot(
        counts, grad_agg, precision=lax.Precision.HIGHEST, preferred_element_type=jnp.float32
    )
    gh_buf[:targets, :] += contract_lanes(out_grad, w2s[...])
    counts = counts.T.astype(jnp.bfloat16)

    def around(s):
        return lambda i: lax.rem(y + (2 * i - 1) * (1 + s) + ny, ny)

    steps = ny // 2
    for s in range(steps):
        below, above = at_y(-1 - s), at_y(1 + s)
        for h in range(2 if s < steps - 1 else 1):
            t = 2 * s + h
            up_copy(t, below).wait_recv()
            if t + 2 < ny - 1:
                up_copy(t + 2, below).start()
            down_copy(t, above).wait_recv()
            if t + 2 < ny - 1:
                down_copy(t + 2, above).start()
        process(2 if s < steps - 1 else 1, around(s))
        if s == 0:
            collect(1, lambda i: y)
        else:
            collect(2, around(s - 1))
        if s == 1:
            absorb(1, lambda i: y)
        if s > 1:
            absorb(2, around(s - 2))

    g_rows = core_rows(c, 32)

    def grad_copy(k):
        return remote(grad_ref.at[g_rows, :], grads.at[d, g_rows, :], g_send.at[k], g_recv.at[k], (dp_peer(k), f))

    def grad_in(k):
        here = grads.at[dp_from(k), g_rows, :]
        return remote(here, here, g_send.at[k], g_recv.at[k], (dp_from(k), f))

    for k in Z_ORDER:
        w1_back(k).wait_recv()
    w1_over(c).start()
    absorb(2, around(steps - 2))
    collect(1, around(steps - 1))
    each(nd, lambda k: grad_copy(k).start())
    grads[d, g_rows, :] = grad_ref[g_rows, :]
    absorb(1, around(steps - 1))
    to_smem.wait()

    def row_copy(k):
        to, device = along_z(k)
        return remote(x_out.at[to], x_in.at[z], a_send.at[k], a_recv.at[z], device)

    def row_back(k):
        source, device = along_z(k)
        return remote(x_out.at[source], x_in.at[source], a_send.at[k], a_recv.at[source], device)

    def sum_rows(t, carry):
        k = lax.rem(t + nz // 2, nz)
        to = lax.rem(z + k, nz)
        base = to * (fanout + 1)

        def eight(m, inner):
            for r in range(8):
                i = m * 8 + r
                own[pl.ds(i, 1), :] = table[pl.ds(slots[base + fanout, i], 1), :]
                terms = [table[pl.ds(slots[base + j, i], 1), :] for j in range(fanout)]
                while len(terms) > 1:
                    terms = [sum(terms[n:n + 2][1:], terms[n]) for n in range(0, len(terms), 2)]
                total[pl.ds(i, 1), :] = terms[0]
            return inner

        lax.fori_loop(0, block // 8, eight, 0)
        x_out[to, 0] = own[...].astype(jnp.bfloat16)
        mean = total[...] * scale[pl.ds(pl.multiple_of(to * block, 8), block), :]
        x_out[to, 1] = mean.astype(jnp.bfloat16)

        @pl.when(k > 0)
        def _():
            row_copy(k).start()

        return carry

    lax.fori_loop(0, nz, sum_rows, 0)
    x_in[z] = x_out[z]
    for kind in range(2):
        rows_t[128 * kind:128 * kind + 128, :] = (
            x_out[:, kind].reshape(half_rows, 128).astype(jnp.float32).T.astype(jnp.bfloat16)
        )
    w1_over(1 - c).wait_recv()

    pre = jnp.zeros((block, w1.shape[-1]), jnp.float32)
    for k in (0,) + tuple(reversed(Z_ORDER)):
        if k > 0:
            row_back(k).wait_recv()
        source = lax.rem(z + k, nz)
        for kind in range(2):
            pre = pre + jnp.dot(x_in[source, kind], w1[kind, source], preferred_element_type=jnp.float32)
    sig = 1.0 / (1.0 + jnp.exp(-pre))
    my_gh = gh_buf[pl.ds(pl.multiple_of(mine * block, 8), block), :]
    hid[mine] = (pre * sig).astype(jnp.bfloat16)
    gpre[z] = (my_gh * (sig * (1.0 + pre * (1.0 - sig)))).astype(jnp.bfloat16)

    def spread(buf, send_sem, recv_sem, k):
        return remote(buf.at[mine], buf.at[mine], send_sem.at[k], recv_sem.at[z], along_z(k)[1])

    def spread_back(buf, send_sem, recv_sem, k):
        source, device = along_z(k)
        slot = buf.at[c * nz + source]
        return remote(slot, slot, send_sem.at[k], recv_sem.at[source], device)

    def hand_over(buf, core, i):
        ours = buf.at[pl.ds(core * nz, nz)]
        return remote(ours, ours, sib_send.at[i], sib_recv.at[i], sibling)

    def gpre_copy(k):
        return remote(gpre.at[z], gpre.at[z], p_send.at[k], p_recv.at[z], along_z(k)[1])

    def gpre_back(k):
        source, device = along_z(k)
        return remote(gpre.at[source], gpre.at[source], p_send.at[k], p_recv.at[source], device)

    for k in Z_ORDER:
        spread(hid, h_send, h_recv, k).start()
    for k in Z_ORDER:
        gpre_copy(k).start()
    for k in Z_ORDER:
        spread_back(hid, h_send, h_recv, k).wait_recv()
    hand_over(hid, c, 1).start()
    hand_over(hid, 1 - c, 1).wait_recv()

    hidden = hid[...].reshape(ROWS, hid.shape[-1])
    self_hidden = hidden[:targets, :]
    agg_two = jnp.dot(counts, hidden, preferred_element_type=jnp.float32) / degree
    agg_two = agg_two.astype(jnp.bfloat16)
    pair = jnp.concatenate([self_hidden, agg_two], axis=0)
    turned[...] = pair.astype(jnp.float32).T.astype(jnp.bfloat16)
    columns = core_rows(f, 16)

    def w2_copy(k):
        return remote(turned.at[columns, :], w2_in.at[d], q_send.at[k], q_recv.at[k], (dp_peer(k), f))

    def w2_back(k):
        here = w2_in.at[dp_from(k)]
        return remote(here, here, q_send.at[k], q_recv.at[k], (dp_from(k), f))

    each(nd, lambda k: w2_copy(k).start())
    w2_in[d] = turned[columns, :]

    for k in Z_ORDER:
        gpre_back(k).wait_recv()
    sums = jnp.dot(
        rows_t[...], gpre[...].reshape(half_rows, gpre.shape[-1]), preferred_element_type=jnp.float32
    )
    part[...] = sums.reshape(part.shape)

    def part_copy(core):
        return remote(part.at[:, core], part_in, sib_send.at[2], sib_recv.at[2], sibling)

    part_copy(1 - c).start()
    part_copy(c).wait_recv()
    part1[...] = (part[:, c] + part_in[...]).reshape(part1.shape)

    def tile_of(index):
        return (
            pl.ds(pl.multiple_of(lax.div(index, 2) * 8, 8), 8),
            pl.ds(pl.multiple_of(lax.rem(index, 2) * 128, 128), 128),
        )

    my_rows, my_lanes = tile_of(d)

    def w1_sum_copy(k):
        to = dp_peer(k)
        rows, lanes = tile_of(to)
        return remote(part1.at[rows, lanes], in1.at[d], r_send.at[k], r_recv.at[k], (to, f))

    def w1_sum_back(k):
        here = in1.at[dp_from(k)]
        return remote(here, here, r_send.at[k], r_recv.at[k], (dp_from(k), f))

    each(nd, lambda k: w1_sum_copy(k).start())
    in1[d] = part1[my_rows, my_lanes]

    each(nd, lambda k: grad_in(k).wait_recv())

    def grads_over(core):
        ours = grads.at[:, core_rows(core, 32), :]
        return remote(ours, ours, sib_send.at[3], sib_recv.at[3], sibling)

    grads_over(c).start()
    emb = jnp.dot(self_hidden, w2s[...], preferred_element_type=jnp.float32)
    emb = emb + jnp.dot(agg_two, w2n[...], preferred_element_type=jnp.float32)
    emb_ref[...] = emb.astype(jnp.bfloat16)
    grads_over(1 - c).wait_recv()
    each(nd, lambda k: w2_back(k).wait_recv())
    lane = lax.broadcasted_iota(jnp.int32, (16, 128), 1)
    total2 = jnp.zeros((32, out_grad.shape[-1]), jnp.float32)
    for p in range(nd // 2):
        first, second = w2_in[2 * p].astype(jnp.float32), w2_in[2 * p + 1].astype(jnp.float32)
        selfs = jnp.where(lane < 64, first, pltpu.roll(second, 64, 1))
        neighs = jnp.where(lane < 64, pltpu.roll(first, 64, 1), second)
        left = jnp.concatenate([selfs, neighs], axis=0).astype(jnp.bfloat16)
        right = grads[2 * p:2 * p + 2].reshape(128, out_grad.shape[-1])
        total2 = total2 + jnp.dot(left, right, preferred_element_type=jnp.float32)
    gw2_ref[mine] = total2.astype(jnp.bfloat16)
    for k in Z_ORDER:
        spread(gw2_ref, f_send, f_recv, k).start()

    each(nd, lambda k: w1_sum_back(k).wait_recv())
    sum1[...] = jnp.sum(in1[...], axis=0)
    gw1_ref[my_rows, my_lanes] = sum1[...]

    def w1_out(k):
        return remote(sum1, gw1_ref.at[my_rows, my_lanes], b_send.at[k], b_recv.at[k], (dp_peer(k), f))

    def w1_done(k):
        rows, lanes = tile_of(dp_from(k))
        return remote(sum1, gw1_ref.at[rows, lanes], b_send.at[k], b_recv.at[k], (dp_from(k), f))

    each(nd, lambda k: w1_out(k).start())
    for k in Z_ORDER:
        spread_back(gw2_ref, f_send, f_recv, k).wait_recv()
    hand_over(gw2_ref, c, 4).start()

    for j in range(1, nx):
        req_copy(j).wait_send()
    for t in range(ny - 1):
        up_copy(t, at_y(-(t // 2))).wait_send()
        down_copy(t, at_y(t // 2)).wait_send()
    for k in Z_ORDER:
        w1_copy(k).wait_send()
        row_copy(k).wait_send()
        spread(hid, h_send, h_recv, k).wait_send()
        gpre_copy(k).wait_send()
        spread(gw2_ref, f_send, f_recv, k).wait_send()
    w1_over(c).wait_send()
    hand_over(hid, c, 1).wait_send()
    part_copy(1 - c).wait_send()
    grads_over(c).wait_send()

    def picked_sent(source, carry):
        for j in range(nx):
            if j > 0:
                x_copy(source, j).wait_send()
            pair_copy(source * nx + at_x(j), c).wait_send()
        return carry

    lax.fori_loop(0, ny, picked_sent, 0)

    def sent(k):
        grad_copy(k).wait_send()
        w2_copy(k).wait_send()
        w1_sum_copy(k).wait_send()

    each(nd, sent)
    hand_over(gw2_ref, 1 - c, 4).wait_recv()
    hand_over(gw2_ref, c, 4).wait_send()

    def finished(k):
        w1_done(k).wait_recv()
        w1_out(k).wait_send()

    each(nd, finished)


def finish_kernel(emb_ref, gw1_ref, gw2_ref, out_emb, out_1s, out_1n, out_2s, out_2n):
    out_emb[...] = emb_ref[...]
    out_1s[...] = gw1_ref[:64, :]
    out_1n[...] = gw1_ref[64:, :]
    nz = gw2_ref.shape[0] // 2
    for i in range(2 * nz):
        f = 2 * (i % nz) + i // nz
        out_2s[16 * f:16 * f + 16, :] = gw2_ref[i, :16, :].astype(jnp.float32)
        out_2n[16 * f:16 * f + 16, :] = gw2_ref[i, 16:, :].astype(jnp.float32)


def local(
    nd, nf,
    features, request_rows, self_slots, adj_one, deg_one, adj_two, deg_two,
    w1_self, w1_neigh, w2_self, w2_neigh, out_grad,
):
    vmem = pl.BlockSpec(memory_space=pltpu.VMEM)
    anywhere = pl.BlockSpec(memory_space=pltpu.HBM)
    f32, bf16, i32 = jnp.float32, jnp.bfloat16, jnp.int32
    dma = pltpu.SemaphoreType.DMA
    nx, ny, nz = 4, nd // 4, nf // 2
    block, half = ROWS // nf, ROWS // 2
    adj_one = adj_one.transpose(2, 0, 1)
    adj_two = adj_two.transpose(2, 0, 1)
    lists = nz * (adj_one.shape[0] + 1)
    emb, gw1, gw2 = pl.pallas_call(
        functools.partial(step_kernel, nd, nf),
        out_shape=(
            jax.ShapeDtypeStruct((64, 256), bf16),
            jax.ShapeDtypeStruct((128, 256), f32),
            jax.ShapeDtypeStruct((nf, 32, 256), bf16),
        ),
        in_specs=[anywhere] * 12,
        out_specs=(vmem,) * 3,
        scratch_shapes=[
            pltpu.VMEM((ny, 256, 512), bf16),
            pltpu.VMEM((nd, 512), i32),
            pltpu.VMEM((nx, ny, 512), i32),
            pltpu.VMEM((nx, ny, 512), i32),
            pltpu.VMEM((ny, nx, 64, 512), bf16),
            pltpu.VMEM((nd, 128, 512), bf16),
            pltpu.VMEM((nd * 512 + 8, 128), f32),
            pltpu.VMEM((2, nz, 128, 256), bf16),
            pltpu.VMEM(adj_one.shape, i32),
            pltpu.VMEM(deg_one.shape, i32),
            pltpu.VMEM(self_slots.shape, i32),
            pltpu.VMEM((16, ROWS), i32),
            pltpu.VMEM((lists, 128), i32),
            pltpu.SMEM((lists, 128), i32),
            pltpu.VMEM((half, 128), f32),
            pltpu.VMEM((block, 128), f32),
            pltpu.VMEM((block, 128), f32),
            pltpu.VMEM(adj_two.shape, i32),
            pltpu.VMEM(deg_two.shape, i32),
            pltpu.VMEM((256, 256), bf16),
            pltpu.VMEM((256, 256), bf16),
            pltpu.VMEM(out_grad.shape, bf16),
            pltpu.VMEM((nz, 2, block, 128), bf16),
            pltpu.VMEM((nz, 2, block, 128), bf16),
            pltpu.VMEM((ROWS, 256), f32),
            pltpu.VMEM((nf, block, 256), bf16),
            pltpu.VMEM((nz, block, 256), bf16),
            pltpu.VMEM((nd, 64, 256), bf16),
            pltpu.VMEM((256, 128), bf16),
            pltpu.VMEM((256, half), bf16),
            pltpu.VMEM((nd, 16, 128), bf16),
            pltpu.VMEM((2, 2, 64, 256), f32),
            pltpu.VMEM((2, 64, 256), f32),
            pltpu.VMEM((128, 256), f32),
            pltpu.VMEM((nd, 8, 128), f32),
            pltpu.VMEM((8, 128), f32),
            dma((15,)),
            dma((ny - 1,)), dma((ny - 1,)), dma((ny - 1,)), dma((ny - 1,)),
            dma((nx,)), dma((nx,)), dma((nd,)), dma((nd,)), dma((nd,)), dma((nd,)),
            dma((nz,)), dma((nz,)), dma((5,)), dma((5,)),
            dma((nz,)), dma((nz,)), dma((nz,)), dma((nz,)), dma((nz,)), dma((nz,)),
            dma((nd,)), dma((nd,)), dma((nd,)), dma((nd,)),
            dma((nd,)), dma((nd,)), dma((nd,)), dma((nd,)),
            dma((nz,)), dma((nz,)), dma((1,)),
        ],
        compiler_params=pltpu.CompilerParams(
            collective_id=1, has_side_effects=True, vmem_limit_bytes=60 * 1024 * 1024
        ),
        name="train_step",
    )(
        features.T, request_rows[0], w1_self, w1_neigh, adj_one, deg_one, self_slots,
        adj_two, deg_two, w2_self, w2_neigh, out_grad,
    )
    return pl.pallas_call(
        finish_kernel,
        out_shape=(
            jax.ShapeDtypeStruct((64, 256), bf16),
            jax.ShapeDtypeStruct((64, 256), f32),
            jax.ShapeDtypeStruct((64, 256), f32),
            jax.ShapeDtypeStruct((256, 256), f32),
            jax.ShapeDtypeStruct((256, 256), f32),
        ),
        in_specs=[vmem] * 3,
        out_specs=(vmem,) * 5,
        compiler_params=pltpu.CompilerParams(vmem_limit_bytes=60 * 1024 * 1024),
        name="finish",
    )(emb, gw1, gw2)


def solution(mesh):
    return jax.shard_map(
        functools.partial(local, mesh.shape["dp"], mesh.shape["feat"]),
        mesh=mesh,
        in_specs=(
            P("dp", "feat"),
            P("dp", None, None),
            P("dp", None),
            P("dp", None, None),
            P("dp", None),
            P("dp", None, None),
            P("dp", None),
            P("feat", None),
            P("feat", None),
            P(),
            P(),
            P("dp", None),
        ),
        out_specs=(P("dp", None), P("feat", None), P("feat", None), P(), P()),
        check_vma=False,
    )
```

time: 473 us -> 93.1 us (0.20)
  waiting for transfers between devices: 318 us -> 0 us
  local copies, waits for them, and re-layouts: 101 us -> 0 us
  Pallas kernels: 0 us -> 92.3 us
  other arithmetic: 15.6 us -> 0 us
  starting transfers between devices: 14.7 us -> 0 us
  between operations: 14.4 us -> 0.64 us
  matrix products: 6.13 us -> 0 us
    psum x2 -> x0, waiting for transfers between devices: 265 us -> none  [the longest x1 154 us: local(): lax.psum((grad_one_self, grad_one_neigh, grad_two_self, grad_two_neigh),...]
    pallas_call x0 -> x2, Pallas kernels: none -> 92.3 us  [the longest x1 90.4 us: local(): pl.pallas_call(functools.partial(step_kernel, nd, nf), out_shape=(jax.Sha...]
    gather x4 -> x0, local copies, waits for them, and re-layouts: 79.1 us -> none  [the longest x1 57.4 us: local(): features[asked_rows.reshape(-1)].reshape(asked_rows.shape + (columns_here,))]
    all_to_all x2 -> x0, waiting for transfers between devices: 53.1 us -> none  [the longest x1 45.5 us: local(): lax.all_to_all(picked, 'dp', split_axis=0, concat_axis=1, tiled=True)]
    all_to_all x2 -> x0, starting transfers between devices: 14.7 us -> none  [the longest x1 10.5 us: local(): lax.all_to_all(request_rows, 'dp', split_axis=1, concat_axis=0, tiled=True)]
    unnamed x27 -> x0, local copies, waits for them, and re-layouts: 9.22 us -> none
    scatter-add x1 -> x0, other arithmetic: 7.94 us -> none  [neighbour_spread(): return empty.at[neighbours.reshape(-1)].add(weighted)]
    dot_general x10 -> x0, matrix products: 6.13 us -> none  [the longest x1 1.1 us: local(): jnp.dot(agg_one, w1_neigh, preferred_element_type=jnp.float32)]
  transfers between devices with their start and end apart: 4 -> 0, of which waited for: 4 -> 0; matrix products, arithmetic and copies ran while one was open for 3% -> 0% of each run, Pallas kernels for 0% -> 0%
where the time goes in v4:
time: 93.1 us; the launch traced here: 93 us
  Pallas kernels  92.3 us (99%)
    pallas_call x1, Pallas kernels, local(): pl.pallas_call(functools.partial(step_kernel, nd, nf), out_shape=(jax.Sha...  90.4 us
    pallas_call x1, Pallas kernels, local(): pl.pallas_call(finish_kernel, out_shape=(jax.ShapeDtypeStruct((64, 256),...  1.89 us

profile of v4, /device:TPU:1, one launch (start us, length us, event | category | flops | bytes accessed | tf_op | source)
XLA Modules:
  0.0 93.0 jit_solution(16531945326805004137)
XLA Ops:
  0.6 90.4 %train_step.1 = (bf16[64,256]{1,0:T(8,128)(2,1)}, f32[128,256]{1,0:T(8,128)}, bf16[16,32,256]{2,1,0:T(8,128)(2,1)}) custom-call(bf16[64,2048]{1,0:T(8,128)(2,1)} %bitcast.4, s32[32,512]{1,0:T(8,128)} %bitcast.5, bf16[64,256]{1,0:T(8,128)(2,1)} %w1s_any.1, bf16[64,256]{1,0:T(8,128)(2,1)} %w1n_any.1, s32[10,1,704]{2,1,0:T(1,128)} %bitcast.6, ...), custom_call_target="tpu_custom_call" | custom-call | tf_op jit(solution)/shard_map/train_step/pallas_call | solution.py:554
  91.1 1.9 %finish.1 = (bf16[64,256]{1,0:T(8,128)(2,1)}, f32[64,256]{1,0:T(8,128)}, f32[64,256]{1,0:T(8,128)}, f32[256,256]{1,0:T(8,128)}, f32[256,256]{1,0:T(8,128)}) custom-call(bf16[64,256]{1,0:T(8,128)(2,1)} %get-tuple-element.8.emb_ref, f32[128,256]{1,0:T(8,128)} %get-tuple-element.9.gw1_ref, bf16[16,32,256]{2,1,0:T(8,128)(2,1)} %get-tuple-element.10.gw2_ref), custom_call_target="tpu_custom_call" | custom-call | tf_op jit(solution)/shard_map/finish/pallas_call | solution.py:617

commit v5 on v4

--- a/solution.py
+++ b/solution.py
@@ -79,76 +79,87 @@
     def core_rows(core, size):
         return pl.ds(pl.multiple_of(core * size, 16), size)
 
+    barrier = pltpu.get_barrier_semaphore()
+
+    def greet(to):
+        pl.semaphore_signal(barrier, inc=1, device_id=to, device_id_type=MESH)
+
     sources = [
         (feat_any.at[:, 512 * q:512 * q + 512], blocks.at[y, 64 * q:64 * q + 64, :]) for q in range(4)
     ] + [
         (req_any, req_ref),
-        (w1s_any, w1.at[0, z, core_rows(c, 64), :]),
-        (w1n_any, w1.at[1, z, core_rows(c, 64), :]),
+        (w1s_any, w1.at[z, 0, core_rows(c, 64), :]),
+        (w1n_any, w1.at[z, 1, core_rows(c, 64), :]),
         (adj_any, adj_ref), (deg_any, deg_ref), (self_any, self_ref),
         (adj_two_any, adj_two), (deg_two_any, deg_two),
         (w2s_any, w2s), (w2n_any, w2n), (grad_any, grad_ref),
     ]
     fetches = [pltpu.make_async_copy(src, dst, fetch.at[i]) for i, (src, dst) in enumerate(sources)]
-    for copy in fetches:
+    for copy in [fetches[4]] + fetches[:4] + fetches[5:7]:
         copy.start()
-
-    barrier = pltpu.get_barrier_semaphore()
-
-    def greet(to):
-        pl.semaphore_signal(barrier, inc=1, device_id=to, device_id_type=MESH)
 
     greet(sibling)
     for k in range(1, nz):
         greet(along_z(k)[1])
     each(nd, lambda k: greet((dp_peer(k), f)))
+    pl.semaphore_wait(barrier, 1 + nz - 1 + nd - 1)
+
+    def req_copy(j):
+        to = at_x(j)
+        return remote(req_by_x.at[to], req_in.at[x], req_send.at[j], req_recv.at[x], (y * nx + to, f))
+
+    def req_back(j):
+        here = at_x(j)
+        return remote(req_by_x.at[here], req_in.at[here], req_send.at[j], req_recv.at[here], (y * nx + here, f))
+
+    def half(source, h):
+        return blocks.at[source, pl.ds(128 * h, 128), :]
+
+    def up_copy(t, source):
+        part = half(source, t % 2)
+        return remote(part, part, up_send.at[t], up_recv.at[t], (at_y(1) * nx + x, f))
+
+    def down_copy(t, source):
+        part = half(source, 1 - t % 2)
+        return remote(part, part, down_send.at[t], down_recv.at[t], (at_y(-1) * nx + x, f))
+
+    def w1_part(source):
+        return w1.at[source, :, core_rows(c, 64), :]
+
+    def w1_copy(k):
+        return remote(w1_part(z), w1_part(z), w1_send.at[k], w1_recv.at[z], along_z(k)[1])
+
+    def w1_back(k):
+        source, device = along_z(k)
+        return remote(w1_part(source), w1_part(source), w1_send.at[k], w1_recv.at[source], device)
+
+    def w1_over(core):
+        ours = w1.at[:, :, core_rows(core, 64), :]
+        return remote(ours, ours, sib_send.at[0], sib_recv.at[0], sibling)
+
+    def first_copies(t):
+        copies = []
+        for up, h in ((True, t % 2), (False, 1 - t % 2)):
+            for q in (2 * h, 2 * h + 1):
+                copies.append(remote(
+                    feat_any.at[:, 512 * q:512 * q + 512], blocks.at[y, 64 * q:64 * q + 64, :],
+                    (up_send if up else down_send).at[t], (up_recv if up else down_recv).at[t],
+                    (at_y(1 if up else -1) * nx + x, f),
+                ))
+        return copies
+
+    for t in range(2):
+        for copy in first_copies(t):
+            copy.start()
+    for copy in fetches[7:]:
+        copy.start()
     fetches[4].wait()
     for owner in range(nd):
         req_by_x[owner % nx, owner // nx:owner // nx + 1, :] = req_ref[owner:owner + 1, :]
+    for j in range(1, nx):
+        req_copy(j).start()
     for copy in fetches[:4] + fetches[5:7]:
         copy.wait()
-    pl.semaphore_wait(barrier, 1 + nz - 1 + nd - 1)
-
-    def req_copy(j):
-        to = at_x(j)
-        return remote(req_by_x.at[to], req_in.at[x], req_send.at[j], req_recv.at[x], (y * nx + to, f))
-
-    def req_back(j):
-        here = at_x(j)
-        return remote(req_by_x.at[here], req_in.at[here], req_send.at[j], req_recv.at[here], (y * nx + here, f))
-
-    def half(source, h):
-        return blocks.at[source, pl.ds(128 * h, 128), :]
-
-    def up_copy(t, source):
-        part = half(source, t % 2)
-        return remote(part, part, up_send.at[t], up_recv.at[t], (at_y(1) * nx + x, f))
-
-    def down_copy(t, source):
-        part = half(source, 1 - t % 2)
-        return remote(part, part, down_send.at[t], down_recv.at[t], (at_y(-1) * nx + x, f))
-
-    def w1_part(source):
-        return w1.at[:, source, core_rows(c, 64), :]
-
-    def w1_copy(k):
-        return remote(w1_part(z), w1_part(z), w1_send.at[k], w1_recv.at[z], along_z(k)[1])
-
-    def w1_back(k):
-        source, device = along_z(k)
-        return remote(w1_part(source), w1_part(source), w1_send.at[k], w1_recv.at[source], device)
-
-    def w1_over(core):
-        ours = w1.at[:, :, core_rows(core, 64), :]
-        return remote(ours, ours, sib_send.at[0], sib_recv.at[0], sibling)
-
-    for j in range(1, nx):
-        req_copy(j).start()
-    for t in range(2):
-        up_copy(t, y).start()
-        down_copy(t, y).start()
-    for k in Z_ORDER:
-        w1_copy(k).start()
     req_in[x] = req_by_x[x]
     for j in range(1, nx):
         req_back(j).wait_recv()
@@ -186,7 +197,7 @@
     def process(count, source_of):
         def step(k, carry):
             source = source_of(lax.div(k, nx))
-            j = lax.rem(k + 1, nx)
+            j = lax.rem(k + 2, nx)
             stage[source, j] = pick(source, j)
 
             @pl.when(j > 0)
@@ -228,6 +239,8 @@
 
     process(1, lambda i: y)
 
+    for k in Z_ORDER:
+        w1_copy(k).start()
     for copy in fetches[7:]:
         copy.wait()
     fanout = adj_ref.shape[0]
@@ -270,26 +283,30 @@
     def around(s):
         return lambda i: lax.rem(y + (2 * i - 1) * (1 + s) + ny, ny)
 
+    def one(offset):
+        return lambda i: at_y(offset)
+
     steps = ny // 2
-    for s in range(steps):
+    for t in range(ny - 1):
+        s = t // 2
         below, above = at_y(-1 - s), at_y(1 + s)
-        for h in range(2 if s < steps - 1 else 1):
-            t = 2 * s + h
-            up_copy(t, below).wait_recv()
-            if t + 2 < ny - 1:
-                up_copy(t + 2, below).start()
-            down_copy(t, above).wait_recv()
-            if t + 2 < ny - 1:
-                down_copy(t + 2, above).start()
-        process(2 if s < steps - 1 else 1, around(s))
-        if s == 0:
-            collect(1, lambda i: y)
-        else:
-            collect(2, around(s - 1))
-        if s == 1:
-            absorb(1, lambda i: y)
-        if s > 1:
-            absorb(2, around(s - 2))
+        up_copy(t, below).wait_recv()
+        if t + 2 < ny - 1:
+            up_copy(t + 2, below).start()
+        down_copy(t, above).wait_recv()
+        if t + 2 < ny - 1:
+            down_copy(t + 2, above).start()
+        if t % 2 == 1:
+            process(2, around(s))
+            if s == 1:
+                collect(1, one(0))
+            if s == 2:
+                collect(2, around(0))
+                absorb(1, one(0))
+        elif t == ny - 2:
+            process(1, one(1 + s))
+    absorb(2, around(0))
+    collect(2, around(1))
 
     g_rows = core_rows(c, 32)
 
@@ -300,15 +317,15 @@
         here = grads.at[dp_from(k), g_rows, :]
         return remote(here, here, g_send.at[k], g_recv.at[k], (dp_from(k), f))
 
+    absorb(2, around(steps - 3))
+    collect(2, around(steps - 2))
+    absorb(2, around(steps - 2))
+    collect(1, around(steps - 1))
+    absorb(1, around(steps - 1))
+    to_smem.wait()
     for k in Z_ORDER:
         w1_back(k).wait_recv()
     w1_over(c).start()
-    absorb(2, around(steps - 2))
-    collect(1, around(steps - 1))
-    each(nd, lambda k: grad_copy(k).start())
-    grads[d, g_rows, :] = grad_ref[g_rows, :]
-    absorb(1, around(steps - 1))
-    to_smem.wait()
 
     def row_copy(k):
         to, device = along_z(k)
@@ -319,24 +336,19 @@
         return remote(x_out.at[source], x_in.at[source], a_send.at[k], a_recv.at[source], device)
 
     def sum_rows(t, carry):
-        k = lax.rem(t + nz // 2, nz)
+        odd = lax.rem(t, 2)
+        k = nz // 2 + lax.div(t, 2) * (1 - odd) - lax.div(t + 1, 2) * odd
         to = lax.rem(z + k, nz)
         base = to * (fanout + 1)
-
-        def eight(m, inner):
-            for r in range(8):
-                i = m * 8 + r
-                own[pl.ds(i, 1), :] = table[pl.ds(slots[base + fanout, i], 1), :]
-                terms = [table[pl.ds(slots[base + j, i], 1), :] for j in range(fanout)]
-                while len(terms) > 1:
-                    terms = [sum(terms[n:n + 2][1:], terms[n]) for n in range(0, len(terms), 2)]
-                total[pl.ds(i, 1), :] = terms[0]
-            return inner
-
-        lax.fori_loop(0, block // 8, eight, 0)
-        x_out[to, 0] = own[...].astype(jnp.bfloat16)
+        for i in range(block):
+            own[i:i + 1, :] = table[pl.ds(slots[base + fanout, i], 1), :]
+            terms = [table[pl.ds(slots[base + j, i], 1), :] for j in range(fanout)]
+            while len(terms) > 1:
+                terms = [sum(terms[n:n + 2][1:], terms[n]) for n in range(0, len(terms), 2)]
+            total[i:i + 1, :] = terms[0]
+        x_out[to, :, :128] = own[...].astype(jnp.bfloat16)
         mean = total[...] * scale[pl.ds(pl.multiple_of(to * block, 8), block), :]
-        x_out[to, 1] = mean.astype(jnp.bfloat16)
+        x_out[to, :, 128:] = mean.astype(jnp.bfloat16)
 
         @pl.when(k > 0)
         def _():
@@ -345,20 +357,20 @@
         return carry
 
     lax.fori_loop(0, nz, sum_rows, 0)
+    each(nd, lambda k: grad_copy(k).start())
+    grads[d, g_rows, :] = grad_ref[g_rows, :]
     x_in[z] = x_out[z]
-    for kind in range(2):
-        rows_t[128 * kind:128 * kind + 128, :] = (
-            x_out[:, kind].reshape(half_rows, 128).astype(jnp.float32).T.astype(jnp.bfloat16)
-        )
+    rows_t[...] = x_out[...].reshape(half_rows, 256).astype(jnp.float32).T.astype(jnp.bfloat16)
     w1_over(1 - c).wait_recv()
 
     pre = jnp.zeros((block, w1.shape[-1]), jnp.float32)
-    for k in (0,) + tuple(reversed(Z_ORDER)):
+    for k in (0, 5, 4, 6, 3, 7, 2, 1):
         if k > 0:
             row_back(k).wait_recv()
         source = lax.rem(z + k, nz)
-        for kind in range(2):
-            pre = pre + jnp.dot(x_in[source, kind], w1[kind, source], preferred_element_type=jnp.float32)
+        pre = pre + jnp.dot(
+            x_in[source], w1[source].reshape(256, w1.shape[-1]), preferred_element_type=jnp.float32
+        )
     sig = 1.0 / (1.0 + jnp.exp(-pre))
     my_gh = gh_buf[pl.ds(pl.multiple_of(mine * block, 8), block), :]
     hid[mine] = (pre * sig).astype(jnp.bfloat16)
@@ -390,6 +402,17 @@
     for k in Z_ORDER:
         spread_back(hid, h_send, h_recv, k).wait_recv()
     hand_over(hid, c, 1).start()
+    for k in Z_ORDER:
+        gpre_back(k).wait_recv()
+    sums = jnp.dot(
+        rows_t[...], gpre[...].reshape(half_rows, gpre.shape[-1]), preferred_element_type=jnp.float32
+    )
+    part[...] = sums.reshape(part.shape)
+
+    def part_copy(core):
+        return remote(part.at[:, core], part_in, sib_send.at[2], sib_recv.at[2], sibling)
+
+    part_copy(1 - c).start()
     hand_over(hid, 1 - c, 1).wait_recv()
 
     hidden = hid[...].reshape(ROWS, hid.shape[-1])
@@ -410,17 +433,6 @@
     each(nd, lambda k: w2_copy(k).start())
     w2_in[d] = turned[columns, :]
 
-    for k in Z_ORDER:
-        gpre_back(k).wait_recv()
-    sums = jnp.dot(
-        rows_t[...], gpre[...].reshape(half_rows, gpre.shape[-1]), preferred_element_type=jnp.float32
-    )
-    part[...] = sums.reshape(part.shape)
-
-    def part_copy(core):
-        return remote(part.at[:, core], part_in, sib_send.at[2], sib_recv.at[2], sibling)
-
-    part_copy(1 - c).start()
     part_copy(c).wait_recv()
     part1[...] = (part[:, c] + part_in[...]).reshape(part1.shape)
 
@@ -568,7 +580,7 @@
             pltpu.VMEM((ny, nx, 64, 512), bf16),
             pltpu.VMEM((nd, 128, 512), bf16),
             pltpu.VMEM((nd * 512 + 8, 128), f32),
-            pltpu.VMEM((2, nz, 128, 256), bf16),
+            pltpu.VMEM((nz, 2, 128, 256), bf16),
             pltpu.VMEM(adj_one.shape, i32),
             pltpu.VMEM(deg_one.shape, i32),
             pltpu.VMEM(self_slots.shape, i32),
@@ -583,8 +595,8 @@
             pltpu.VMEM((256, 256), bf16),
             pltpu.VMEM((256, 256), bf16),
             pltpu.VMEM(out_grad.shape, bf16),
-            pltpu.VMEM((nz, 2, block, 128), bf16),
-            pltpu.VMEM((nz, 2, block, 128), bf16),
+            pltpu.VMEM((nz, block, 256), bf16),
+            pltpu.VMEM((nz, block, 256), bf16),
             pltpu.VMEM((ROWS, 256), f32),
             pltpu.VMEM((nf, block, 256), bf16),
             pltpu.VMEM((nz, block, 256), bf16),

time: 93.1 us -> 89.7 us (0.963)
  Pallas kernels: 92.3 us -> 88.6 us
    pallas_call x1, Pallas kernels: 90.4 us -> 86.7 us  [local(): pl.pallas_call(functools.partial(step_kernel, nd, nf), out_shape=(jax.Sha...]
where the time goes in v5:
time: 89.7 us; the launch traced here: 89.3 us
  Pallas kernels  88.6 us (99%)
    pallas_call x1, Pallas kernels, local(): pl.pallas_call(functools.partial(step_kernel, nd, nf), out_shape=(jax.Sha...  86.7 us
    pallas_call x1, Pallas kernels, local(): pl.pallas_call(finish_kernel, out_shape=(jax.ShapeDtypeStruct((64, 256),...  1.89 us

profile of v5, /device:TPU:1, one launch (start us, length us, event | category | flops | bytes accessed | tf_op | source)
XLA Modules:
  0.0 89.3 jit_solution(6789515244784944221)
XLA Ops:
  0.6 86.7 %train_step.1 = (bf16[64,256]{1,0:T(8,128)(2,1)}, f32[128,256]{1,0:T(8,128)}, bf16[16,32,256]{2,1,0:T(8,128)(2,1)}) custom-call(bf16[64,2048]{1,0:T(8,128)(2,1)} %bitcast.4, s32[32,512]{1,0:T(8,128)} %bitcast.5, bf16[64,256]{1,0:T(8,128)(2,1)} %w1s_any.1, bf16[64,256]{1,0:T(8,128)(2,1)} %w1n_any.1, s32[10,1,704]{2,1,0:T(1,128)} %bitcast.6, ...), custom_call_target="tpu_custom_call" | custom-call | tf_op jit(solution)/shard_map/train_step/pallas_call | solution.py:566
  87.4 1.9 %finish.1 = (bf16[64,256]{1,0:T(8,128)(2,1)}, f32[64,256]{1,0:T(8,128)}, f32[64,256]{1,0:T(8,128)}, f32[256,256]{1,0:T(8,128)}, f32[256,256]{1,0:T(8,128)}) custom-call(bf16[64,256]{1,0:T(8,128)(2,1)} %get-tuple-element.8.emb_ref, f32[128,256]{1,0:T(8,128)} %get-tuple-element.9.gw1_ref, bf16[16,32,256]{2,1,0:T(8,128)(2,1)} %get-tuple-element.10.gw2_ref), custom_call_target="tpu_custom_call" | custom-call | tf_op jit(solution)/shard_map/finish/pallas_call | solution.py:629

commit v6 on v5

--- a/solution.py
+++ b/solution.py
@@ -76,6 +76,12 @@
             device_id=to, device_id_type=MESH,
         )
 
+    def all_in(ref, sem):
+        remote(ref, ref, sem, sem, sibling).wait_recv()
+
+    def all_out(ref, sem):
+        remote(ref, ref, sem, sem, sibling).wait_send()
+
     def core_rows(core, size):
         return pl.ds(pl.multiple_of(core * size, 16), size)
 
@@ -94,7 +100,8 @@
         (adj_two_any, adj_two), (deg_two_any, deg_two),
         (w2s_any, w2s), (w2n_any, w2n), (grad_any, grad_ref),
     ]
-    fetches = [pltpu.make_async_copy(src, dst, fetch.at[i]) for i, (src, dst) in enumerate(sources)]
+    kinds = (0, 0, 0, 0, 1, 2, 2, 3, 4, 5, 6, 7, 8, 9, 10)
+    fetches = [pltpu.make_async_copy(src, dst, fetch.at[i]) for i, (src, dst) in zip(kinds, sources)]
     for copy in [fetches[4]] + fetches[:4] + fetches[5:7]:
         copy.start()
 
@@ -106,32 +113,24 @@
 
     def req_copy(j):
         to = at_x(j)
-        return remote(req_by_x.at[to], req_in.at[x], req_send.at[j], req_recv.at[x], (y * nx + to, f))
-
-    def req_back(j):
-        here = at_x(j)
-        return remote(req_by_x.at[here], req_in.at[here], req_send.at[j], req_recv.at[here], (y * nx + here, f))
+        return remote(req_by_x.at[to], req_in.at[x], req_send.at[0], req_recv.at[0], (y * nx + to, f))
 
     def half(source, h):
-        return blocks.at[source, pl.ds(128 * h, 128), :]
+        return blocks.at[source, core_rows(h, 128), :]
 
     def up_copy(t, source):
-        part = half(source, t % 2)
-        return remote(part, part, up_send.at[t], up_recv.at[t], (at_y(1) * nx + x, f))
+        part = half(source, lax.rem(t, 2))
+        return remote(part, part, up_send.at[0], up_recv.at[t], (at_y(1) * nx + x, f))
 
     def down_copy(t, source):
-        part = half(source, 1 - t % 2)
-        return remote(part, part, down_send.at[t], down_recv.at[t], (at_y(-1) * nx + x, f))
+        part = half(source, 1 - lax.rem(t, 2))
+        return remote(part, part, down_send.at[0], down_recv.at[t], (at_y(-1) * nx + x, f))
 
     def w1_part(source):
         return w1.at[source, :, core_rows(c, 64), :]
 
     def w1_copy(k):
-        return remote(w1_part(z), w1_part(z), w1_send.at[k], w1_recv.at[z], along_z(k)[1])
-
-    def w1_back(k):
-        source, device = along_z(k)
-        return remote(w1_part(source), w1_part(source), w1_send.at[k], w1_recv.at[source], device)
+        return remote(w1_part(z), w1_part(z), w1_send.at[0], w1_recv.at[0], along_z(k)[1])
 
     def w1_over(core):
         ours = w1.at[:, :, core_rows(core, 64), :]
@@ -143,7 +142,7 @@
             for q in (2 * h, 2 * h + 1):
                 copies.append(remote(
                     feat_any.at[:, 512 * q:512 * q + 512], blocks.at[y, 64 * q:64 * q + 64, :],
-                    (up_send if up else down_send).at[t], (up_recv if up else down_recv).at[t],
+                    (up_send if up else down_send).at[0], (up_recv if up else down_recv).at[t],
                     (at_y(1 if up else -1) * nx + x, f),
                 ))
         return copies
@@ -158,29 +157,24 @@
         req_by_x[owner % nx, owner // nx:owner // nx + 1, :] = req_ref[owner:owner + 1, :]
     for j in range(1, nx):
         req_copy(j).start()
-    for copy in fetches[:4] + fetches[5:7]:
-        copy.wait()
+    pltpu.make_async_copy(blocks.at[y], blocks.at[y], fetch.at[0]).wait()
+    pltpu.make_async_copy(w1.at[z, :, core_rows(c, 64), :], w1.at[z, :, core_rows(c, 64), :], fetch.at[2]).wait()
     req_in[x] = req_by_x[x]
-    for j in range(1, nx):
-        req_back(j).wait_recv()
+    all_in(req_in.at[pl.ds(0, nx - 1)], req_recv.at[0])
 
     def x_copy(source, j):
         slot = source * nx + x
         return remote(
             stage.at[source, j], samp.at[slot, core_rows(c, 64), :],
-            x_send.at[source * nx + j], x_recv.at[slot], (y * nx + at_x(j), f),
+            x_send.at[0], x_recv.at[source], (y * nx + at_x(j), f),
         )
 
-    def x_back(source, j):
-        slot = source * nx + at_x(j)
-        return remote(
-            stage.at[source, j], samp.at[slot, core_rows(c, 64), :],
-            x_send.at[source * nx + j], x_recv.at[slot], (y * nx + at_x(j), f),
-        )
-
-    def pair_copy(slot, core):
-        ours = samp.at[slot, core_rows(core, 64), :]
-        return remote(ours, ours, pair_send.at[slot], pair_recv.at[slot], sibling)
+    def slots_of(source, count, core):
+        return samp.at[pl.ds(source * nx, count), core_rows(core, 64), :]
+
+    def pair_copy(source, core):
+        ours = slots_of(source, nx, core)
+        return remote(ours, ours, pair_send.at[0], pair_recv.at[source], sibling)
 
     node = lax.broadcasted_iota(jnp.int32, (512, cap), 0)
 
@@ -209,38 +203,76 @@
         lax.fori_loop(0, count * nx, step, 0)
 
     def collect(count, source_of):
-        def step(k, carry):
-            source = source_of(lax.div(k, nx))
-            j = lax.rem(k, nx)
-
-            @pl.when(j > 0)
-            def _():
-                x_back(source, j).wait_recv()
-
-            @pl.when(j == 0)
-            def _():
-                samp[source * nx + x, core_rows(c, 64), :] = stage[source, 0]
-
-            pair_copy(source * nx + at_x(j), c).start()
+        def step(u, carry):
+            source = source_of(u)
+            all_in(slots_of(source, nx - 1, c), x_recv.at[source])
+            samp[source * nx + x, core_rows(c, 64), :] = stage[source, 0]
+            pair_copy(source, c).start()
             return carry
 
-        lax.fori_loop(0, count * nx, step, 0)
+        lax.fori_loop(0, count, step, 0)
 
     def absorb(count, source_of):
-        def step(k, carry):
-            source = source_of(lax.div(k, nx))
-            slot = source * nx + at_x(lax.rem(k, nx))
-            pair_copy(slot, 1 - c).wait_recv()
-            here = pl.ds(pl.multiple_of(slot * cap, 8), cap)
-            table[here, :] = samp[slot].astype(jnp.float32).T
+        def step(u, carry):
+            source = source_of(u)
+            pair_copy(source, 1 - c).wait_recv()
+            for j in range(nx):
+                slot = source * nx + j
+                here = pl.ds(pl.multiple_of(slot * cap, 8), cap)
+                table[here, :] = samp[slot].astype(jnp.float32).T
             return carry
 
-        lax.fori_loop(0, count * nx, step, 0)
-
-    process(1, lambda i: y)
+        lax.fori_loop(0, count, step, 0)
 
     for k in Z_ORDER:
         w1_copy(k).start()
+    steps = ny // 2
+
+    def in_step(i):
+        return 2 - lax.div(steps - i, steps) - lax.div(i, steps)
+
+    def source_in(i):
+        return lambda u: lax.rem(y + (2 * u - 1) * i + ny, ny)
+
+    def pass_on(t, i):
+        below, above = at_y(-i), at_y(i)
+        more = t + 2 < ny - 1
+        up_copy(t, below).wait_recv()
+
+        @pl.when(more)
+        def _():
+            up_copy(t + 2, below).start()
+
+        down_copy(t, above).wait_recv()
+
+        @pl.when(more)
+        def _():
+            down_copy(t + 2, above).start()
+
+    def gather_late(i):
+        @pl.when(i >= 3)
+        def _():
+            absorb(in_step(i - 3), source_in(i - 3))
+
+        @pl.when((i >= 2) & (i <= steps + 2))
+        def _():
+            collect(in_step(i - 2), source_in(i - 2))
+
+    def ring_step(i, carry):
+        @pl.when(i > 0)
+        def _():
+            pass_on(2 * i - 2, i)
+
+        @pl.when((i > 0) & (i < steps))
+        def _():
+            pass_on(2 * i - 1, i)
+
+        process(in_step(i), source_in(i))
+        gather_late(i)
+        return carry
+
+    lax.fori_loop(0, steps + 1, ring_step, 0)
+
     for copy in fetches[7:]:
         copy.wait()
     fanout = adj_ref.shape[0]
@@ -274,66 +306,33 @@
     degree_row = degree_row.astype(jnp.float32)
     degree = jnp.broadcast_to(degree_row, (8, targets)).T[:, :1]
     grad_agg = contract_lanes(out_grad, w2n[...]) / degree
-    gh_buf[...] = jnp.dot(
-        counts, grad_agg, precision=lax.Precision.HIGHEST, preferred_element_type=jnp.float32
-    )
+    high = grad_agg.astype(jnp.bfloat16)
+    low = (grad_agg - high.astype(jnp.float32)).astype(jnp.bfloat16)
+    both = jnp.concatenate([counts, counts], axis=1).astype(jnp.bfloat16)
+    gh_buf[...] = jnp.dot(both, jnp.concatenate([high, low], axis=0), preferred_element_type=jnp.float32)
     gh_buf[:targets, :] += contract_lanes(out_grad, w2s[...])
     counts = counts.T.astype(jnp.bfloat16)
 
-    def around(s):
-        return lambda i: lax.rem(y + (2 * i - 1) * (1 + s) + ny, ny)
-
-    def one(offset):
-        return lambda i: at_y(offset)
-
-    steps = ny // 2
-    for t in range(ny - 1):
-        s = t // 2
-        below, above = at_y(-1 - s), at_y(1 + s)
-        up_copy(t, below).wait_recv()
-        if t + 2 < ny - 1:
-            up_copy(t + 2, below).start()
-        down_copy(t, above).wait_recv()
-        if t + 2 < ny - 1:
-            down_copy(t + 2, above).start()
-        if t % 2 == 1:
-            process(2, around(s))
-            if s == 1:
-                collect(1, one(0))
-            if s == 2:
-                collect(2, around(0))
-                absorb(1, one(0))
-        elif t == ny - 2:
-            process(1, one(1 + s))
-    absorb(2, around(0))
-    collect(2, around(1))
+    lax.fori_loop(steps + 1, steps + 4, lambda i, carry: (gather_late(i), carry)[1], 0)
 
     g_rows = core_rows(c, 32)
 
     def grad_copy(k):
-        return remote(grad_ref.at[g_rows, :], grads.at[d, g_rows, :], g_send.at[k], g_recv.at[k], (dp_peer(k), f))
-
-    def grad_in(k):
-        here = grads.at[dp_from(k), g_rows, :]
-        return remote(here, here, g_send.at[k], g_recv.at[k], (dp_from(k), f))
-
-    absorb(2, around(steps - 3))
-    collect(2, around(steps - 2))
-    absorb(2, around(steps - 2))
-    collect(1, around(steps - 1))
-    absorb(1, around(steps - 1))
+        return remote(grad_ref.at[g_rows, :], grads.at[d, g_rows, :], g_send.at[0], g_recv.at[0], (dp_peer(k), f))
+
+    some_grads = grads.at[pl.ds(0, nd - 1), pl.ds(0, 32), :]
+
     to_smem.wait()
-    for k in Z_ORDER:
-        w1_back(k).wait_recv()
+    all_in(w1.at[pl.ds(0, nz - 1), :, pl.ds(0, 64), :], w1_recv.at[0])
     w1_over(c).start()
 
     def row_copy(k):
         to, device = along_z(k)
-        return remote(x_out.at[to], x_in.at[z], a_send.at[k], a_recv.at[z], device)
+        return remote(x_out.at[to], x_in.at[z], a_send.at[0], a_recv.at[z], device)
 
     def row_back(k):
         source, device = along_z(k)
-        return remote(x_out.at[source], x_in.at[source], a_send.at[k], a_recv.at[source], device)
+        return remote(x_out.at[source], x_in.at[source], a_send.at[0], a_recv.at[source], device)
 
     def sum_rows(t, carry):
         odd = lax.rem(t, 2)
@@ -377,33 +376,25 @@
     gpre[z] = (my_gh * (sig * (1.0 + pre * (1.0 - sig)))).astype(jnp.bfloat16)
 
     def spread(buf, send_sem, recv_sem, k):
-        return remote(buf.at[mine], buf.at[mine], send_sem.at[k], recv_sem.at[z], along_z(k)[1])
-
-    def spread_back(buf, send_sem, recv_sem, k):
-        source, device = along_z(k)
-        slot = buf.at[c * nz + source]
-        return remote(slot, slot, send_sem.at[k], recv_sem.at[source], device)
+        return remote(buf.at[mine], buf.at[mine], send_sem.at[0], recv_sem.at[0], along_z(k)[1])
+
+    def most(buf):
+        return buf.at[pl.ds(0, nz - 1)]
 
     def hand_over(buf, core, i):
         ours = buf.at[pl.ds(core * nz, nz)]
         return remote(ours, ours, sib_send.at[i], sib_recv.at[i], sibling)
 
     def gpre_copy(k):
-        return remote(gpre.at[z], gpre.at[z], p_send.at[k], p_recv.at[z], along_z(k)[1])
-
-    def gpre_back(k):
-        source, device = along_z(k)
-        return remote(gpre.at[source], gpre.at[source], p_send.at[k], p_recv.at[source], device)
+        return remote(gpre.at[z], gpre.at[z], p_send.at[0], p_recv.at[0], along_z(k)[1])
 
     for k in Z_ORDER:
         spread(hid, h_send, h_recv, k).start()
     for k in Z_ORDER:
         gpre_copy(k).start()
-    for k in Z_ORDER:
-        spread_back(hid, h_send, h_recv, k).wait_recv()
+    all_in(most(hid), h_recv.at[0])
     hand_over(hid, c, 1).start()
-    for k in Z_ORDER:
-        gpre_back(k).wait_recv()
+    all_in(most(gpre), p_recv.at[0])
     sums = jnp.dot(
         rows_t[...], gpre[...].reshape(half_rows, gpre.shape[-1]), preferred_element_type=jnp.float32
     )
@@ -424,11 +415,7 @@
     columns = core_rows(f, 16)
 
     def w2_copy(k):
-        return remote(turned.at[columns, :], w2_in.at[d], q_send.at[k], q_recv.at[k], (dp_peer(k), f))
-
-    def w2_back(k):
-        here = w2_in.at[dp_from(k)]
-        return remote(here, here, q_send.at[k], q_recv.at[k], (dp_from(k), f))
+        return remote(turned.at[columns, :], w2_in.at[d], q_send.at[0], q_recv.at[0], (dp_peer(k), f))
 
     each(nd, lambda k: w2_copy(k).start())
     w2_in[d] = turned[columns, :]
@@ -447,16 +434,13 @@
     def w1_sum_copy(k):
         to = dp_peer(k)
         rows, lanes = tile_of(to)
-        return remote(part1.at[rows, lanes], in1.at[d], r_send.at[k], r_recv.at[k], (to, f))
-
-    def w1_sum_back(k):
-        here = in1.at[dp_from(k)]
-        return remote(here, here, r_send.at[k], r_recv.at[k], (dp_from(k), f))
-
+        return remote(part1.at[rows, lanes], in1.at[d], r_send.at[0], r_recv.at[0], (to, f))
+
+    some_tiles = in1.at[pl.ds(0, nd - 1)]
     each(nd, lambda k: w1_sum_copy(k).start())
     in1[d] = part1[my_rows, my_lanes]
 
-    each(nd, lambda k: grad_in(k).wait_recv())
+    all_in(some_grads, g_recv.at[0])
 
     def grads_over(core):
         ours = grads.at[:, core_rows(core, 32), :]
@@ -467,7 +451,7 @@
     emb = emb + jnp.dot(agg_two, w2n[...], preferred_element_type=jnp.float32)
     emb_ref[...] = emb.astype(jnp.bfloat16)
     grads_over(1 - c).wait_recv()
-    each(nd, lambda k: w2_back(k).wait_recv())
+    all_in(w2_in.at[pl.ds(0, nd - 1)], q_recv.at[0])
     lane = lax.broadcasted_iota(jnp.int32, (16, 128), 1)
     total2 = jnp.zeros((32, out_grad.shape[-1]), jnp.float32)
     for p in range(nd // 2):
@@ -481,61 +465,38 @@
     for k in Z_ORDER:
         spread(gw2_ref, f_send, f_recv, k).start()
 
-    each(nd, lambda k: w1_sum_back(k).wait_recv())
+    all_in(some_tiles, r_recv.at[0])
     sum1[...] = jnp.sum(in1[...], axis=0)
     gw1_ref[my_rows, my_lanes] = sum1[...]
 
     def w1_out(k):
-        return remote(sum1, gw1_ref.at[my_rows, my_lanes], b_send.at[k], b_recv.at[k], (dp_peer(k), f))
-
-    def w1_done(k):
-        rows, lanes = tile_of(dp_from(k))
-        return remote(sum1, gw1_ref.at[rows, lanes], b_send.at[k], b_recv.at[k], (dp_from(k), f))
+        return remote(sum1, gw1_ref.at[my_rows, my_lanes], b_send.at[0], b_recv.at[0], (dp_peer(k), f))
 
     each(nd, lambda k: w1_out(k).start())
-    for k in Z_ORDER:
-        spread_back(gw2_ref, f_send, f_recv, k).wait_recv()
+    all_in(most(gw2_ref), f_recv.at[0])
     hand_over(gw2_ref, c, 4).start()
 
-    for j in range(1, nx):
-        req_copy(j).wait_send()
-    for t in range(ny - 1):
-        up_copy(t, at_y(-(t // 2))).wait_send()
-        down_copy(t, at_y(t // 2)).wait_send()
-    for k in Z_ORDER:
-        w1_copy(k).wait_send()
-        row_copy(k).wait_send()
-        spread(hid, h_send, h_recv, k).wait_send()
-        gpre_copy(k).wait_send()
-        spread(gw2_ref, f_send, f_recv, k).wait_send()
+    all_out(req_in.at[pl.ds(0, nx - 1)], req_send.at[0])
+    all_out(blocks.at[pl.ds(0, ny - 1), pl.ds(0, 128), :], up_send.at[0])
+    all_out(blocks.at[pl.ds(0, ny - 1), pl.ds(0, 128), :], down_send.at[0])
+    all_out(w1.at[pl.ds(0, nz - 1), :, pl.ds(0, 64), :], w1_send.at[0])
+    all_out(most(x_out), a_send.at[0])
+    all_out(most(hid), h_send.at[0])
+    all_out(most(gpre), p_send.at[0])
+    all_out(most(gw2_ref), f_send.at[0])
     w1_over(c).wait_send()
     hand_over(hid, c, 1).wait_send()
     part_copy(1 - c).wait_send()
     grads_over(c).wait_send()
-
-    def picked_sent(source, carry):
-        for j in range(nx):
-            if j > 0:
-                x_copy(source, j).wait_send()
-            pair_copy(source * nx + at_x(j), c).wait_send()
-        return carry
-
-    lax.fori_loop(0, ny, picked_sent, 0)
-
-    def sent(k):
-        grad_copy(k).wait_send()
-        w2_copy(k).wait_send()
-        w1_sum_copy(k).wait_send()
-
-    each(nd, sent)
+    all_out(stage.at[:, pl.ds(0, nx - 1)], x_send.at[0])
+    all_out(samp.at[:, core_rows(c, 64), :], pair_send.at[0])
+    all_out(some_grads, g_send.at[0])
+    all_out(w2_in.at[pl.ds(0, nd - 1)], q_send.at[0])
+    all_out(some_tiles, r_send.at[0])
     hand_over(gw2_ref, 1 - c, 4).wait_recv()
     hand_over(gw2_ref, c, 4).wait_send()
-
-    def finished(k):
-        w1_done(k).wait_recv()
-        w1_out(k).wait_send()
-
-    each(nd, finished)
+    all_in(some_tiles, b_recv.at[0])
+    all_out(some_tiles, b_send.at[0])
 
 
 def finish_kernel(emb_ref, gw1_ref, gw2_ref, out_emb, out_1s, out_1n, out_2s, out_2n):
@@ -609,14 +570,14 @@
             pltpu.VMEM((128, 256), f32),
             pltpu.VMEM((nd, 8, 128), f32),
             pltpu.VMEM((8, 128), f32),
-            dma((15,)),
-            dma((ny - 1,)), dma((ny - 1,)), dma((ny - 1,)), dma((ny - 1,)),
-            dma((nx,)), dma((nx,)), dma((nd,)), dma((nd,)), dma((nd,)), dma((nd,)),
-            dma((nz,)), dma((nz,)), dma((5,)), dma((5,)),
-            dma((nz,)), dma((nz,)), dma((nz,)), dma((nz,)), dma((nz,)), dma((nz,)),
-            dma((nd,)), dma((nd,)), dma((nd,)), dma((nd,)),
-            dma((nd,)), dma((nd,)), dma((nd,)), dma((nd,)),
-            dma((nz,)), dma((nz,)), dma((1,)),
+            dma((11,)),
+            dma((1,)), dma((ny - 1,)), dma((1,)), dma((ny - 1,)),
+            dma((1,)), dma((1,)), dma((1,)), dma((ny,)), dma((1,)), dma((ny,)),
+            dma((1,)), dma((1,)), dma((5,)), dma((5,)),
+            dma((1,)), dma((nz,)), dma((1,)), dma((1,)), dma((1,)), dma((1,)),
+            dma((1,)), dma((1,)), dma((1,)), dma((1,)),
+            dma((1,)), dma((1,)), dma((1,)), dma((1,)),
+            dma((1,)), dma((1,)), dma((1,)),
         ],
         compiler_params=pltpu.CompilerParams(
             collective_id=1, has_side_effects=True, vmem_limit_bytes=60 * 1024 * 1024

time: 89.7 us -> 85.5 us (0.953)
  Pallas kernels: 88.6 us -> 84.2 us
    pallas_call x1, Pallas kernels: 86.7 us -> 82.3 us  [local(): pl.pallas_call(functools.partial(step_kernel, nd, nf), out_shape=(jax.Sha...]
where the time goes in v6:
time: 85.5 us; the launch traced here: 84.9 us
  Pallas kernels  84.2 us (98%)
    pallas_call x1, Pallas kernels, local(): pl.pallas_call(functools.partial(step_kernel, nd, nf), out_shape=(jax.Sha...  82.3 us
    pallas_call x1, Pallas kernels, local(): pl.pallas_call(finish_kernel, out_shape=(jax.ShapeDtypeStruct((64, 256),...  1.89 us

profile of v6, /device:TPU:1, one launch (start us, length us, event | category | flops | bytes accessed | tf_op | source)
XLA Modules:
  0.0 84.9 jit_solution(13156247989104899919)
XLA Ops:
  0.6 82.3 %train_step.1 = (bf16[64,256]{1,0:T(8,128)(2,1)}, f32[128,256]{1,0:T(8,128)}, bf16[16,32,256]{2,1,0:T(8,128)(2,1)}) custom-call(bf16[64,2048]{1,0:T(8,128)(2,1)} %bitcast.4, s32[32,512]{1,0:T(8,128)} %bitcast.5, bf16[64,256]{1,0:T(8,128)(2,1)} %w1s_any.1, bf16[64,256]{1,0:T(8,128)(2,1)} %w1n_any.1, s32[10,1,704]{2,1,0:T(1,128)} %bitcast.6, ...), custom_call_target="tpu_custom_call" | custom-call | tf_op jit(solution)/shard_map/train_step/pallas_call | solution.py:527
  83.0 1.9 %finish.1 = (bf16[64,256]{1,0:T(8,128)(2,1)}, f32[64,256]{1,0:T(8,128)}, f32[64,256]{1,0:T(8,128)}, f32[256,256]{1,0:T(8,128)}, f32[256,256]{1,0:T(8,128)}) custom-call(bf16[64,256]{1,0:T(8,128)(2,1)} %get-tuple-element.8.emb_ref, f32[128,256]{1,0:T(8,128)} %get-tuple-element.9.gw1_ref, bf16[16,32,256]{2,1,0:T(8,128)(2,1)} %get-tuple-element.10.gw2_ref), custom_call_target="tpu_custom_call" | custom-call | tf_op jit(solution)/shard_map/finish/pallas_call | solution.py:590

commit v7 on v6

--- a/solution.py
+++ b/solution.py
@@ -38,7 +38,7 @@
     blocks, req_ref, req_by_x, req_in, stage, samp, table, w1,
     adj_ref, deg_ref, self_ref, padded, lists, slots, scale, own, total,
     adj_two, deg_two, w2s, w2n, grad_ref,
-    x_out, x_in, gh_buf, hid, gpre, grads, turned, rows_t, w2_in, part, part_in, part1, in1, sum1,
+    x_out, x_in, gh_buf, hid, gpre, grads, turned, rows_t, w2_in, left, part, part_in, part1, in1, sum1,
     fetch, up_send, up_recv, down_send, down_recv, req_send, req_recv, x_send, x_recv,
     pair_send, pair_recv, w1_send, w1_recv, sib_send, sib_recv, a_send, a_recv, h_send, h_recv,
     p_send, p_recv, g_send, g_recv, q_send, q_recv, r_send, r_recv, b_send, b_recv,
@@ -67,8 +67,12 @@
     def dp_peer(k):
         return lax.rem(d + k, nd)
 
-    def dp_from(k):
-        return lax.rem(d - k + nd, nd)
+    offsets = [(dx, dy) for dy in range(ny) for dx in range(nx) if dx + dy > 0]
+    offsets.sort(key=lambda o: -min(o[0], nx - o[0]) - min(o[1], ny - o[1]))
+
+    def to_dp_peers(copy_to):
+        for dx, dy in offsets:
+            copy_to(at_y(dy) * nx + at_x(dx)).start()
 
     def remote(src, dst, send_sem, recv_sem, to):
         return pltpu.make_async_remote_copy(
@@ -317,8 +321,8 @@
 
     g_rows = core_rows(c, 32)
 
-    def grad_copy(k):
-        return remote(grad_ref.at[g_rows, :], grads.at[d, g_rows, :], g_send.at[0], g_recv.at[0], (dp_peer(k), f))
+    def grad_copy(to):
+        return remote(grad_ref.at[g_rows, :], grads.at[d, g_rows, :], g_send.at[0], g_recv.at[0], (to, f))
 
     some_grads = grads.at[pl.ds(0, nd - 1), pl.ds(0, 32), :]
 
@@ -356,7 +360,7 @@
         return carry
 
     lax.fori_loop(0, nz, sum_rows, 0)
-    each(nd, lambda k: grad_copy(k).start())
+    to_dp_peers(grad_copy)
     grads[d, g_rows, :] = grad_ref[g_rows, :]
     x_in[z] = x_out[z]
     rows_t[...] = x_out[...].reshape(half_rows, 256).astype(jnp.float32).T.astype(jnp.bfloat16)
@@ -414,10 +418,10 @@
     turned[...] = pair.astype(jnp.float32).T.astype(jnp.bfloat16)
     columns = core_rows(f, 16)
 
-    def w2_copy(k):
-        return remote(turned.at[columns, :], w2_in.at[d], q_send.at[0], q_recv.at[0], (dp_peer(k), f))
-
-    each(nd, lambda k: w2_copy(k).start())
+    def w2_copy(to):
+        return remote(turned.at[columns, :], w2_in.at[d], q_send.at[0], q_recv.at[0], (to, f))
+
+    to_dp_peers(w2_copy)
     w2_in[d] = turned[columns, :]
 
     part_copy(c).wait_recv()
@@ -431,13 +435,12 @@
 
     my_rows, my_lanes = tile_of(d)
 
-    def w1_sum_copy(k):
-        to = dp_peer(k)
+    def w1_sum_copy(to):
         rows, lanes = tile_of(to)
         return remote(part1.at[rows, lanes], in1.at[d], r_send.at[0], r_recv.at[0], (to, f))
 
     some_tiles = in1.at[pl.ds(0, nd - 1)]
-    each(nd, lambda k: w1_sum_copy(k).start())
+    to_dp_peers(w1_sum_copy)
     in1[d] = part1[my_rows, my_lanes]
 
     all_in(some_grads, g_recv.at[0])
@@ -453,14 +456,14 @@
     grads_over(1 - c).wait_recv()
     all_in(w2_in.at[pl.ds(0, nd - 1)], q_recv.at[0])
     lane = lax.broadcasted_iota(jnp.int32, (16, 128), 1)
-    total2 = jnp.zeros((32, out_grad.shape[-1]), jnp.float32)
     for p in range(nd // 2):
         first, second = w2_in[2 * p].astype(jnp.float32), w2_in[2 * p + 1].astype(jnp.float32)
         selfs = jnp.where(lane < 64, first, pltpu.roll(second, 64, 1))
         neighs = jnp.where(lane < 64, pltpu.roll(first, 64, 1), second)
-        left = jnp.concatenate([selfs, neighs], axis=0).astype(jnp.bfloat16)
-        right = grads[2 * p:2 * p + 2].reshape(128, out_grad.shape[-1])
-        total2 = total2 + jnp.dot(left, right, preferred_element_type=jnp.float32)
+        left[:, 128 * p:128 * p + 128] = jnp.concatenate([selfs, neighs], axis=0).astype(jnp.bfloat16)
+    total2 = jnp.dot(
+        left[...], grads[...].reshape(nd * targets, grads.shape[-1]), preferred_element_type=jnp.float32
+    )
     gw2_ref[mine] = total2.astype(jnp.bfloat16)
     for k in Z_ORDER:
         spread(gw2_ref, f_send, f_recv, k).start()
@@ -469,10 +472,10 @@
     sum1[...] = jnp.sum(in1[...], axis=0)
     gw1_ref[my_rows, my_lanes] = sum1[...]
 
-    def w1_out(k):
-        return remote(sum1, gw1_ref.at[my_rows, my_lanes], b_send.at[0], b_recv.at[0], (dp_peer(k), f))
-
-    each(nd, lambda k: w1_out(k).start())
+    def w1_out(to):
+        return remote(sum1, gw1_ref.at[my_rows, my_lanes], b_send.at[0], b_recv.at[0], (to, f))
+
+    to_dp_peers(w1_out)
     all_in(most(gw2_ref), f_recv.at[0])
     hand_over(gw2_ref, c, 4).start()
 
@@ -565,6 +568,7 @@
             pltpu.VMEM((256, 128), bf16),
             pltpu.VMEM((256, half), bf16),
             pltpu.VMEM((nd, 16, 128), bf16),
+            pltpu.VMEM((32, nd * 64), bf16),
             pltpu.VMEM((2, 2, 64, 256), f32),
             pltpu.VMEM((2, 64, 256), f32),
             pltpu.VMEM((128, 256), f32),

time: 85.5 us -> 85.3 us (level)
  no operation moved by 1% of the time
where the time goes in v7:
time: 85.3 us; the launch traced here: 85.1 us
  Pallas kernels  84.5 us (99%)
    pallas_call x1, Pallas kernels, local(): pl.pallas_call(functools.partial(step_kernel, nd, nf), out_shape=(jax.Sha...  82.6 us
    pallas_call x1, Pallas kernels, local(): pl.pallas_call(finish_kernel, out_shape=(jax.ShapeDtypeStruct((64, 256),...  1.89 us

profile of v7, /device:TPU:1, one launch (start us, length us, event | category | flops | bytes accessed | tf_op | source)
XLA Modules:
  0.0 85.1 jit_solution(2172787101945183314)
XLA Ops:
  0.6 82.6 %train_step.1 = (bf16[64,256]{1,0:T(8,128)(2,1)}, f32[128,256]{1,0:T(8,128)}, bf16[16,32,256]{2,1,0:T(8,128)(2,1)}) custom-call(bf16[64,2048]{1,0:T(8,128)(2,1)} %bitcast.4, s32[32,512]{1,0:T(8,128)} %bitcast.5, bf16[64,256]{1,0:T(8,128)(2,1)} %w1s_any.1, bf16[64,256]{1,0:T(8,128)(2,1)} %w1n_any.1, s32[10,1,704]{2,1,0:T(1,128)} %bitcast.6, ...), custom_call_target="tpu_custom_call" | custom-call | tf_op jit(solution)/shard_map/train_step/pallas_call | solution.py:530
  83.2 1.9 %finish.1 = (bf16[64,256]{1,0:T(8,128)(2,1)}, f32[64,256]{1,0:T(8,128)}, f32[64,256]{1,0:T(8,128)}, f32[256,256]{1,0:T(8,128)}, f32[256,256]{1,0:T(8,128)}) custom-call(bf16[64,256]{1,0:T(8,128)(2,1)} %get-tuple-element.8.emb_ref, f32[128,256]{1,0:T(8,128)} %get-tuple-element.9.gw1_ref, bf16[16,32,256]{2,1,0:T(8,128)(2,1)} %get-tuple-element.10.gw2_ref), custom_call_target="tpu_custom_call" | custom-call | tf_op jit(solution)/shard_map/finish/pallas_call | solution.py:594

commit v8 on v7

--- a/solution.py
+++ b/solution.py
@@ -17,14 +17,6 @@
 
 def contract_lanes(a, b):
     return lax.dot_general(a, b, (((1,), (1,)), ((), ())), preferred_element_type=jnp.float32)
-
-
-def each(count, body):
-    def step(k, carry):
-        body(k)
-        return carry
-
-    lax.fori_loop(1, count, step, 0)
 
 
 Z_ORDER = (4, 3, 5, 2, 6, 1, 7)
@@ -37,7 +29,7 @@
     emb_ref, gw1_ref, gw2_ref,
     blocks, req_ref, req_by_x, req_in, stage, samp, table, w1,
     adj_ref, deg_ref, self_ref, padded, lists, slots, scale, own, total,
-    adj_two, deg_two, w2s, w2n, grad_ref,
+    adj_two, deg_two, w2s, w2n, grad_ref, counts_ref, degree_ref,
     x_out, x_in, gh_buf, hid, gpre, grads, turned, rows_t, w2_in, left, part, part_in, part1, in1, sum1,
     fetch, up_send, up_recv, down_send, down_recv, req_send, req_recv, x_send, x_recv,
     pair_send, pair_recv, w1_send, w1_recv, sib_send, sib_recv, a_send, a_recv, h_send, h_recv,
@@ -64,9 +56,6 @@
         to = lax.rem(z + k, nz)
         return to, (d, 2 * to + c)
 
-    def dp_peer(k):
-        return lax.rem(d + k, nd)
-
     offsets = [(dx, dy) for dy in range(ny) for dx in range(nx) if dx + dy > 0]
     offsets.sort(key=lambda o: -min(o[0], nx - o[0]) - min(o[1], ny - o[1]))
 
@@ -109,11 +98,14 @@
     for copy in [fetches[4]] + fetches[:4] + fetches[5:7]:
         copy.start()
 
+    for s in (1, -1):
+        greet((at_y(s) * nx + x, f))
+    for j in range(1, nx):
+        greet((y * nx + at_x(j), f))
     greet(sibling)
     for k in range(1, nz):
         greet(along_z(k)[1])
-    each(nd, lambda k: greet((dp_peer(k), f)))
-    pl.semaphore_wait(barrier, 1 + nz - 1 + nd - 1)
+    pl.semaphore_wait(barrier, 2 + nx - 1 + 1 + nz - 1)
 
     def req_copy(j):
         to = at_x(j)
@@ -262,6 +254,49 @@
         def _():
             collect(in_step(i - 2), source_in(i - 2))
 
+    fanout = adj_ref.shape[0]
+    present = self_ref.shape[1]
+    targets = deg_two.shape[1]
+    to_smem = pltpu.make_async_copy(lists, slots, smem_sem.at[0])
+
+    def prepare():
+        for copy in fetches[7:]:
+            copy.wait()
+        table[nd * cap:, :] = jnp.zeros((8, 128), jnp.float32)
+        padded[...] = jnp.full(padded.shape, nd * cap, jnp.int32)
+        for j in range(fanout):
+            padded[j:j + 1, :present] = jnp.where(deg_ref[...] > j, adj_ref[j], nd * cap)
+        padded[fanout:fanout + 1, :present] = self_ref[...]
+        my_lanes_half = pl.ds(pl.multiple_of(c * half_rows, 128), half_rows)
+        for j in range(fanout + 1):
+            line = padded[j:j + 1, my_lanes_half]
+            for to in range(nz):
+                at = to * (fanout + 1) + j
+                lists[at:at + 1, :block] = line[:, block * to:block * to + block]
+        to_smem.start()
+        padded[:1, :] = jnp.ones((1, ROWS), jnp.int32)
+        padded[:1, :present] = deg_ref[...]
+        inverse = 1.0 / padded[:1, my_lanes_half].astype(jnp.float32)
+        scale[...] = jnp.broadcast_to(jnp.broadcast_to(inverse, (8, half_rows)).T[:, :1], scale.shape)
+
+        out_grad = grad_ref[...]
+        degree_row = deg_two[...]
+        row = lax.broadcasted_iota(jnp.int32, (ROWS, targets), 0)
+        counts = jnp.zeros((ROWS, targets), jnp.float32)
+        for j in range(fanout):
+            listed = jnp.where(degree_row > j, adj_two[j], -1)
+            counts = counts + jnp.where(row == listed, 1.0, 0.0)
+        degree_row = degree_row.astype(jnp.float32)
+        degree = jnp.broadcast_to(degree_row, (8, targets)).T[:, :1]
+        degree_ref[...] = jnp.broadcast_to(degree, degree_ref.shape)
+        grad_agg = contract_lanes(out_grad, w2n[...]) / degree
+        high = grad_agg.astype(jnp.bfloat16)
+        low = (grad_agg - high.astype(jnp.float32)).astype(jnp.bfloat16)
+        both = jnp.concatenate([counts, counts], axis=1).astype(jnp.bfloat16)
+        gh_buf[...] = jnp.dot(both, jnp.concatenate([high, low], axis=0), preferred_element_type=jnp.float32)
+        gh_buf[:targets, :] += contract_lanes(out_grad, w2s[...])
+        counts_ref[...] = counts.T.astype(jnp.bfloat16)
+
     def ring_step(i, carry):
         @pl.when(i > 0)
         def _():
@@ -272,50 +307,15 @@
             pass_on(2 * i - 1, i)
 
         process(in_step(i), source_in(i))
+
+        @pl.when(i == 1)
+        def _():
+            prepare()
+
         gather_late(i)
         return carry
 
     lax.fori_loop(0, steps + 1, ring_step, 0)
-
-    for copy in fetches[7:]:
-        copy.wait()
-    fanout = adj_ref.shape[0]
-    present = self_ref.shape[1]
-    table[nd * cap:, :] = jnp.zeros((8, 128), jnp.float32)
-    padded[...] = jnp.full(padded.shape, nd * cap, jnp.int32)
-    for j in range(fanout):
-        padded[j:j + 1, :present] = jnp.where(deg_ref[...] > j, adj_ref[j], nd * cap)
-    padded[fanout:fanout + 1, :present] = self_ref[...]
-    my_lanes_half = pl.ds(pl.multiple_of(c * half_rows, 128), half_rows)
-    for j in range(fanout + 1):
-        line = padded[j:j + 1, my_lanes_half]
-        for to in range(nz):
-            at = to * (fanout + 1) + j
-            lists[at:at + 1, :block] = line[:, block * to:block * to + block]
-    to_smem = pltpu.make_async_copy(lists, slots, smem_sem.at[0])
-    to_smem.start()
-    padded[:1, :] = jnp.ones((1, ROWS), jnp.int32)
-    padded[:1, :present] = deg_ref[...]
-    inverse = 1.0 / padded[:1, my_lanes_half].astype(jnp.float32)
-    scale[...] = jnp.broadcast_to(jnp.broadcast_to(inverse, (8, half_rows)).T[:, :1], scale.shape)
-
-    out_grad = grad_ref[...]
-    degree_row = deg_two[...]
-    targets = degree_row.shape[1]
-    row = lax.broadcasted_iota(jnp.int32, (ROWS, targets), 0)
-    counts = jnp.zeros((ROWS, targets), jnp.float32)
-    for j in range(fanout):
-        listed = jnp.where(degree_row > j, adj_two[j], -1)
-        counts = counts + jnp.where(row == listed, 1.0, 0.0)
-    degree_row = degree_row.astype(jnp.float32)
-    degree = jnp.broadcast_to(degree_row, (8, targets)).T[:, :1]
-    grad_agg = contract_lanes(out_grad, w2n[...]) / degree
-    high = grad_agg.astype(jnp.bfloat16)
-    low = (grad_agg - high.astype(jnp.float32)).astype(jnp.bfloat16)
-    both = jnp.concatenate([counts, counts], axis=1).astype(jnp.bfloat16)
-    gh_buf[...] = jnp.dot(both, jnp.concatenate([high, low], axis=0), preferred_element_type=jnp.float32)
-    gh_buf[:targets, :] += contract_lanes(out_grad, w2s[...])
-    counts = counts.T.astype(jnp.bfloat16)
 
     lax.fori_loop(steps + 1, steps + 4, lambda i, carry: (gather_late(i), carry)[1], 0)
 
@@ -412,7 +412,7 @@
 
     hidden = hid[...].reshape(ROWS, hid.shape[-1])
     self_hidden = hidden[:targets, :]
-    agg_two = jnp.dot(counts, hidden, preferred_element_type=jnp.float32) / degree
+    agg_two = jnp.dot(counts_ref[...], hidden, preferred_element_type=jnp.float32) / degree_ref[...]
     agg_two = agg_two.astype(jnp.bfloat16)
     pair = jnp.concatenate([self_hidden, agg_two], axis=0)
     turned[...] = pair.astype(jnp.float32).T.astype(jnp.bfloat16)
@@ -559,6 +559,8 @@
             pltpu.VMEM((256, 256), bf16),
             pltpu.VMEM((256, 256), bf16),
             pltpu.VMEM(out_grad.shape, bf16),
+            pltpu.VMEM((64, ROWS), bf16),
+            pltpu.VMEM((64, 256), f32),
             pltpu.VMEM((nz, block, 256), bf16),
             pltpu.VMEM((nz, block, 256), bf16),
             pltpu.VMEM((ROWS, 256), f32),

time: 85.3 us -> 83.1 us (0.974)
  Pallas kernels: 84.5 us -> 81.8 us
    pallas_call x1, Pallas kernels: 82.6 us -> 80 us  [local(): pl.pallas_call(functools.partial(step_kernel, nd, nf), out_shape=(jax.Sha...]
where the time goes in v8:
time: 83.1 us; the launch traced here: 82.5 us
  Pallas kernels  81.8 us (98%)
    pallas_call x1, Pallas kernels, local(): pl.pallas_call(functools.partial(step_kernel, nd, nf), out_shape=(jax.Sha...  80 us
    pallas_call x1, Pallas kernels, local(): pl.pallas_call(finish_kernel, out_shape=(jax.ShapeDtypeStruct((64, 256),...  1.89 us

profile of v8, /device:TPU:1, one launch (start us, length us, event | category | flops | bytes accessed | tf_op | source)
XLA Modules:
  0.0 82.5 jit_solution(12347286158674979419)
XLA Ops:
  0.6 80.0 %train_step.1 = (bf16[64,256]{1,0:T(8,128)(2,1)}, f32[128,256]{1,0:T(8,128)}, bf16[16,32,256]{2,1,0:T(8,128)(2,1)}) custom-call(bf16[64,2048]{1,0:T(8,128)(2,1)} %bitcast.4, s32[32,512]{1,0:T(8,128)} %bitcast.5, bf16[64,256]{1,0:T(8,128)(2,1)} %w1s_any.1, bf16[64,256]{1,0:T(8,128)(2,1)} %w1n_any.1, s32[10,1,704]{2,1,0:T(1,128)} %bitcast.6, ...), custom_call_target="tpu_custom_call" | custom-call | tf_op jit(solution)/shard_map/train_step/pallas_call | solution.py:530
  80.6 1.9 %finish.1 = (bf16[64,256]{1,0:T(8,128)(2,1)}, f32[64,256]{1,0:T(8,128)}, f32[64,256]{1,0:T(8,128)}, f32[256,256]{1,0:T(8,128)}, f32[256,256]{1,0:T(8,128)}) custom-call(bf16[64,256]{1,0:T(8,128)(2,1)} %get-tuple-element.8.emb_ref, f32[128,256]{1,0:T(8,128)} %get-tuple-element.9.gw1_ref, bf16[16,32,256]{2,1,0:T(8,128)(2,1)} %get-tuple-element.10.gw2_ref), custom_call_target="tpu_custom_call" | custom-call | tf_op jit(solution)/shard_map/finish/pallas_call | solution.py:596

commit v9 on v8

--- a/solution.py
+++ b/solution.py
@@ -187,7 +187,8 @@
     def process(count, source_of):
         def step(k, carry):
             source = source_of(lax.div(k, nx))
-            j = lax.rem(k + 2, nx)
+            late = lax.div(lax.rem(k, nx), 2)
+            j = (2 + lax.rem(k, nx)) * (1 - late) + (3 - lax.rem(k, nx)) * late
             stage[source, j] = pick(source, j)
 
             @pl.when(j > 0)
@@ -360,8 +361,6 @@
         return carry
 
     lax.fori_loop(0, nz, sum_rows, 0)
-    to_dp_peers(grad_copy)
-    grads[d, g_rows, :] = grad_ref[g_rows, :]
     x_in[z] = x_out[z]
     rows_t[...] = x_out[...].reshape(half_rows, 256).astype(jnp.float32).T.astype(jnp.bfloat16)
     w1_over(1 - c).wait_recv()
@@ -396,6 +395,8 @@
         spread(hid, h_send, h_recv, k).start()
     for k in Z_ORDER:
         gpre_copy(k).start()
+    to_dp_peers(grad_copy)
+    grads[d, g_rows, :] = grad_ref[g_rows, :]
     all_in(most(hid), h_recv.at[0])
     hand_over(hid, c, 1).start()
     all_in(most(gpre), p_recv.at[0])

time: 83.1 us -> 82.9 us (level)
  no operation moved by 1% of the time
where the time goes in v9:
time: 82.9 us; the launch traced here: 82.7 us
  Pallas kernels  82.1 us (99%)
    pallas_call x1, Pallas kernels, local(): pl.pallas_call(functools.partial(step_kernel, nd, nf), out_shape=(jax.Sha...  80.2 us
    pallas_call x1, Pallas kernels, local(): pl.pallas_call(finish_kernel, out_shape=(jax.ShapeDtypeStruct((64, 256),...  1.89 us

profile of v9, /device:TPU:1, one launch (start us, length us, event | category | flops | bytes accessed | tf_op | source)
XLA Modules:
  0.0 82.7 jit_solution(16819825689915771923)
XLA Ops:
  0.6 80.2 %train_step.1 = (bf16[64,256]{1,0:T(8,128)(2,1)}, f32[128,256]{1,0:T(8,128)}, bf16[16,32,256]{2,1,0:T(8,128)(2,1)}) custom-call(bf16[64,2048]{1,0:T(8,128)(2,1)} %bitcast.4, s32[32,512]{1,0:T(8,128)} %bitcast.5, bf16[64,256]{1,0:T(8,128)(2,1)} %w1s_any.1, bf16[64,256]{1,0:T(8,128)(2,1)} %w1n_any.1, s32[10,1,704]{2,1,0:T(1,128)} %bitcast.6, ...), custom_call_target="tpu_custom_call" | custom-call | tf_op jit(solution)/shard_map/train_step/pallas_call | solution.py:531
  80.8 1.9 %finish.1 = (bf16[64,256]{1,0:T(8,128)(2,1)}, f32[64,256]{1,0:T(8,128)}, f32[64,256]{1,0:T(8,128)}, f32[256,256]{1,0:T(8,128)}, f32[256,256]{1,0:T(8,128)}) custom-call(bf16[64,256]{1,0:T(8,128)(2,1)} %get-tuple-element.8.emb_ref, f32[128,256]{1,0:T(8,128)} %get-tuple-element.9.gw1_ref, bf16[16,32,256]{2,1,0:T(8,128)(2,1)} %get-tuple-element.10.gw2_ref), custom_call_target="tpu_custom_call" | custom-call | tf_op jit(solution)/shard_map/finish/pallas_call | solution.py:597
